TPU v7x, 32 devices: a whole 2x2x4 slice. The times are simulated.
32 devices in a mesh: row: 4 (over x, core), col: 4 (over z), slab: 2 (over y).
Axes of the slice: x: 2, y: 2, z: 4, core: 2. Of those that a mesh axis runs over, the one named last changes fastest.
Arguments:
- fields: bfloat16 [2, 2048, 1024], P(None, ('row', 'col', 'slab')), may hold values from -0.8984375 to 0.8984375
Outputs:
- gram: float32 [2, 2048, 2048], P(None, ('row', 'slab'), 'col')
All inputs are finite; a program needn't handle non-finite values.
Results may differ from a plain program's by a relative error of at most 0.01.
Values may be sent and summed in bfloat16 or wider, within the bound.
No kernel may reach another device: no remote copies, remote signals or barrier semaphores. Data moves between devices by JAX's collectives and lax.ppermute only.
A program may use at most 64 MiB of HBM per device.

v0:
```python
import jax
import jax.numpy as jnp
from jax import lax
from jax.sharding import PartitionSpec as P


def pair_terms(left_real, left_imag, piece):
    right_real = jnp.concatenate([piece[0], piece[1]], axis=1)
    right_imag = jnp.concatenate([piece[1], piece[0]], axis=1)
    dims = (((1,), (1,)), ((), ()))
    real = lax.dot_general(left_real, right_real, dims, preferred_element_type=jnp.float32)
    imag = lax.dot_general(left_imag, right_imag, dims, preferred_element_type=jnp.float32)
    return jnp.stack([real, imag])


def body(fields):
    local = lax.all_to_all(fields, "slab", split_axis=2, concat_axis=1, tiled=True)
    row_block = lax.all_gather(local, "col", axis=1, tiled=True)
    left_real = jnp.concatenate([row_block[0], row_block[1]], axis=1)
    left_imag = jnp.concatenate([row_block[0], -row_block[1]], axis=1)
    column_set = lax.all_gather(local, "row", axis=1, tiled=True)
    terms = pair_terms(left_real, left_imag, column_set)
    gram = lax.psum_scatter(
        terms.astype(jnp.bfloat16), "slab", scatter_dimension=1, tiled=True
    ).astype(jnp.float32)
    return gram


def solution(mesh):
    placed = (P(None, ("row", "col", "slab"), None),)
    return jax.shard_map(
        body, mesh=mesh, in_specs=placed, out_specs=P(None, ("row", "slab"), "col"), check_vma=False
    )
```

profile of v0, /device:TPU:0, one launch (start us, length us, event | category | flops | bytes accessed | tf_op | source)
XLA Modules:
  0.0 98.6 jit_solution(5196075837851762547)
XLA Ops:
  6.5 0.0 all-gather.5.cloned.1.call-start
  6.5 1.3 %copy.3 = bf16[2,64,1024]{1,0,2:T(2,128)(2,1)S(1)} copy(bf16[2,64,1024]{2,1,0:T(8,128)(2,1)} %param.1) | data formatting | bytes 524288 | tf_op args[0]
  7.8 0.4 reshape
  8.2 9.2 %all_to_all.18 = bf16[2,2,32768]{2,1,0:T(2,128)(2,1)S(1)} all-to-all(bf16[2,2,32768]{2,1,0:T(2,128)(2,1)S(1)} %reshape), channel_id=1, replica_groups=mesh['row'=4,'col'=4,'slab'=2] {'slab'}, dimensions={0} | all-to-all | bytes 524288 | tf_op jit(solution)/shard_map/all_to_all | solution.py:17
  17.4 0.3 reshape.1
  17.8 1.0 %copy.5 = bf16[2,2,64,512]{3,2,1,0:T(8,128)(2,1)} copy(bf16[2,2,64,512]{2,0,3,1:T(2,128)(2,1)S(1)} %bitcast.23) | data formatting | bytes 524288 | tf_op jit(solution)/shard_map/all_to_all | solution.py:17
  18.8 0.0 all-gather.5.cloned.1.call-update
  18.8 0.0 all-gather.3.cloned.1.call-start
  18.9 0.7 all-gather.3.cloned.1.call-update
  19.6 0.0 reduce-scatter.2.cloned.1.call-start
  19.6 16.4 %all-gather.5.cloned.1.call-done = bf16[2,512,512]{2,1,0:T(8,128)(2,1)} async-done(((bf16[2,128,512]{2,1,0:T(8,128)(2,1)}), bf16[2,512,512]{2,1,0:T(8,128)(2,1)}) %all-gather.5.cloned.1.call-update) | async-done | bytes 1048592 | tf_op jit(solution)/shard_map/all_gather | solution.py:21
  36.1 1.3 %slice_bitcast_fusion = (bf16[512,512]{1,0:T(8,128)(2,1)S(1)}, bf16[512,512]{1,0:T(8,128)(2,1)S(1)}) fusion(bf16[2,512,512]{2,1,0:T(8,128)(2,1)} %all-gather.5.cloned.1.call-done), kind=kLoop, calls=%fused_computation.15 | loop fusion | bytes 2097152 | tf_op jit(solution)/shard_map/squeeze | solution.py:8
  37.3 28.3 %all-gather.3.cloned.1.call-done = bf16[2,512,512]{2,1,0:T(8,128)(2,1)} async-done(((bf16[2,128,512]{2,1,0:T(8,128)(2,1)}), bf16[2,512,512]{2,1,0:T(8,128)(2,1)}) %all-gather.3.cloned.1.call-update) | async-done | bytes 1048592 | tf_op jit(solution)/shard_map/all_gather | solution.py:18
  65.6 1.3 %slice_bitcast_fusion.2 = (bf16[512,512]{1,0:T(8,128)(2,1)S(1)}, bf16[512,512]{1,0:T(8,128)(2,1)S(1)}) fusion(bf16[2,512,512]{2,1,0:T(8,128)(2,1)} %all-gather.3.cloned.1.call-done), kind=kLoop, calls=%fused_computation.17 | loop fusion | bytes 2097152 | tf_op jit(solution)/shard_map/squeeze | solution.py:19
  66.9 0.0 copy-start
  66.9 0.7 fusion
  67.6 0.5 copy-done
  68.1 0.7 fusion.1
  68.9 1.1 %pad_maximum_fusion.4 = bf16[2,512,512]{2,1,0:T(8,128)(2,1)} fusion(bf16[1,512,512]{2,1,0:T(8,128)(2,1)S(1)} %fusion.1, bf16[1,512,512]{2,1,0:T(8,128)(2,1)S(1)} %fusion), kind=kLoop, calls=%fused_computation.14 | loop fusion | flops 524288 | bytes 2097152 | tf_op jit(solution)/shard_map/stack | solution.py:13
  69.9 0.0 reduce-scatter.2.cloned.1.call-update
  70.0 20.0 %reduce-scatter.2.cloned.1.call-done = bf16[2,256,512]{2,1,0:T(8,128)(2,1)} async-done(((bf16[2,512,512]{2,1,0:T(8,128)(2,1)}), bf16[2,256,512]{2,1,0:T(8,128)(2,1)}) %reduce-scatter.2.cloned.1.call-update) | async-done | bytes 524304 | tf_op jit(solution)/shard_map/reduce_scatter | solution.py:23
  89.9 2.1 %convert_element_type.4 = f32[2,256,512]{2,1,0:T(8,128)} convert(bf16[2,256,512]{2,1,0:T(8,128)(2,1)} %reduce-scatter.2.cloned.1.call-done) | non-fusion elementwise | flops 262144 | bytes 1572864 | tf_op jit(solution)/shard_map/convert_element_type | solution.py:25
  (1 shorter events, 0.0 us)
Async XLA Ops:
  6.5 29.5 %all-gather.5.cloned.1.call-start = ((), (), s32[]{:S(2)}) async-start(), calls=%async_computation.3 | async-start | bytes 1310720 | tf_op jit(solution)/shard_map/all_gather | solution.py:21
  18.8 46.8 %all-gather.3.cloned.1.call-start = ((), (), s32[]{:S(2)}) async-start(), calls=%async_computation.2 | async-start | bytes 1310720 | tf_op jit(solution)/shard_map/all_gather | solution.py:18
  19.6 70.4 %reduce-scatter.2.cloned.1.call-start = ((), (), s32[]{:S(2)}) async-start(), calls=%async_computation.4 | async-start | bytes 1572864 | tf_op jit(solution)/shard_map/reduce_scatter | solution.py:23
  66.9 1.2 %copy-start = (bf16[2,512,512]{2,1,0:T(8,128)(2,1)S(1)}, bf16[2,512,512]{2,1,0:T(8,128)(2,1)}, u32[]{:S(2)}) copy-start(bf16[2,512,512]{2,1,0:T(8,128)(2,1)} %all-gather.3.cloned.1.call-done) | copy-start | bytes 3145732
Sparse Core Ops, SparseCore 0:
  18.9 17.0 all-gather.4
  37.6 27.9 all-gather.2
  70.1 19.8 reduce-scatter.1
where the time goes:
time: 98.9 us; the launch traced here: 98.6 us
  waiting for transfers between devices  65.4 us (66%)
  between operations  13.2 us (13%)
  blocking collectives  9.21 us (9%)
  local copies, waits for them, and re-layouts  6.04 us (6%)
  other arithmetic  3.24 us (3%)
  matrix products  1.47 us (1%)
    all_gather x1, waiting for transfers between devices, body(): row_block = lax.all_gather(local, 'col', axis=1, tiled=True)  28.3 us
    reduce_scatter x1, waiting for transfers between devices, body(): lax.psum_scatter(terms.astype(jnp.bfloat16), 'slab', scatter_dimension=1,...  20 us
    all_gather x1, waiting for transfers between devices, body(): column_set = lax.all_gather(local, 'row', axis=1, tiled=True)  16.4 us
    all_to_all x1, blocking collectives, body(): lax.all_to_all(fields, 'slab', split_axis=2, concat_axis=1, tiled=True)  9.21 us
    unnamed x5, local copies, waits for them, and re-layouts  2.48 us
    convert_element_type x1, other arithmetic, body(): gram = lax.psum_scatter(terms.astype(jnp.bfloat16), 'slab', scatter_dimen...  2.14 us
  transfers between devices with their start and end apart: 3, of which 3 were waited for; matrix products, arithmetic and copies ran while one was open for 1% of the time, Pallas kernels for 0%

commit v1 on v0

v1 whole, which is shorter than its diff:
```python
import functools

import jax
import jax.numpy as jnp
from jax import lax
from jax.experimental import pallas as pl
from jax.experimental.pallas import tpu as pltpu
from jax.sharding import PartitionSpec as P

AXES = ("row", "col", "slab")
TILE = 512


def dot(left, right):
    return lax.dot_general(left, right, (((1,), (1,)), ((), ())), preferred_element_type=jnp.float32)


def device_pairs(sizes, target):
    rows, cols, slabs = sizes
    pairs = []
    for r in range(rows):
        for c in range(cols):
            for s in range(slabs):
                to = target(r, c, s)
                if to is not None:
                    pairs.append(((r * cols + c) * slabs + s, (to[0] * cols + to[1]) * slabs + to[2]))
    return pairs


def row_plan(sizes):
    _, cols, _ = sizes
    half = cols // 2
    plan = []
    for shift in list(range(1, half)) + [0]:
        for turn in range(2):
            plan.append((shift if shift > 0 else None, (shift + 1) % half, turn))
    return plan


def row_pairs(sizes, near_shift, far_shift, turn):
    rows, cols, slabs = sizes
    half = cols // 2
    pairs = []
    for r in range(rows):
        for c in range(cols):
            for s in range(slabs):
                near = c // half == s
                shift = near_shift if near else far_shift
                if shift is None:
                    continue
                source = (r, s * half + (c + shift) % half, s ^ turn if near else s ^ turn ^ 1)
                pairs.append(((source[0] * cols + source[1]) * slabs + source[2], (r * cols + c) * slabs + s))
    return pairs


def gram_kernel(sizes, plan, offsets, *refs):
    rows, cols, slabs = sizes
    half = cols // 2
    n_col = len(offsets)
    col_refs = refs[:n_col]
    row_refs = refs[n_col : n_col + len(plan)]
    out_ref, left, right = refs[n_col + len(plan) :]
    r, c, s = (lax.axis_index(axis) for axis in AXES)
    near = lax.div(c, half) == s
    _, size, pixels = col_refs[0].shape

    for ref, (dr, ds) in zip(col_refs, offsets):
        at = pl.multiple_of((lax.bitwise_xor(r, dr) * slabs + lax.bitwise_xor(s, ds)) * size, size)
        right[:, pl.ds(at, size), :] = ref[...]

    for ref, (near_shift, far_shift, turn) in zip(row_refs, plan):
        near_place = lax.rem(c + (near_shift or 0), half) * slabs + lax.bitwise_xor(s, turn)
        far_place = lax.rem(c + far_shift, half) * slabs + lax.bitwise_xor(s, turn ^ 1)
        at = pl.multiple_of(jnp.where(near, near_place, far_place) * size, size)
        block = ref[...]
        if near_shift is None:
            block = jnp.where(near, col_refs[turn][...], block)
        left[:, pl.ds(at, size), :] = block

    @pl.loop(0, right.shape[1] // TILE)
    def _(tile):
        at = pl.multiple_of(tile * TILE, TILE)
        here = pl.ds(at, TILE)
        out_ref[0, :, here] = dot(left[0], right[0, here]) + dot(left[1], right[1, here])
        out_ref[1, :, here] = dot(left[0], right[1, here]) - dot(left[1], right[0, here])


def solution(mesh):
    sizes = tuple(mesh.shape[axis] for axis in AXES)
    rows, cols, slabs = sizes
    plan = row_plan(sizes)

    def body(fields):
        _, size, pixels = fields.shape
        blocks, offsets = [fields], [(0, 0)]
        steps = [(0, 1)]
        bit = rows // 2
        while bit > 0:
            steps.append((bit, 0))
            bit //= 2
        for dr, ds in steps:
            pairs = device_pairs(sizes, lambda r, c, s: (r ^ dr, c, s ^ ds))
            blocks = blocks + [lax.ppermute(block, AXES, pairs) for block in blocks]
            offsets = offsets + [(a ^ dr, b ^ ds) for a, b in offsets]
        row_blocks = [lax.ppermute(fields, AXES, row_pairs(sizes, *step)) for step in plan]
        out_rows = cols // 2 * slabs * size
        out_cols = rows * slabs * size
        return pl.pallas_call(
            functools.partial(gram_kernel, sizes, plan, offsets),
            out_shape=jax.ShapeDtypeStruct((2, out_rows, out_cols), jnp.float32),
            in_specs=[pl.BlockSpec(memory_space=pltpu.VMEM)] * (len(blocks) + len(plan)),
            out_specs=pl.BlockSpec(memory_space=pltpu.VMEM),
            scratch_shapes=[
                pltpu.VMEM((2, out_rows, pixels), jnp.bfloat16),
                pltpu.VMEM((2, out_cols, pixels), jnp.bfloat16),
            ],
            compiler_params=pltpu.CompilerParams(vmem_limit_bytes=32 * 1024 * 1024),
        )(*[pltpu.with_memory_space_constraint(block, pltpu.VMEM) for block in blocks + row_blocks])

    placed = (P(None, AXES, None),)
    return jax.shard_map(
        body, mesh=mesh, in_specs=placed, out_specs=P(None, ("row", "slab"), "col"), check_vma=False
    )
```

time: 98.9 us -> 39.6 us (0.40)
  the two profiles are of different devices: /device:TPU:0 before, /device:TPU:19 now
where the time goes in v1:
time: 39.6 us; the launch traced here: 39.5 us
  waiting for transfers between devices  20.6 us (52%)
  starting transfers between devices  15.4 us (39%)
  Pallas kernels  2.44 us (6%)
  local copies, waits for them, and re-layouts  0.94 us (2%)
    ppermute x4, waiting for transfers between devices, body(): lax.ppermute(fields, AXES, row_pairs(sizes, *step))  19 us
    ppermute x7, starting transfers between devices, body(): blocks = blocks + [lax.ppermute(block, AXES, pairs) for block in blocks]  7.85 us
    ppermute x4, starting transfers between devices, body(): lax.ppermute(fields, AXES, row_pairs(sizes, *step))  7.58 us
    pallas_call x1, Pallas kernels, body(): pl.pallas_call(functools.partial(gram_kernel, sizes, plan, offsets), out_...  2.44 us
    ppermute x7, waiting for transfers between devices, body(): blocks = blocks + [lax.ppermute(block, AXES, pairs) for block in blocks]  1.56 us
    unnamed x2, local copies, waits for them, and re-layouts  0.94 us
  transfers between devices with their start and end apart: 11, of which 4 were waited for; matrix products, arithmetic and copies ran while one was open for 0% of the time, Pallas kernels for 0%

profile of v1, /device:TPU:19, one launch (start us, length us, event | category | flops | bytes accessed | tf_op | source)
XLA Modules:
  0.0 39.5 jit_solution(14949345369884979330)
XLA Ops:
  0.0 1.2 %collective-permute-start = (bf16[2,64,1024]{2,1,0:T(8,128)(2,1)}, bf16[2,64,1024]{2,1,0:T(8,128)(2,1)S(1)}, u32[]{:S(2)}, u32[]{:S(2)}) collective-permute-start(bf16[2,64,1024]{2,1,0:T(8,128)(2,1)} %refs_0_.1), channel_id=1, source_target_pairs={{0,1},{1,0},{2,3},{3,2},{4,5},{5,4},{6,7},{7,6},{8,9},{9,8},{10,11... | collective-permute-start | bytes 786440 | tf_op jit(solution)/shard_map/ppermute | solution.py:103
  1.2 2.0 %collective-permute-start.9 = (bf16[2,64,1024]{2,1,0:T(8,128)(2,1)}, bf16[2,64,1024]{2,1,0:T(8,128)(2,1)S(1)}, u32[]{:S(2)}, u32[]{:S(2)}) collective-permute-start(bf16[2,64,1024]{2,1,0:T(8,128)(2,1)} %refs_0_.1), channel_id=1, source_target_pairs={{6,1},{4,3},{3,4},{1,6},{14,9},{12,11},{11,12},{9,14},{22,17},{20,... | collective-permute-start | bytes 786440 | tf_op jit(solution)/shard_map/ppermute | solution.py:105
  3.3 0.1 collective-permute-start.8
  3.3 4.2 %collective-permute-start.7 = (bf16[2,64,1024]{2,1,0:T(8,128)(2,1)}, bf16[2,64,1024]{2,1,0:T(8,128)(2,1)S(1)}, u32[]{:S(2)}, u32[]{:S(2)}) collective-permute-start(bf16[2,64,1024]{2,1,0:T(8,128)(2,1)} %refs_0_.1), channel_id=1, source_target_pairs={{2,0},{4,1},{0,2},{6,3},{1,4},{7,5},{3,6},{5,7},{10,8},{12,9},{8,1... | collective-permute-start | bytes 786440 | tf_op jit(solution)/shard_map/ppermute | solution.py:105
  7.6 0.3 collective-permute-start.1
  7.8 1.5 %collective-permute-done.refs_1_ = bf16[2,64,1024]{2,1,0:T(8,128)(2,1)S(1)} collective-permute-done((bf16[2,64,1024]{2,1,0:T(8,128)(2,1)}, bf16[2,64,1024]{2,1,0:T(8,128)(2,1)S(1)}, u32[]{:S(2)}, u32[]{:S(2)}) %collective-permute-start) | collective-permute-done | bytes 262176 | tf_op jit(solution)/shard_map/ppermute | solution.py:103
  9.4 0.3 collective-permute-start.2
  9.6 7.2 %collective-permute-done.9.refs_10_ = bf16[2,64,1024]{2,1,0:T(8,128)(2,1)S(1)} collective-permute-done((bf16[2,64,1024]{2,1,0:T(8,128)(2,1)}, bf16[2,64,1024]{2,1,0:T(8,128)(2,1)S(1)}, u32[]{:S(2)}, u32[]{:S(2)}) %collective-permute-start.9) | collective-permute-done | bytes 262176 | tf_op jit(solution)/shard_map/ppermute | solution.py:105
  16.8 4.1 %collective-permute-start.3 = (bf16[2,64,1024]{2,1,0:T(8,128)(2,1)}, bf16[2,64,1024]{2,1,0:T(8,128)(2,1)S(1)}, u32[]{:S(2)}, u32[]{:S(2)}) collective-permute-start(bf16[2,64,1024]{2,1,0:T(8,128)(2,1)} %refs_0_.1), channel_id=1, source_target_pairs={{0,8},{1,9},{2,10},{3,11},{4,12},{5,13},{6,14},{7,15},{8,0},{9,1},... | collective-permute-start | bytes 786440 | tf_op jit(solution)/shard_map/ppermute | solution.py:103
  20.9 0.0 collective-permute-done.8.refs_9_
  20.9 1.3 %collective-permute-start.10 = (bf16[2,64,1024]{2,1,0:T(8,128)(2,1)}, bf16[2,64,1024]{2,1,0:T(8,128)(2,1)S(1)}, u32[]{:S(2)}, u32[]{:S(2)}) collective-permute-start(bf16[2,64,1024]{2,1,0:T(8,128)(2,1)} %refs_0_.1), channel_id=1, source_target_pairs={{7,1},{5,3},{2,4},{0,6},{15,9},{13,11},{10,12},{8,14},{23,17},{21,... | collective-permute-start | bytes 786440 | tf_op jit(solution)/shard_map/ppermute | solution.py:105
  22.2 3.2 %collective-permute-done.7.refs_8_ = bf16[2,64,1024]{2,1,0:T(8,128)(2,1)S(1)} collective-permute-done((bf16[2,64,1024]{2,1,0:T(8,128)(2,1)}, bf16[2,64,1024]{2,1,0:T(8,128)(2,1)S(1)}, u32[]{:S(2)}, u32[]{:S(2)}) %collective-permute-start.7) | collective-permute-done | bytes 262176 | tf_op jit(solution)/shard_map/ppermute | solution.py:105
  25.5 1.5 %collective-permute-start.4 = (bf16[2,64,1024]{2,1,0:T(8,128)(2,1)S(1)}, bf16[2,64,1024]{2,1,0:T(8,128)(2,1)S(1)}, u32[]{:S(2)}, u32[]{:S(2)}) collective-permute-start(bf16[2,64,1024]{2,1,0:T(8,128)(2,1)S(1)} %collective-permute-done.refs_1_), channel_id=1, source_target_pairs={{0,8},{1,9},{2,10},{3,11},{4,12},{5,13},{6,14},{7,15},{8,0},{9,1},... | collective-permute-start | bytes 786440 | tf_op jit(solution)/shard_map/ppermute | solution.py:103
  26.9 0.0 collective-permute-done.1.refs_2_
  26.9 0.0 collective-permute-start.5
  26.9 0.0 collective-permute-done.2.refs_3_
  26.9 0.5 %collective-permute-start.6 = (bf16[2,64,1024]{2,1,0:T(8,128)(2,1)S(1)}, bf16[2,64,1024]{2,1,0:T(8,128)(2,1)S(1)}, u32[]{:S(2)}, u32[]{:S(2)}) collective-permute-start(bf16[2,64,1024]{2,1,0:T(8,128)(2,1)S(1)} %collective-permute-done.2.refs_3_), channel_id=1, source_target_pairs={{0,8},{1,9},{2,10},{3,11},{4,12},{5,13},{6,14},{7,15},{8,0},{9,1},... | collective-permute-start | bytes 786440 | tf_op jit(solution)/shard_map/ppermute | solution.py:103
  27.4 0.0 collective-permute-done.3.refs_4_
  27.4 8.6 %collective-permute-done.10.refs_11_ = bf16[2,64,1024]{2,1,0:T(8,128)(2,1)S(1)} collective-permute-done((bf16[2,64,1024]{2,1,0:T(8,128)(2,1)}, bf16[2,64,1024]{2,1,0:T(8,128)(2,1)S(1)}, u32[]{:S(2)}, u32[]{:S(2)}) %collective-permute-start.10) | collective-permute-done | bytes 262176 | tf_op jit(solution)/shard_map/ppermute | solution.py:105
  36.1 0.0 collective-permute-done.5.refs_6_
  36.1 0.0 collective-permute-done.4.refs_5_
  36.1 0.0 collective-permute-done.6.refs_7_
  36.1 0.9 %copy-done = bf16[2,64,1024]{2,1,0:T(8,128)(2,1)S(1)} copy-done((bf16[2,64,1024]{2,1,0:T(8,128)(2,1)S(1)}, bf16[2,64,1024]{2,1,0:T(8,128)(2,1)}, u32[]{:S(2)}) %copy-start) | copy-done | bytes 262168
  37.0 2.4 %shard_map.17 = f32[2,256,512]{2,1,0:T(8,128)} custom-call(bf16[2,64,1024]{2,1,0:T(8,128)(2,1)S(1)} %copy-done, bf16[2,64,1024]{2,1,0:T(8,128)(2,1)S(1)} %collective-permute-done.refs_1_, bf16[2,64,1024]{2,1,0:T(8,128)(2,1)S(1)} %collective-permute-done.1.refs_2_, bf16[2,64,1024]{2,1,0:T(8,128)(2,1)S(1)} %collective-permute-done.2.refs_3_, ...), custom_call_target="tpu_custom_call" | custom-call | tf_op jit(solution)/shard_map/pallas_call | solution.py:108
  (1 shorter events, 0.0 us)
Async XLA Ops:
  0.0 9.4 %collective-permute-start = (bf16[2,64,1024]{2,1,0:T(8,128)(2,1)}, bf16[2,64,1024]{2,1,0:T(8,128)(2,1)S(1)}, u32[]{:S(2)}, u32[]{:S(2)}) collective-permute-start(bf16[2,64,1024]{2,1,0:T(8,128)(2,1)} %refs_0_.1), channel_id=1, source_target_pairs={{0,1},{1,0},{2,3},{3,2},{4,5},{5,4},{6,7},{7,6},{8,9},{9,8},{10,11... | collective-permute-start | bytes 786440 | tf_op jit(solution)/shard_map/ppermute | solution.py:103
  1.2 15.6 %collective-permute-start.9 = (bf16[2,64,1024]{2,1,0:T(8,128)(2,1)}, bf16[2,64,1024]{2,1,0:T(8,128)(2,1)S(1)}, u32[]{:S(2)}, u32[]{:S(2)}) collective-permute-start(bf16[2,64,1024]{2,1,0:T(8,128)(2,1)} %refs_0_.1), channel_id=1, source_target_pairs={{6,1},{4,3},{3,4},{1,6},{14,9},{12,11},{11,12},{9,14},{22,17},{20,... | collective-permute-start | bytes 786440 | tf_op jit(solution)/shard_map/ppermute | solution.py:105
  3.3 17.7 %collective-permute-start.8 = (bf16[2,64,1024]{2,1,0:T(8,128)(2,1)}, bf16[2,64,1024]{2,1,0:T(8,128)(2,1)S(1)}, u32[]{:S(2)}, u32[]{:S(2)}) collective-permute-start(bf16[2,64,1024]{2,1,0:T(8,128)(2,1)} %refs_0_.1), channel_id=1, source_target_pairs={{3,0},{5,1},{1,2},{7,3},{0,4},{6,5},{2,6},{4,7},{11,8},{13,9},{9,1... | collective-permute-start | bytes 786440 | tf_op jit(solution)/shard_map/ppermute | solution.py:105
  3.3 22.1 %collective-permute-start.7 = (bf16[2,64,1024]{2,1,0:T(8,128)(2,1)}, bf16[2,64,1024]{2,1,0:T(8,128)(2,1)S(1)}, u32[]{:S(2)}, u32[]{:S(2)}) collective-permute-start(bf16[2,64,1024]{2,1,0:T(8,128)(2,1)} %refs_0_.1), channel_id=1, source_target_pairs={{2,0},{4,1},{0,2},{6,3},{1,4},{7,5},{3,6},{5,7},{10,8},{12,9},{8,1... | collective-permute-start | bytes 786440 | tf_op jit(solution)/shard_map/ppermute | solution.py:105
  7.6 19.4 %collective-permute-start.1 = (bf16[2,64,1024]{2,1,0:T(8,128)(2,1)}, bf16[2,64,1024]{2,1,0:T(8,128)(2,1)S(1)}, u32[]{:S(2)}, u32[]{:S(2)}) collective-permute-start(bf16[2,64,1024]{2,1,0:T(8,128)(2,1)} %refs_0_.1), channel_id=1, source_target_pairs={{0,16},{1,17},{2,18},{3,19},{4,20},{5,21},{6,22},{7,23},{8,24},{9,... | collective-permute-start | bytes 786440 | tf_op jit(solution)/shard_map/ppermute | solution.py:103
  9.4 17.6 %collective-permute-start.2 = (bf16[2,64,1024]{2,1,0:T(8,128)(2,1)S(1)}, bf16[2,64,1024]{2,1,0:T(8,128)(2,1)S(1)}, u32[]{:S(2)}, u32[]{:S(2)}) collective-permute-start(bf16[2,64,1024]{2,1,0:T(8,128)(2,1)S(1)} %collective-permute-done.refs_1_), channel_id=1, source_target_pairs={{0,16},{1,17},{2,18},{3,19},{4,20},{5,21},{6,22},{7,23},{8,24},{9,... | collective-permute-start | bytes 786440 | tf_op jit(solution)/shard_map/ppermute | solution.py:103
  16.8 10.7 %collective-permute-start.3 = (bf16[2,64,1024]{2,1,0:T(8,128)(2,1)}, bf16[2,64,1024]{2,1,0:T(8,128)(2,1)S(1)}, u32[]{:S(2)}, u32[]{:S(2)}) collective-permute-start(bf16[2,64,1024]{2,1,0:T(8,128)(2,1)} %refs_0_.1), channel_id=1, source_target_pairs={{0,8},{1,9},{2,10},{3,11},{4,12},{5,13},{6,14},{7,15},{8,0},{9,1},... | collective-permute-start | bytes 786440 | tf_op jit(solution)/shard_map/ppermute | solution.py:103
  20.9 15.1 %collective-permute-start.10 = (bf16[2,64,1024]{2,1,0:T(8,128)(2,1)}, bf16[2,64,1024]{2,1,0:T(8,128)(2,1)S(1)}, u32[]{:S(2)}, u32[]{:S(2)}) collective-permute-start(bf16[2,64,1024]{2,1,0:T(8,128)(2,1)} %refs_0_.1), channel_id=1, source_target_pairs={{7,1},{5,3},{2,4},{0,6},{15,9},{13,11},{10,12},{8,14},{23,17},{21,... | collective-permute-start | bytes 786440 | tf_op jit(solution)/shard_map/ppermute | solution.py:105
  25.5 10.6 %collective-permute-start.4 = (bf16[2,64,1024]{2,1,0:T(8,128)(2,1)S(1)}, bf16[2,64,1024]{2,1,0:T(8,128)(2,1)S(1)}, u32[]{:S(2)}, u32[]{:S(2)}) collective-permute-start(bf16[2,64,1024]{2,1,0:T(8,128)(2,1)S(1)} %collective-permute-done.refs_1_), channel_id=1, source_target_pairs={{0,8},{1,9},{2,10},{3,11},{4,12},{5,13},{6,14},{7,15},{8,0},{9,1},... | collective-permute-start | bytes 786440 | tf_op jit(solution)/shard_map/ppermute | solution.py:103
  26.9 9.1 %collective-permute-start.5 = (bf16[2,64,1024]{2,1,0:T(8,128)(2,1)S(1)}, bf16[2,64,1024]{2,1,0:T(8,128)(2,1)S(1)}, u32[]{:S(2)}, u32[]{:S(2)}) collective-permute-start(bf16[2,64,1024]{2,1,0:T(8,128)(2,1)S(1)} %collective-permute-done.1.refs_2_), channel_id=1, source_target_pairs={{0,8},{1,9},{2,10},{3,11},{4,12},{5,13},{6,14},{7,15},{8,0},{9,1},... | collective-permute-start | bytes 786440 | tf_op jit(solution)/shard_map/ppermute | solution.py:103
  26.9 9.1 %collective-permute-start.6 = (bf16[2,64,1024]{2,1,0:T(8,128)(2,1)S(1)}, bf16[2,64,1024]{2,1,0:T(8,128)(2,1)S(1)}, u32[]{:S(2)}, u32[]{:S(2)}) collective-permute-start(bf16[2,64,1024]{2,1,0:T(8,128)(2,1)S(1)} %collective-permute-done.2.refs_3_), channel_id=1, source_target_pairs={{0,8},{1,9},{2,10},{3,11},{4,12},{5,13},{6,14},{7,15},{8,0},{9,1},... | collective-permute-start | bytes 786440 | tf_op jit(solution)/shard_map/ppermute | solution.py:103
  36.1 1.0 %copy-start = (bf16[2,64,1024]{2,1,0:T(8,128)(2,1)S(1)}, bf16[2,64,1024]{2,1,0:T(8,128)(2,1)}, u32[]{:S(2)}) copy-start(bf16[2,64,1024]{2,1,0:T(8,128)(2,1)} %refs_0_.1) | copy-start | bytes 786436

commit v2 on v0

v2 whole, which is shorter than its diff:
```python
import functools

import jax
import jax.numpy as jnp
from jax import lax
from jax.experimental import pallas as pl
from jax.experimental.pallas import tpu as pltpu
from jax.sharding import PartitionSpec as P

AXES = ("row", "col", "slab")
TILE = 256
ANY = pl.BlockSpec(memory_space=pl.ANY)
VMEM = pl.BlockSpec(memory_space=pltpu.VMEM)
PARAMS = pltpu.CompilerParams(vmem_limit_bytes=24 * 1024 * 1024)
EARLY, MIDDLE = 30_000_000_000, 10_000_000_000


def weight(flops):
    return pl.CostEstimate(flops=flops, bytes_accessed=1 << 18, transcendentals=0) if flops else None


def dot(left, right):
    return lax.dot_general(left, right, (((1,), (1,)), ((), ())), preferred_element_type=jnp.float32)


def in_vmem(arrays):
    return [pltpu.with_memory_space_constraint(array, pltpu.VMEM) for array in arrays]


def split_kernel(fields, *refs):
    outs, sems = refs[:-1], refs[-1]
    copies = [pltpu.make_async_copy(fields.at[i], out, sems.at[i]) for i, out in enumerate(outs)]
    for copy in copies:
        copy.start()
    for copy in copies:
        copy.wait()


def choose_kernel(sizes, own, far, keep, give):
    near = lax.div(lax.axis_index("col"), sizes[1] // 2) == lax.axis_index("slab")
    keep[...] = jnp.where(near, own[...], far[...])
    give[...] = jnp.where(near, far[...], own[...])


def order_kernel(sizes, offsets, own_real, own_imag, *refs):
    r, s = lax.axis_index("row"), lax.axis_index("slab")
    cols, mine = refs[:-1], refs[-1]
    size = own_real.shape[0]

    def place(dr, ds):
        at = lax.div(lax.bitwise_xor(r, dr), 2) * sizes[2] + lax.bitwise_xor(s, ds)
        return pl.ds(pl.multiple_of(at * size, size), size)

    for i, own in enumerate((own_real, own_imag)):
        mine[i, place(0, 0)] = own[...]
    for ref, (dr, ds) in zip(cols, offsets[1:]):
        mine[:, place(dr, ds)] = ref[...]


def rows_in_order(sizes, places, refs, left):
    c, s = lax.axis_index("col"), lax.axis_index("slab")
    for ref, (shift, turn) in zip(refs, places):
        size = ref.shape[0]
        at = lax.rem(lax.bitwise_xor(c, shift), sizes[1] // 2) * sizes[2] + lax.bitwise_xor(s, turn)
        left[pl.ds(pl.multiple_of(at * size, size), size)] = ref[...]


def over_columns(sizes, mine, other, step):
    group = mine.shape[1] // (sizes[0] // 2)
    core = lax.rem(lax.axis_index("row"), 2)
    for cols, which in ((mine, core), (other, 1 - core)):

        @pl.loop(0, mine.shape[1] // TILE)
        def _(tile):
            here = pl.ds(pl.multiple_of(tile * TILE, TILE), TILE)
            parts = []
            for i in range(TILE // group):
                at = (2 * (tile * (TILE // group) + i) + which) * group
                parts.append((slice(i * group, (i + 1) * group), pl.ds(pl.multiple_of(at, group), group)))
            step(cols[0, here], cols[1, here], parts)


def real_rows_kernel(sizes, places, mine, other, *refs):
    blocks, out, left = refs[:-2], refs[-2], refs[-1]
    rows_in_order(sizes, places, blocks, left)

    def step(real, imag, parts):
        with_real, with_imag = dot(left[...], real), dot(left[...], imag)
        for part, at in parts:
            out[0, :, at] = with_real[:, part]
            out[1, :, at] = with_imag[:, part]

    over_columns(sizes, mine, other, step)


def imag_rows_kernel(sizes, places, mine, other, so_far, *refs):
    blocks, out, left = refs[:-2], refs[-2], refs[-1]
    rows_in_order(sizes, places, blocks, left)

    def step(real, imag, parts):
        with_real, with_imag = dot(left[...], real), dot(left[...], imag)
        for part, at in parts:
            out[0, :, at] = so_far[0, :, at] + with_imag[:, part]
            out[1, :, at] = so_far[1, :, at] - with_real[:, part]

    over_columns(sizes, mine, other, step)


def solution(mesh):
    sizes = tuple(mesh.shape[axis] for axis in AXES)
    rows, cols, slabs = sizes
    half = cols // 2

    def exchange(array, dr, dc, ds):
        pairs = []
        for r in range(rows):
            for c in range(cols):
                for s in range(slabs):
                    pairs.append(((r * cols + c) * slabs + s, ((r ^ dr) * cols + (c ^ dc)) * slabs + (s ^ ds)))
        return lax.ppermute(array, AXES, pairs)

    def body(fields):
        _, size, pixels = fields.shape
        out_rows, out_cols = half * slabs * size, rows * slabs * size
        part_shape = pltpu.VMEM((size, pixels), fields.dtype)

        def call(kernel, out_shape, arrays, scratch=(), specs=None, flops=0):
            return pl.pallas_call(
                kernel,
                out_shape=out_shape,
                in_specs=specs or [VMEM] * len(arrays),
                out_specs=jax.tree.map(lambda _: VMEM, out_shape),
                scratch_shapes=scratch,
                compiler_params=PARAMS,
                cost_estimate=weight(flops),
            )(*(arrays if specs else in_vmem(arrays)))

        own = call(
            split_kernel, [part_shape] * 2, [pltpu.with_memory_space_constraint(fields, pltpu.HBM)],
            [pltpu.SemaphoreType.DMA((2,))], [ANY],
        )
        blocks, offsets = [fields], [(0, 0)]
        steps = [(0, 1)]
        bit = rows // 2
        while bit > 1:
            steps.append((bit, 0))
            bit //= 2
        for dr, ds in steps:
            blocks = blocks + [exchange(block, dr, 0, ds) for block in blocks]
            offsets = offsets + [(a ^ dr, b ^ ds) for a, b in offsets]
        mine = call(
            functools.partial(order_kernel, sizes, offsets),
            pltpu.VMEM((2, out_cols // 2, pixels), fields.dtype), [*own, *blocks[1:]],
        )
        other = exchange(mine, 1, 0, 0)
        places = [(shift, turn) for shift in range(half) for turn in range(slabs)]
        slots = []
        for part in own:
            far = exchange(part, 0, half, 0)
            keep, give = call(functools.partial(choose_kernel, sizes), [part_shape] * 2, [part, far], flops=EARLY)
            got = [keep]
            for shift, turn in places[1:]:
                got.append(exchange(give if turn else keep, 0, shift, turn))
            slots.append(got)
        left = pltpu.VMEM((out_rows, pixels), fields.dtype)
        so_far = call(
            functools.partial(real_rows_kernel, sizes, places),
            pltpu.VMEM((2, out_rows, out_cols), jnp.float32), [mine, other, *slots[0]], [left], flops=MIDDLE,
        )
        return call(
            functools.partial(imag_rows_kernel, sizes, places),
            jax.ShapeDtypeStruct((2, out_rows, out_cols), jnp.float32), [mine, other, so_far, *slots[1]], [left],
        )

    placed = (P(None, AXES, None),)
    return jax.shard_map(
        body, mesh=mesh, in_specs=placed, out_specs=P(None, ("row", "slab"), "col"), check_vma=False
    )
```

time: 98.9 us -> 32 us (0.32)
  waiting for transfers between devices: 65.4 us -> 12.9 us
  starting transfers between devices: 0.08 us -> 15.3 us
  between operations: 13.2 us -> 0.07 us
  blocking collectives: 9.21 us -> 0 us
  local copies, waits for them, and re-layouts: 6.04 us -> 0.01 us
  Pallas kernels: 0 us -> 3.62 us
  other arithmetic: 3.24 us -> 0 us
  matrix products: 1.47 us -> 0 us
    all_gather x2 -> x0, waiting for transfers between devices: 44.7 us -> none  [the longest x1 28.3 us: body(): row_block = lax.all_gather(local, 'col', axis=1, tiled=True)]
    reduce_scatter x1 -> x0, waiting for transfers between devices: 20 us -> none  [body(): lax.psum_scatter(terms.astype(jnp.bfloat16), 'slab', scatter_dimension=1,...]
    ppermute x0 -> x12, starting transfers between devices: none -> 15.3 us  [exchange(): return lax.ppermute(array, AXES, pairs)]
    ppermute x0 -> x12, waiting for transfers between devices: none -> 12.9 us  [exchange(): return lax.ppermute(array, AXES, pairs)]
    all_to_all x1 -> x0, blocking collectives: 9.21 us -> none  [body(): lax.all_to_all(fields, 'slab', split_axis=2, concat_axis=1, tiled=True)]
    pallas_call x0 -> x6, Pallas kernels: none -> 3.62 us  [call(): pl.pallas_call(kernel, out_shape=out_shape, in_specs=specs or [VMEM] * le...]
    squeeze x2 -> x0, local copies, waits for them, and re-layouts: 2.53 us -> none  [the longest x1 1.27 us: pair_terms(): right_real = jnp.concatenate([piece[0], piece[1]], axis=1)]
    unnamed x5 -> x2, local copies, waits for them, and re-layouts: 2.48 us -> 0.01 us
  transfers between devices with their start and end apart: 3 -> 12, of which waited for: 3 -> 5; matrix products, arithmetic and copies ran while one was open for 1% -> 0% of each run, Pallas kernels for 0% -> 6%
where the time goes in v2:
time: 32 us; the launch traced here: 31.9 us
  starting transfers between devices  15.3 us (48%)
  waiting for transfers between devices  12.9 us (40%)
  Pallas kernels  3.62 us (11%)
    ppermute x12, starting transfers between devices, exchange(): return lax.ppermute(array, AXES, pairs)  15.3 us
    ppermute x12, waiting for transfers between devices, exchange(): return lax.ppermute(array, AXES, pairs)  12.9 us
    pallas_call x6, Pallas kernels, call(): pl.pallas_call(kernel, out_shape=out_shape, in_specs=specs or [VMEM] * le...  3.62 us
  transfers between devices with their start and end apart: 12, of which 5 were waited for; matrix products, arithmetic and copies ran while one was open for 0% of the time, Pallas kernels for 6%

profile of v2, /device:TPU:0, one launch (start us, length us, event | category | flops | bytes accessed | tf_op | source)
XLA Modules:
  0.0 31.9 jit_solution(3230720183287352142)
XLA Ops:
  0.0 3.0 %collective-permute-start = (bf16[2,64,1024]{2,1,0:T(8,128)(2,1)}, bf16[2,64,1024]{2,1,0:T(8,128)(2,1)S(1)}, u32[]{:S(2)}, u32[]{:S(2)}) collective-permute-start(bf16[2,64,1024]{2,1,0:T(8,128)(2,1)} %fields.1), channel_id=1, source_target_pairs={{0,1},{1,0},{2,3},{3,2},{4,5},{5,4},{6,7},{7,6},{8,9},{9,8},{10,11... | collective-permute-start | bytes 786440 | tf_op jit(solution)/shard_map/ppermute | solution.py:120
  3.0 1.0 %shard_map.17 = (bf16[64,1024]{1,0:T(8,128)(2,1)S(1)}, bf16[64,1024]{1,0:T(8,128)(2,1)S(1)}) custom-call(bf16[2,64,1024]{2,1,0:T(8,128)(2,1)} %fields.1), custom_call_target="tpu_custom_call" | custom-call | tf_op jit(solution)/shard_map/pallas_call | solution.py:128
  4.0 2.7 %collective-permute-start.4 = (bf16[64,1024]{1,0:T(8,128)(2,1)S(1)}, bf16[64,1024]{1,0:T(8,128)(2,1)S(1)}, u32[]{:S(2)}, u32[]{:S(2)}) collective-permute-start(bf16[64,1024]{1,0:T(8,128)(2,1)S(1)} %get-tuple-element.11.own_real.own), channel_id=1, source_target_pairs={{0,4},{1,5},{2,6},{3,7},{4,0},{5,1},{6,2},{7,3},{8,12},{9,13},{10,... | collective-permute-start | bytes 393224 | tf_op jit(solution)/shard_map/ppermute | solution.py:120
  6.6 1.5 %collective-permute-start.1 = (bf16[2,64,1024]{2,1,0:T(8,128)(2,1)S(1)}, bf16[2,64,1024]{2,1,0:T(8,128)(2,1)S(1)}, u32[]{:S(2)}, u32[]{:S(2)}) collective-permute-start(bf16[2,64,1024]{2,1,0:T(8,128)(2,1)S(1)} %copy-done), channel_id=1, source_target_pairs={{0,16},{1,17},{2,18},{3,19},{4,20},{5,21},{6,22},{7,23},{8,24},{9,... | collective-permute-start | bytes 786440 | tf_op jit(solution)/shard_map/ppermute | solution.py:120
  8.1 0.3 %collective-permute-start.8 = (bf16[64,1024]{1,0:T(8,128)(2,1)S(1)}, bf16[64,1024]{1,0:T(8,128)(2,1)S(1)}, u32[]{:S(2)}, u32[]{:S(2)}) collective-permute-start(bf16[64,1024]{1,0:T(8,128)(2,1)S(1)} %get-tuple-element.12.own_imag.own), channel_id=1, source_target_pairs={{0,4},{1,5},{2,6},{3,7},{4,0},{5,1},{6,2},{7,3},{8,12},{9,13},{10,... | collective-permute-start | bytes 393224 | tf_op jit(solution)/shard_map/ppermute | solution.py:120
  8.5 1.1 %collective-permute-done.refs_0_ = bf16[2,64,1024]{2,1,0:T(8,128)(2,1)S(1)} collective-permute-done((bf16[2,64,1024]{2,1,0:T(8,128)(2,1)}, bf16[2,64,1024]{2,1,0:T(8,128)(2,1)S(1)}, u32[]{:S(2)}, u32[]{:S(2)}) %collective-permute-start) | collective-permute-done | bytes 262176 | tf_op jit(solution)/shard_map/ppermute | solution.py:120
  9.6 1.6 %collective-permute-start.2 = (bf16[2,64,1024]{2,1,0:T(8,128)(2,1)S(1)}, bf16[2,64,1024]{2,1,0:T(8,128)(2,1)S(1)}, u32[]{:S(2)}, u32[]{:S(2)}) collective-permute-start(bf16[2,64,1024]{2,1,0:T(8,128)(2,1)S(1)} %collective-permute-done.refs_0_), channel_id=1, source_target_pairs={{0,16},{1,17},{2,18},{3,19},{4,20},{5,21},{6,22},{7,23},{8,24},{9,... | collective-permute-start | bytes 786440 | tf_op jit(solution)/shard_map/ppermute | solution.py:120
  11.2 5.5 %collective-permute-done.4.far = bf16[64,1024]{1,0:T(8,128)(2,1)S(1)} collective-permute-done((bf16[64,1024]{1,0:T(8,128)(2,1)S(1)}, bf16[64,1024]{1,0:T(8,128)(2,1)S(1)}, u32[]{:S(2)}, u32[]{:S(2)}) %collective-permute-start.4) | collective-permute-done | bytes 131104 | tf_op jit(solution)/shard_map/ppermute | solution.py:120
  16.7 0.1 collective-permute-start.7
  16.8 1.1 %collective-permute-start.5 = (bf16[64,1024]{1,0:T(8,128)(2,1)S(1)}, bf16[64,1024]{1,0:T(8,128)(2,1)S(1)}, u32[]{:S(2)}, u32[]{:S(2)}) collective-permute-start(bf16[64,1024]{1,0:T(8,128)(2,1)S(1)} %get-tuple-element.14), channel_id=1, source_target_pairs={{0,1},{1,0},{2,3},{3,2},{4,5},{5,4},{6,7},{7,6},{8,9},{9,8},{10,11... | collective-permute-start | bytes 393224 | tf_op jit(solution)/shard_map/ppermute | solution.py:120
  17.8 0.0 collective-permute-done.1.refs_1_
  17.8 2.4 %collective-permute-start.6 = (bf16[64,1024]{1,0:T(8,128)(2,1)S(1)}, bf16[64,1024]{1,0:T(8,128)(2,1)S(1)}, u32[]{:S(2)}, u32[]{:S(2)}) collective-permute-start(bf16[64,1024]{1,0:T(8,128)(2,1)S(1)} %get-tuple-element.13.refs_0_), channel_id=1, source_target_pairs={{0,2},{1,3},{2,0},{3,1},{4,6},{5,7},{6,4},{7,5},{8,10},{9,11},{10,... | collective-permute-start | bytes 393224 | tf_op jit(solution)/shard_map/ppermute | solution.py:120
  20.3 0.0 collective-permute-done.2.refs_2_
  20.3 0.1 shard_map.18.mine
  20.4 0.1 collective-permute-start.3
  20.4 0.0 collective-permute-done.8.far
  20.5 1.0 %collective-permute-start.11 = (bf16[64,1024]{1,0:T(8,128)(2,1)S(1)}, bf16[64,1024]{1,0:T(8,128)(2,1)S(1)}, u32[]{:S(2)}, u32[]{:S(2)}) collective-permute-start(bf16[64,1024]{1,0:T(8,128)(2,1)S(1)} %get-tuple-element.16), channel_id=1, source_target_pairs={{0,3},{1,2},{2,1},{3,0},{4,7},{5,6},{6,5},{7,4},{8,11},{9,10},{10,... | collective-permute-start | bytes 393224 | tf_op jit(solution)/shard_map/ppermute | solution.py:120
  21.5 2.9 %collective-permute-done.6.refs_2_ = bf16[64,1024]{1,0:T(8,128)(2,1)S(1)} collective-permute-done((bf16[64,1024]{1,0:T(8,128)(2,1)S(1)}, bf16[64,1024]{1,0:T(8,128)(2,1)S(1)}, u32[]{:S(2)}, u32[]{:S(2)}) %collective-permute-start.6) | collective-permute-done | bytes 131104 | tf_op jit(solution)/shard_map/ppermute | solution.py:120
  24.5 0.2 collective-permute-start.9
  24.7 1.4 %collective-permute-start.10 = (bf16[64,1024]{1,0:T(8,128)(2,1)S(1)}, bf16[64,1024]{1,0:T(8,128)(2,1)S(1)}, u32[]{:S(2)}, u32[]{:S(2)}) collective-permute-start(bf16[64,1024]{1,0:T(8,128)(2,1)S(1)} %get-tuple-element.15.refs_0_), channel_id=1, source_target_pairs={{0,2},{1,3},{2,0},{3,1},{4,6},{5,7},{6,4},{7,5},{8,10},{9,11},{10,... | collective-permute-start | bytes 393224 | tf_op jit(solution)/shard_map/ppermute | solution.py:120
  26.0 0.7 %shard_map.20.so_far = f32[2,256,512]{2,1,0:T(8,128)S(1)} custom-call(bf16[2,256,1024]{2,1,0:T(8,128)(2,1)S(1)} %shard_map.18.mine, bf16[2,256,1024]{2,1,0:T(8,128)(2,1)S(1)} %collective-permute-done.3.other, bf16[64,1024]{1,0:T(8,128)(2,1)S(1)} %get-tuple-element.13.refs_0_, bf16[64,1024]{1,0:T(8,128)(2,1)S(1)} %collective-permute-done.5.refs_1_, ...), custom_call_target="tpu_custom_call" | custom-call | flops 10000000000 | bytes 262144 | tf_op jit(solution)/shard_map/pallas_call | solution.py:128
  26.8 2.9 %collective-permute-done.10.refs_2_ = bf16[64,1024]{1,0:T(8,128)(2,1)S(1)} collective-permute-done((bf16[64,1024]{1,0:T(8,128)(2,1)S(1)}, bf16[64,1024]{1,0:T(8,128)(2,1)S(1)}, u32[]{:S(2)}, u32[]{:S(2)}) %collective-permute-start.10) | collective-permute-done | bytes 131104 | tf_op jit(solution)/shard_map/ppermute | solution.py:120
  29.7 0.5 %collective-permute-done.9.refs_1_ = bf16[64,1024]{1,0:T(8,128)(2,1)S(1)} collective-permute-done((bf16[64,1024]{1,0:T(8,128)(2,1)S(1)}, bf16[64,1024]{1,0:T(8,128)(2,1)S(1)}, u32[]{:S(2)}, u32[]{:S(2)}) %collective-permute-start.9) | collective-permute-done | bytes 131104 | tf_op jit(solution)/shard_map/ppermute | solution.py:120
  30.2 1.7 %shard_map.22 = f32[2,256,512]{2,1,0:T(8,128)} custom-call(bf16[2,256,1024]{2,1,0:T(8,128)(2,1)S(1)} %shard_map.18.mine, bf16[2,256,1024]{2,1,0:T(8,128)(2,1)S(1)} %collective-permute-done.3.other, f32[2,256,512]{2,1,0:T(8,128)S(1)} %shard_map.20.so_far, bf16[64,1024]{1,0:T(8,128)(2,1)S(1)} %get-tuple-element.15.refs_0_, ...), custom_call_target="tpu_custom_call" | custom-call | tf_op jit(solution)/shard_map/pallas_call | solution.py:128
  (8 shorter events, 0.1 us)
Async XLA Ops:
  0.0 6.6 %copy-start = (bf16[2,64,1024]{2,1,0:T(8,128)(2,1)S(1)}, bf16[2,64,1024]{2,1,0:T(8,128)(2,1)}, u32[]{:S(2)}) copy-start(bf16[2,64,1024]{2,1,0:T(8,128)(2,1)} %fields.1) | copy-start | bytes 786436
  0.0 9.6 %collective-permute-start = (bf16[2,64,1024]{2,1,0:T(8,128)(2,1)}, bf16[2,64,1024]{2,1,0:T(8,128)(2,1)S(1)}, u32[]{:S(2)}, u32[]{:S(2)}) collective-permute-start(bf16[2,64,1024]{2,1,0:T(8,128)(2,1)} %fields.1), channel_id=1, source_target_pairs={{0,1},{1,0},{2,3},{3,2},{4,5},{5,4},{6,7},{7,6},{8,9},{9,8},{10,11... | collective-permute-start | bytes 786440 | tf_op jit(solution)/shard_map/ppermute | solution.py:120
  4.0 12.7 %collective-permute-start.4 = (bf16[64,1024]{1,0:T(8,128)(2,1)S(1)}, bf16[64,1024]{1,0:T(8,128)(2,1)S(1)}, u32[]{:S(2)}, u32[]{:S(2)}) collective-permute-start(bf16[64,1024]{1,0:T(8,128)(2,1)S(1)} %get-tuple-element.11.own_real.own), channel_id=1, source_target_pairs={{0,4},{1,5},{2,6},{3,7},{4,0},{5,1},{6,2},{7,3},{8,12},{9,13},{10,... | collective-permute-start | bytes 393224 | tf_op jit(solution)/shard_map/ppermute | solution.py:120
  6.6 11.2 %collective-permute-start.1 = (bf16[2,64,1024]{2,1,0:T(8,128)(2,1)S(1)}, bf16[2,64,1024]{2,1,0:T(8,128)(2,1)S(1)}, u32[]{:S(2)}, u32[]{:S(2)}) collective-permute-start(bf16[2,64,1024]{2,1,0:T(8,128)(2,1)S(1)} %copy-done), channel_id=1, source_target_pairs={{0,16},{1,17},{2,18},{3,19},{4,20},{5,21},{6,22},{7,23},{8,24},{9,... | collective-permute-start | bytes 786440 | tf_op jit(solution)/shard_map/ppermute | solution.py:120
  8.1 12.3 %collective-permute-start.8 = (bf16[64,1024]{1,0:T(8,128)(2,1)S(1)}, bf16[64,1024]{1,0:T(8,128)(2,1)S(1)}, u32[]{:S(2)}, u32[]{:S(2)}) collective-permute-start(bf16[64,1024]{1,0:T(8,128)(2,1)S(1)} %get-tuple-element.12.own_imag.own), channel_id=1, source_target_pairs={{0,4},{1,5},{2,6},{3,7},{4,0},{5,1},{6,2},{7,3},{8,12},{9,13},{10,... | collective-permute-start | bytes 393224 | tf_op jit(solution)/shard_map/ppermute | solution.py:120
  9.6 10.7 %collective-permute-start.2 = (bf16[2,64,1024]{2,1,0:T(8,128)(2,1)S(1)}, bf16[2,64,1024]{2,1,0:T(8,128)(2,1)S(1)}, u32[]{:S(2)}, u32[]{:S(2)}) collective-permute-start(bf16[2,64,1024]{2,1,0:T(8,128)(2,1)S(1)} %collective-permute-done.refs_0_), channel_id=1, source_target_pairs={{0,16},{1,17},{2,18},{3,19},{4,20},{5,21},{6,22},{7,23},{8,24},{9,... | collective-permute-start | bytes 786440 | tf_op jit(solution)/shard_map/ppermute | solution.py:120
  16.7 7.9 %collective-permute-start.7 = (bf16[64,1024]{1,0:T(8,128)(2,1)S(1)}, bf16[64,1024]{1,0:T(8,128)(2,1)S(1)}, u32[]{:S(2)}, u32[]{:S(2)}) collective-permute-start(bf16[64,1024]{1,0:T(8,128)(2,1)S(1)} %get-tuple-element.14), channel_id=1, source_target_pairs={{0,3},{1,2},{2,1},{3,0},{4,7},{5,6},{6,5},{7,4},{8,11},{9,10},{10,... | collective-permute-start | bytes 393224 | tf_op jit(solution)/shard_map/ppermute | solution.py:120
  16.8 9.2 %collective-permute-start.5 = (bf16[64,1024]{1,0:T(8,128)(2,1)S(1)}, bf16[64,1024]{1,0:T(8,128)(2,1)S(1)}, u32[]{:S(2)}, u32[]{:S(2)}) collective-permute-start(bf16[64,1024]{1,0:T(8,128)(2,1)S(1)} %get-tuple-element.14), channel_id=1, source_target_pairs={{0,1},{1,0},{2,3},{3,2},{4,5},{5,4},{6,7},{7,6},{8,9},{9,8},{10,11... | collective-permute-start | bytes 393224 | tf_op jit(solution)/shard_map/ppermute | solution.py:120
  17.8 6.6 %collective-permute-start.6 = (bf16[64,1024]{1,0:T(8,128)(2,1)S(1)}, bf16[64,1024]{1,0:T(8,128)(2,1)S(1)}, u32[]{:S(2)}, u32[]{:S(2)}) collective-permute-start(bf16[64,1024]{1,0:T(8,128)(2,1)S(1)} %get-tuple-element.13.refs_0_), channel_id=1, source_target_pairs={{0,2},{1,3},{2,0},{3,1},{4,6},{5,7},{6,4},{7,5},{8,10},{9,11},{10,... | collective-permute-start | bytes 393224 | tf_op jit(solution)/shard_map/ppermute | solution.py:120
  20.4 5.7 %collective-permute-start.3 = (bf16[2,256,1024]{2,1,0:T(8,128)(2,1)S(1)}, bf16[2,256,1024]{2,1,0:T(8,128)(2,1)S(1)}, u32[]{:S(2)}, u32[]{:S(2)}) collective-permute-start(bf16[2,256,1024]{2,1,0:T(8,128)(2,1)S(1)} %shard_map.18.mine), channel_id=1, source_target_pairs={{0,8},{1,9},{2,10},{3,11},{4,12},{5,13},{6,14},{7,15},{8,0},{9,1},... | collective-permute-start | bytes 3145736 | tf_op jit(solution)/shard_map/ppermute | solution.py:120
  20.5 9.2 %collective-permute-start.11 = (bf16[64,1024]{1,0:T(8,128)(2,1)S(1)}, bf16[64,1024]{1,0:T(8,128)(2,1)S(1)}, u32[]{:S(2)}, u32[]{:S(2)}) collective-permute-start(bf16[64,1024]{1,0:T(8,128)(2,1)S(1)} %get-tuple-element.16), channel_id=1, source_target_pairs={{0,3},{1,2},{2,1},{3,0},{4,7},{5,6},{6,5},{7,4},{8,11},{9,10},{10,... | collective-permute-start | bytes 393224 | tf_op jit(solution)/shard_map/ppermute | solution.py:120
  24.5 5.7 %collective-permute-start.9 = (bf16[64,1024]{1,0:T(8,128)(2,1)S(1)}, bf16[64,1024]{1,0:T(8,128)(2,1)S(1)}, u32[]{:S(2)}, u32[]{:S(2)}) collective-permute-start(bf16[64,1024]{1,0:T(8,128)(2,1)S(1)} %get-tuple-element.16), channel_id=1, source_target_pairs={{0,1},{1,0},{2,3},{3,2},{4,5},{5,4},{6,7},{7,6},{8,9},{9,8},{10,11... | collective-permute-start | bytes 393224 | tf_op jit(solution)/shard_map/ppermute | solution.py:120
  24.7 5.0 %collective-permute-start.10 = (bf16[64,1024]{1,0:T(8,128)(2,1)S(1)}, bf16[64,1024]{1,0:T(8,128)(2,1)S(1)}, u32[]{:S(2)}, u32[]{:S(2)}) collective-permute-start(bf16[64,1024]{1,0:T(8,128)(2,1)S(1)} %get-tuple-element.15.refs_0_), channel_id=1, source_target_pairs={{0,2},{1,3},{2,0},{3,1},{4,6},{5,7},{6,4},{7,5},{8,10},{9,11},{10,... | collective-permute-start | bytes 393224 | tf_op jit(solution)/shard_map/ppermute | solution.py:120

commit v3 on v2

--- a/solution.py
+++ b/solution.py
@@ -34,6 +34,10 @@
         copy.start()
     for copy in copies:
         copy.wait()
+
+
+def relay_kernel(part, after, out):
+    out[...] = part[...]
 
 
 def choose_kernel(sizes, own, far, keep, give):
@@ -76,7 +80,7 @@
             parts = []
             for i in range(TILE // group):
                 at = (2 * (tile * (TILE // group) + i) + which) * group
-                parts.append((slice(i * group, (i + 1) * group), pl.ds(pl.multiple_of(at, group), group)))
+                parts.append((slice(i * group, (i + 1) * group), pl.multiple_of(at, group)))
             step(cols[0, here], cols[1, here], parts)
 
 
@@ -87,23 +91,34 @@
     def step(real, imag, parts):
         with_real, with_imag = dot(left[...], real), dot(left[...], imag)
         for part, at in parts:
-            out[0, :, at] = with_real[:, part]
-            out[1, :, at] = with_imag[:, part]
+            here = pl.ds(at, mine.shape[1] // (sizes[0] // 2))
+            out[0, :, here] = with_real[:, part]
+            out[1, :, here] = with_imag[:, part]
 
     over_columns(sizes, mine, other, step)
 
 
 def imag_rows_kernel(sizes, places, mine, other, so_far, *refs):
-    blocks, out, left = refs[:-2], refs[-2], refs[-1]
+    blocks, (out, left, wide, sem) = refs[:-4], refs[-4:]
     rows_in_order(sizes, places, blocks, left)
+    group = mine.shape[1] // (sizes[0] // 2)
+
+    def copy(at):
+        return pltpu.make_async_copy(wide.at[:, :, pl.ds(at, group)], out.at[:, :, pl.ds(at, group)], sem.at[at // group])
 
     def step(real, imag, parts):
         with_real, with_imag = dot(left[...], real), dot(left[...], imag)
         for part, at in parts:
-            out[0, :, at] = so_far[0, :, at] + with_imag[:, part]
-            out[1, :, at] = so_far[1, :, at] - with_real[:, part]
+            here = pl.ds(at, group)
+            wide[0, :, here] = so_far[0, :, here] + with_imag[:, part]
+            wide[1, :, here] = so_far[1, :, here] - with_real[:, part]
+            copy(at).start()
 
     over_columns(sizes, mine, other, step)
+
+    @pl.loop(0, out.shape[2] // group)
+    def _(i):
+        copy(pl.multiple_of(i * group, group)).wait()
 
 
 def solution(mesh):
@@ -124,12 +139,12 @@
         out_rows, out_cols = half * slabs * size, rows * slabs * size
         part_shape = pltpu.VMEM((size, pixels), fields.dtype)
 
-        def call(kernel, out_shape, arrays, scratch=(), specs=None, flops=0):
+        def call(kernel, out_shape, arrays, scratch=(), specs=None, flops=0, out_spec=VMEM):
             return pl.pallas_call(
                 kernel,
                 out_shape=out_shape,
                 in_specs=specs or [VMEM] * len(arrays),
-                out_specs=jax.tree.map(lambda _: VMEM, out_shape),
+                out_specs=jax.tree.map(lambda _: out_spec, out_shape),
                 scratch_shapes=scratch,
                 compiler_params=PARAMS,
                 cost_estimate=weight(flops),
@@ -155,7 +170,9 @@
         other = exchange(mine, 1, 0, 0)
         places = [(shift, turn) for shift in range(half) for turn in range(slabs)]
         slots = []
-        for part in own:
+        for i, part in enumerate(own):
+            if i > 0:
+                part = call(relay_kernel, part_shape, [part, blocks[1]])
             far = exchange(part, 0, half, 0)
             keep, give = call(functools.partial(choose_kernel, sizes), [part_shape] * 2, [part, far], flops=EARLY)
             got = [keep]
@@ -169,7 +186,8 @@
         )
         return call(
             functools.partial(imag_rows_kernel, sizes, places),
-            jax.ShapeDtypeStruct((2, out_rows, out_cols), jnp.float32), [mine, other, so_far, *slots[1]], [left],
+            jax.ShapeDtypeStruct((2, out_rows, out_cols), jnp.float32), [mine, other, so_far, *slots[1]],
+            [left, pltpu.VMEM((2, out_rows, out_cols), jnp.float32), pltpu.SemaphoreType.DMA((rows,))], out_spec=ANY,
         )
 
     placed = (P(None, AXES, None),)

time: 32 us -> 31.4 us (0.981)
  waiting for transfers between devices: 12.9 us -> 9.09 us
  starting transfers between devices: 15.3 us -> 18.6 us
    ppermute x12, waiting for transfers between devices: 12.9 us -> 9.09 us  [exchange(): return lax.ppermute(array, AXES, pairs)]
    ppermute x12, starting transfers between devices: 15.3 us -> 18.6 us  [exchange(): return lax.ppermute(array, AXES, pairs)]
    pallas_call x6 -> x7, Pallas kernels: 3.62 us -> 3.53 us  [call(): pl.pallas_call(kernel, out_shape=out_shape, in_specs=specs or [VMEM] * le...]
where the time goes in v3:
time: 31.4 us; the launch traced here: 31.2 us
  starting transfers between devices  18.6 us (59%)
  waiting for transfers between devices  9.09 us (29%)
  Pallas kernels  3.53 us (11%)
    ppermute x12, starting transfers between devices, exchange(): return lax.ppermute(array, AXES, pairs)  18.6 us
    ppermute x12, waiting for transfers between devices, exchange(): return lax.ppermute(array, AXES, pairs)  9.09 us
    pallas_call x7, Pallas kernels, call(): pl.pallas_call(kernel, out_shape=out_shape, in_specs=specs or [VMEM] * le...  3.53 us
  transfers between devices with their start and end apart: 12, of which 5 were waited for; matrix products, arithmetic and copies ran while one was open for 0% of the time, Pallas kernels for 6%

profile of v3, /device:TPU:0, one launch (start us, length us, event | category | flops | bytes accessed | tf_op | source)
XLA Modules:
  0.0 31.2 jit_solution(15381290649992952232)
XLA Ops:
  0.0 3.0 %collective-permute-start = (bf16[2,64,1024]{2,1,0:T(8,128)(2,1)}, bf16[2,64,1024]{2,1,0:T(8,128)(2,1)S(1)}, u32[]{:S(2)}, u32[]{:S(2)}) collective-permute-start(bf16[2,64,1024]{2,1,0:T(8,128)(2,1)} %fields.1), channel_id=1, source_target_pairs={{0,1},{1,0},{2,3},{3,2},{4,5},{5,4},{6,7},{7,6},{8,9},{9,8},{10,11... | collective-permute-start | bytes 786440 | tf_op jit(solution)/shard_map/ppermute | solution.py:135
  3.0 1.0 %shard_map.17 = (bf16[64,1024]{1,0:T(8,128)(2,1)S(1)}, bf16[64,1024]{1,0:T(8,128)(2,1)S(1)}) custom-call(bf16[2,64,1024]{2,1,0:T(8,128)(2,1)} %fields.1), custom_call_target="tpu_custom_call" | custom-call | tf_op jit(solution)/shard_map/pallas_call | solution.py:143
  4.0 2.7 %collective-permute-start.4 = (bf16[64,1024]{1,0:T(8,128)(2,1)S(1)}, bf16[64,1024]{1,0:T(8,128)(2,1)S(1)}, u32[]{:S(2)}, u32[]{:S(2)}) collective-permute-start(bf16[64,1024]{1,0:T(8,128)(2,1)S(1)} %get-tuple-element.11.own_real.own), channel_id=1, source_target_pairs={{0,4},{1,5},{2,6},{3,7},{4,0},{5,1},{6,2},{7,3},{8,12},{9,13},{10,... | collective-permute-start | bytes 393224 | tf_op jit(solution)/shard_map/ppermute | solution.py:135
  6.6 1.5 %collective-permute-start.1 = (bf16[2,64,1024]{2,1,0:T(8,128)(2,1)S(1)}, bf16[2,64,1024]{2,1,0:T(8,128)(2,1)S(1)}, u32[]{:S(2)}, u32[]{:S(2)}) collective-permute-start(bf16[2,64,1024]{2,1,0:T(8,128)(2,1)S(1)} %copy-done), channel_id=1, source_target_pairs={{0,16},{1,17},{2,18},{3,19},{4,20},{5,21},{6,22},{7,23},{8,24},{9,... | collective-permute-start | bytes 786440 | tf_op jit(solution)/shard_map/ppermute | solution.py:135
  8.1 1.4 %collective-permute-done.refs_0_.after = bf16[2,64,1024]{2,1,0:T(8,128)(2,1)S(1)} collective-permute-done((bf16[2,64,1024]{2,1,0:T(8,128)(2,1)}, bf16[2,64,1024]{2,1,0:T(8,128)(2,1)S(1)}, u32[]{:S(2)}, u32[]{:S(2)}) %collective-permute-start) | collective-permute-done | bytes 262176 | tf_op jit(solution)/shard_map/ppermute | solution.py:135
  9.6 2.8 %collective-permute-start.8 = (bf16[64,1024]{1,0:T(8,128)(2,1)S(1)}, bf16[64,1024]{1,0:T(8,128)(2,1)S(1)}, u32[]{:S(2)}, u32[]{:S(2)}) collective-permute-start(bf16[64,1024]{1,0:T(8,128)(2,1)S(1)} %shard_map.21.own), channel_id=1, source_target_pairs={{0,4},{1,5},{2,6},{3,7},{4,0},{5,1},{6,2},{7,3},{8,12},{9,13},{10,... | collective-permute-start | bytes 393224 | tf_op jit(solution)/shard_map/ppermute | solution.py:135
  12.4 1.5 %collective-permute-start.2 = (bf16[2,64,1024]{2,1,0:T(8,128)(2,1)S(1)}, bf16[2,64,1024]{2,1,0:T(8,128)(2,1)S(1)}, u32[]{:S(2)}, u32[]{:S(2)}) collective-permute-start(bf16[2,64,1024]{2,1,0:T(8,128)(2,1)S(1)} %collective-permute-done.refs_0_.after), channel_id=1, source_target_pairs={{0,16},{1,17},{2,18},{3,19},{4,20},{5,21},{6,22},{7,23},{8,24},{9,... | collective-permute-start | bytes 786440 | tf_op jit(solution)/shard_map/ppermute | solution.py:135
  13.9 0.0 collective-permute-done.4.far
  13.9 2.6 %collective-permute-start.7 = (bf16[64,1024]{1,0:T(8,128)(2,1)S(1)}, bf16[64,1024]{1,0:T(8,128)(2,1)S(1)}, u32[]{:S(2)}, u32[]{:S(2)}) collective-permute-start(bf16[64,1024]{1,0:T(8,128)(2,1)S(1)} %get-tuple-element.14), channel_id=1, source_target_pairs={{0,3},{1,2},{2,1},{3,0},{4,7},{5,6},{6,5},{7,4},{8,11},{9,10},{10,... | collective-permute-start | bytes 393224 | tf_op jit(solution)/shard_map/ppermute | solution.py:135
  16.5 0.5 %collective-permute-start.5 = (bf16[64,1024]{1,0:T(8,128)(2,1)S(1)}, bf16[64,1024]{1,0:T(8,128)(2,1)S(1)}, u32[]{:S(2)}, u32[]{:S(2)}) collective-permute-start(bf16[64,1024]{1,0:T(8,128)(2,1)S(1)} %get-tuple-element.14), channel_id=1, source_target_pairs={{0,1},{1,0},{2,3},{3,2},{4,5},{5,4},{6,7},{7,6},{8,9},{9,8},{10,11... | collective-permute-start | bytes 393224 | tf_op jit(solution)/shard_map/ppermute | solution.py:135
  17.0 0.0 collective-permute-done.1.refs_1_
  17.0 0.5 %collective-permute-start.6 = (bf16[64,1024]{1,0:T(8,128)(2,1)S(1)}, bf16[64,1024]{1,0:T(8,128)(2,1)S(1)}, u32[]{:S(2)}, u32[]{:S(2)}) collective-permute-start(bf16[64,1024]{1,0:T(8,128)(2,1)S(1)} %get-tuple-element.13.refs_0_), channel_id=1, source_target_pairs={{0,2},{1,3},{2,0},{3,1},{4,6},{5,7},{6,4},{7,5},{8,10},{9,11},{10,... | collective-permute-start | bytes 393224 | tf_op jit(solution)/shard_map/ppermute | solution.py:135
  17.5 2.3 %collective-permute-done.2.refs_2_ = bf16[2,64,1024]{2,1,0:T(8,128)(2,1)S(1)} collective-permute-done((bf16[2,64,1024]{2,1,0:T(8,128)(2,1)S(1)}, bf16[2,64,1024]{2,1,0:T(8,128)(2,1)S(1)}, u32[]{:S(2)}, u32[]{:S(2)}) %collective-permute-start.2) | collective-permute-done | bytes 262176 | tf_op jit(solution)/shard_map/ppermute | solution.py:135
  19.7 0.1 shard_map.18.mine
  19.8 0.1 collective-permute-start.3
  20.0 2.1 %collective-permute-start.11 = (bf16[64,1024]{1,0:T(8,128)(2,1)S(1)}, bf16[64,1024]{1,0:T(8,128)(2,1)S(1)}, u32[]{:S(2)}, u32[]{:S(2)}) collective-permute-start(bf16[64,1024]{1,0:T(8,128)(2,1)S(1)} %get-tuple-element.16), channel_id=1, source_target_pairs={{0,3},{1,2},{2,1},{3,0},{4,7},{5,6},{6,5},{7,4},{8,11},{9,10},{10,... | collective-permute-start | bytes 393224 | tf_op jit(solution)/shard_map/ppermute | solution.py:135
  22.1 1.0 %collective-permute-done.6.refs_2_ = bf16[64,1024]{1,0:T(8,128)(2,1)S(1)} collective-permute-done((bf16[64,1024]{1,0:T(8,128)(2,1)S(1)}, bf16[64,1024]{1,0:T(8,128)(2,1)S(1)}, u32[]{:S(2)}, u32[]{:S(2)}) %collective-permute-start.6) | collective-permute-done | bytes 131104 | tf_op jit(solution)/shard_map/ppermute | solution.py:135
  23.1 0.5 %collective-permute-start.9 = (bf16[64,1024]{1,0:T(8,128)(2,1)S(1)}, bf16[64,1024]{1,0:T(8,128)(2,1)S(1)}, u32[]{:S(2)}, u32[]{:S(2)}) collective-permute-start(bf16[64,1024]{1,0:T(8,128)(2,1)S(1)} %get-tuple-element.16), channel_id=1, source_target_pairs={{0,1},{1,0},{2,3},{3,2},{4,5},{5,4},{6,7},{7,6},{8,9},{9,8},{10,11... | collective-permute-start | bytes 393224 | tf_op jit(solution)/shard_map/ppermute | solution.py:135
  23.6 0.9 %collective-permute-start.10 = (bf16[64,1024]{1,0:T(8,128)(2,1)S(1)}, bf16[64,1024]{1,0:T(8,128)(2,1)S(1)}, u32[]{:S(2)}, u32[]{:S(2)}) collective-permute-start(bf16[64,1024]{1,0:T(8,128)(2,1)S(1)} %get-tuple-element.15.refs_0_), channel_id=1, source_target_pairs={{0,2},{1,3},{2,0},{3,1},{4,6},{5,7},{6,4},{7,5},{8,10},{9,11},{10,... | collective-permute-start | bytes 393224 | tf_op jit(solution)/shard_map/ppermute | solution.py:135
  24.5 0.0 collective-permute-done.5.refs_1_
  24.5 0.7 %shard_map.20.so_far = f32[2,256,512]{2,1,0:T(8,128)S(1)} custom-call(bf16[2,256,1024]{2,1,0:T(8,128)(2,1)S(1)} %shard_map.18.mine, bf16[2,256,1024]{2,1,0:T(8,128)(2,1)S(1)} %collective-permute-done.3.other, bf16[64,1024]{1,0:T(8,128)(2,1)S(1)} %get-tuple-element.13.refs_0_, bf16[64,1024]{1,0:T(8,128)(2,1)S(1)} %collective-permute-done.5.refs_1_, ...), custom_call_target="tpu_custom_call" | custom-call | flops 10000000000 | bytes 262144 | tf_op jit(solution)/shard_map/pallas_call | solution.py:143
  25.2 4.0 %collective-permute-done.10.refs_2_ = bf16[64,1024]{1,0:T(8,128)(2,1)S(1)} collective-permute-done((bf16[64,1024]{1,0:T(8,128)(2,1)S(1)}, bf16[64,1024]{1,0:T(8,128)(2,1)S(1)}, u32[]{:S(2)}, u32[]{:S(2)}) %collective-permute-start.10) | collective-permute-done | bytes 131104 | tf_op jit(solution)/shard_map/ppermute | solution.py:135
  29.2 0.4 %collective-permute-done.9.refs_1_ = bf16[64,1024]{1,0:T(8,128)(2,1)S(1)} collective-permute-done((bf16[64,1024]{1,0:T(8,128)(2,1)S(1)}, bf16[64,1024]{1,0:T(8,128)(2,1)S(1)}, u32[]{:S(2)}, u32[]{:S(2)}) %collective-permute-start.9) | collective-permute-done | bytes 131104 | tf_op jit(solution)/shard_map/ppermute | solution.py:135
  29.6 1.6 %shard_map.23 = f32[2,256,512]{2,1,0:T(8,128)} custom-call(bf16[2,256,1024]{2,1,0:T(8,128)(2,1)S(1)} %shard_map.18.mine, bf16[2,256,1024]{2,1,0:T(8,128)(2,1)S(1)} %collective-permute-done.3.other, f32[2,256,512]{2,1,0:T(8,128)S(1)} %shard_map.20.so_far, bf16[64,1024]{1,0:T(8,128)(2,1)S(1)} %get-tuple-element.15.refs_0_, ...), custom_call_target="tpu_custom_call" | custom-call | tf_op jit(solution)/shard_map/pallas_call | solution.py:143
  (9 shorter events, 0.1 us)
Async XLA Ops:
  0.0 6.6 %copy-start = (bf16[2,64,1024]{2,1,0:T(8,128)(2,1)S(1)}, bf16[2,64,1024]{2,1,0:T(8,128)(2,1)}, u32[]{:S(2)}) copy-start(bf16[2,64,1024]{2,1,0:T(8,128)(2,1)} %fields.1) | copy-start | bytes 786436
  0.0 9.6 %collective-permute-start = (bf16[2,64,1024]{2,1,0:T(8,128)(2,1)}, bf16[2,64,1024]{2,1,0:T(8,128)(2,1)S(1)}, u32[]{:S(2)}, u32[]{:S(2)}) collective-permute-start(bf16[2,64,1024]{2,1,0:T(8,128)(2,1)} %fields.1), channel_id=1, source_target_pairs={{0,1},{1,0},{2,3},{3,2},{4,5},{5,4},{6,7},{7,6},{8,9},{9,8},{10,11... | collective-permute-start | bytes 786440 | tf_op jit(solution)/shard_map/ppermute | solution.py:135
  4.0 9.9 %collective-permute-start.4 = (bf16[64,1024]{1,0:T(8,128)(2,1)S(1)}, bf16[64,1024]{1,0:T(8,128)(2,1)S(1)}, u32[]{:S(2)}, u32[]{:S(2)}) collective-permute-start(bf16[64,1024]{1,0:T(8,128)(2,1)S(1)} %get-tuple-element.11.own_real.own), channel_id=1, source_target_pairs={{0,4},{1,5},{2,6},{3,7},{4,0},{5,1},{6,2},{7,3},{8,12},{9,13},{10,... | collective-permute-start | bytes 393224 | tf_op jit(solution)/shard_map/ppermute | solution.py:135
  6.6 10.4 %collective-permute-start.1 = (bf16[2,64,1024]{2,1,0:T(8,128)(2,1)S(1)}, bf16[2,64,1024]{2,1,0:T(8,128)(2,1)S(1)}, u32[]{:S(2)}, u32[]{:S(2)}) collective-permute-start(bf16[2,64,1024]{2,1,0:T(8,128)(2,1)S(1)} %copy-done), channel_id=1, source_target_pairs={{0,16},{1,17},{2,18},{3,19},{4,20},{5,21},{6,22},{7,23},{8,24},{9,... | collective-permute-start | bytes 786440 | tf_op jit(solution)/shard_map/ppermute | solution.py:135
  9.6 10.3 %collective-permute-start.8 = (bf16[64,1024]{1,0:T(8,128)(2,1)S(1)}, bf16[64,1024]{1,0:T(8,128)(2,1)S(1)}, u32[]{:S(2)}, u32[]{:S(2)}) collective-permute-start(bf16[64,1024]{1,0:T(8,128)(2,1)S(1)} %shard_map.21.own), channel_id=1, source_target_pairs={{0,4},{1,5},{2,6},{3,7},{4,0},{5,1},{6,2},{7,3},{8,12},{9,13},{10,... | collective-permute-start | bytes 393224 | tf_op jit(solution)/shard_map/ppermute | solution.py:135
  12.4 7.4 %collective-permute-start.2 = (bf16[2,64,1024]{2,1,0:T(8,128)(2,1)S(1)}, bf16[2,64,1024]{2,1,0:T(8,128)(2,1)S(1)}, u32[]{:S(2)}, u32[]{:S(2)}) collective-permute-start(bf16[2,64,1024]{2,1,0:T(8,128)(2,1)S(1)} %collective-permute-done.refs_0_.after), channel_id=1, source_target_pairs={{0,16},{1,17},{2,18},{3,19},{4,20},{5,21},{6,22},{7,23},{8,24},{9,... | collective-permute-start | bytes 786440 | tf_op jit(solution)/shard_map/ppermute | solution.py:135
  13.9 9.7 %collective-permute-start.7 = (bf16[64,1024]{1,0:T(8,128)(2,1)S(1)}, bf16[64,1024]{1,0:T(8,128)(2,1)S(1)}, u32[]{:S(2)}, u32[]{:S(2)}) collective-permute-start(bf16[64,1024]{1,0:T(8,128)(2,1)S(1)} %get-tuple-element.14), channel_id=1, source_target_pairs={{0,3},{1,2},{2,1},{3,0},{4,7},{5,6},{6,5},{7,4},{8,11},{9,10},{10,... | collective-permute-start | bytes 393224 | tf_op jit(solution)/shard_map/ppermute | solution.py:135
  16.5 8.0 %collective-permute-start.5 = (bf16[64,1024]{1,0:T(8,128)(2,1)S(1)}, bf16[64,1024]{1,0:T(8,128)(2,1)S(1)}, u32[]{:S(2)}, u32[]{:S(2)}) collective-permute-start(bf16[64,1024]{1,0:T(8,128)(2,1)S(1)} %get-tuple-element.14), channel_id=1, source_target_pairs={{0,1},{1,0},{2,3},{3,2},{4,5},{5,4},{6,7},{7,6},{8,9},{9,8},{10,11... | collective-permute-start | bytes 393224 | tf_op jit(solution)/shard_map/ppermute | solution.py:135
  17.0 6.1 %collective-permute-start.6 = (bf16[64,1024]{1,0:T(8,128)(2,1)S(1)}, bf16[64,1024]{1,0:T(8,128)(2,1)S(1)}, u32[]{:S(2)}, u32[]{:S(2)}) collective-permute-start(bf16[64,1024]{1,0:T(8,128)(2,1)S(1)} %get-tuple-element.13.refs_0_), channel_id=1, source_target_pairs={{0,2},{1,3},{2,0},{3,1},{4,6},{5,7},{6,4},{7,5},{8,10},{9,11},{10,... | collective-permute-start | bytes 393224 | tf_op jit(solution)/shard_map/ppermute | solution.py:135
  19.8 4.7 %collective-permute-start.3 = (bf16[2,256,1024]{2,1,0:T(8,128)(2,1)S(1)}, bf16[2,256,1024]{2,1,0:T(8,128)(2,1)S(1)}, u32[]{:S(2)}, u32[]{:S(2)}) collective-permute-start(bf16[2,256,1024]{2,1,0:T(8,128)(2,1)S(1)} %shard_map.18.mine), channel_id=1, source_target_pairs={{0,8},{1,9},{2,10},{3,11},{4,12},{5,13},{6,14},{7,15},{8,0},{9,1},... | collective-permute-start | bytes 3145736 | tf_op jit(solution)/shard_map/ppermute | solution.py:135
  20.0 9.3 %collective-permute-start.11 = (bf16[64,1024]{1,0:T(8,128)(2,1)S(1)}, bf16[64,1024]{1,0:T(8,128)(2,1)S(1)}, u32[]{:S(2)}, u32[]{:S(2)}) collective-permute-start(bf16[64,1024]{1,0:T(8,128)(2,1)S(1)} %get-tuple-element.16), channel_id=1, source_target_pairs={{0,3},{1,2},{2,1},{3,0},{4,7},{5,6},{6,5},{7,4},{8,11},{9,10},{10,... | collective-permute-start | bytes 393224 | tf_op jit(solution)/shard_map/ppermute | solution.py:135
  23.1 6.5 %collective-permute-start.9 = (bf16[64,1024]{1,0:T(8,128)(2,1)S(1)}, bf16[64,1024]{1,0:T(8,128)(2,1)S(1)}, u32[]{:S(2)}, u32[]{:S(2)}) collective-permute-start(bf16[64,1024]{1,0:T(8,128)(2,1)S(1)} %get-tuple-element.16), channel_id=1, source_target_pairs={{0,1},{1,0},{2,3},{3,2},{4,5},{5,4},{6,7},{7,6},{8,9},{9,8},{10,11... | collective-permute-start | bytes 393224 | tf_op jit(solution)/shard_map/ppermute | solution.py:135
  23.6 5.6 %collective-permute-start.10 = (bf16[64,1024]{1,0:T(8,128)(2,1)S(1)}, bf16[64,1024]{1,0:T(8,128)(2,1)S(1)}, u32[]{:S(2)}, u32[]{:S(2)}) collective-permute-start(bf16[64,1024]{1,0:T(8,128)(2,1)S(1)} %get-tuple-element.15.refs_0_), channel_id=1, source_target_pairs={{0,2},{1,3},{2,0},{3,1},{4,6},{5,7},{6,4},{7,5},{8,10},{9,11},{10,... | collective-permute-start | bytes 393224 | tf_op jit(solution)/shard_map/ppermute | solution.py:135

commit v4 on v3

--- a/solution.py
+++ b/solution.py
@@ -12,7 +12,7 @@
 ANY = pl.BlockSpec(memory_space=pl.ANY)
 VMEM = pl.BlockSpec(memory_space=pltpu.VMEM)
 PARAMS = pltpu.CompilerParams(vmem_limit_bytes=24 * 1024 * 1024)
-EARLY, MIDDLE = 30_000_000_000, 10_000_000_000
+EARLY, MIDDLE, LIGHT = 30_000_000_000, 10_000_000_000, 1_000_000_000
 
 
 def weight(flops):
@@ -36,7 +36,7 @@
         copy.wait()
 
 
-def relay_kernel(part, after, out):
+def relay_kernel(part, out):
     out[...] = part[...]
 
 
@@ -171,10 +171,10 @@
         places = [(shift, turn) for shift in range(half) for turn in range(slabs)]
         slots = []
         for i, part in enumerate(own):
-            if i > 0:
-                part = call(relay_kernel, part_shape, [part, blocks[1]])
             far = exchange(part, 0, half, 0)
-            keep, give = call(functools.partial(choose_kernel, sizes), [part_shape] * 2, [part, far], flops=EARLY)
+            if i == 0:
+                far = call(relay_kernel, part_shape, [far], flops=LIGHT)
+            keep, give = call(functools.partial(choose_kernel, sizes), [part_shape] * 2, [part, far], flops=EARLY if i else LIGHT)
             got = [keep]
             for shift, turn in places[1:]:
                 got.append(exchange(give if turn else keep, 0, shift, turn))

time: 31.4 us -> 31.4 us (level)
  no operation moved by 1% of the time
where the time goes in v4:
time: 31.4 us; the launch traced here: 31.2 us
  starting transfers between devices  18.4 us (59%)
  waiting for transfers between devices  9.27 us (30%)
  Pallas kernels  3.53 us (11%)
    ppermute x12, starting transfers between devices, exchange(): return lax.ppermute(array, AXES, pairs)  18.4 us
    ppermute x12, waiting for transfers between devices, exchange(): return lax.ppermute(array, AXES, pairs)  9.27 us
    pallas_call x7, Pallas kernels, call(): pl.pallas_call(kernel, out_shape=out_shape, in_specs=specs or [VMEM] * le...  3.53 us
  transfers between devices with their start and end apart: 12, of which 5 were waited for; matrix products, arithmetic and copies ran while one was open for 0% of the time, Pallas kernels for 6%

profile of v4, /device:TPU:0, one launch (start us, length us, event | category | flops | bytes accessed | tf_op | source)
XLA Modules:
  0.0 31.2 jit_solution(2760375302775527291)
XLA Ops:
  0.0 3.0 %collective-permute-start = (bf16[2,64,1024]{2,1,0:T(8,128)(2,1)}, bf16[2,64,1024]{2,1,0:T(8,128)(2,1)S(1)}, u32[]{:S(2)}, u32[]{:S(2)}) collective-permute-start(bf16[2,64,1024]{2,1,0:T(8,128)(2,1)} %fields.1), channel_id=1, source_target_pairs={{0,1},{1,0},{2,3},{3,2},{4,5},{5,4},{6,7},{7,6},{8,9},{9,8},{10,11... | collective-permute-start | bytes 786440 | tf_op jit(solution)/shard_map/ppermute | solution.py:135
  3.0 1.0 %shard_map.17 = (bf16[64,1024]{1,0:T(8,128)(2,1)S(1)}, bf16[64,1024]{1,0:T(8,128)(2,1)S(1)}) custom-call(bf16[2,64,1024]{2,1,0:T(8,128)(2,1)} %fields.1), custom_call_target="tpu_custom_call" | custom-call | tf_op jit(solution)/shard_map/pallas_call | solution.py:143
  4.0 2.7 %collective-permute-start.4 = (bf16[64,1024]{1,0:T(8,128)(2,1)S(1)}, bf16[64,1024]{1,0:T(8,128)(2,1)S(1)}, u32[]{:S(2)}, u32[]{:S(2)}) collective-permute-start(bf16[64,1024]{1,0:T(8,128)(2,1)S(1)} %get-tuple-element.11.own_real.own), channel_id=1, source_target_pairs={{0,4},{1,5},{2,6},{3,7},{4,0},{5,1},{6,2},{7,3},{8,12},{9,13},{10,... | collective-permute-start | bytes 393224 | tf_op jit(solution)/shard_map/ppermute | solution.py:135
  6.6 1.5 %collective-permute-start.1 = (bf16[2,64,1024]{2,1,0:T(8,128)(2,1)S(1)}, bf16[2,64,1024]{2,1,0:T(8,128)(2,1)S(1)}, u32[]{:S(2)}, u32[]{:S(2)}) collective-permute-start(bf16[2,64,1024]{2,1,0:T(8,128)(2,1)S(1)} %copy-done), channel_id=1, source_target_pairs={{0,16},{1,17},{2,18},{3,19},{4,20},{5,21},{6,22},{7,23},{8,24},{9,... | collective-permute-start | bytes 786440 | tf_op jit(solution)/shard_map/ppermute | solution.py:135
  8.1 1.4 %collective-permute-done.refs_0_ = bf16[2,64,1024]{2,1,0:T(8,128)(2,1)S(1)} collective-permute-done((bf16[2,64,1024]{2,1,0:T(8,128)(2,1)}, bf16[2,64,1024]{2,1,0:T(8,128)(2,1)S(1)}, u32[]{:S(2)}, u32[]{:S(2)}) %collective-permute-start) | collective-permute-done | bytes 262176 | tf_op jit(solution)/shard_map/ppermute | solution.py:135
  9.6 1.6 %collective-permute-start.2 = (bf16[2,64,1024]{2,1,0:T(8,128)(2,1)S(1)}, bf16[2,64,1024]{2,1,0:T(8,128)(2,1)S(1)}, u32[]{:S(2)}, u32[]{:S(2)}) collective-permute-start(bf16[2,64,1024]{2,1,0:T(8,128)(2,1)S(1)} %collective-permute-done.refs_0_), channel_id=1, source_target_pairs={{0,16},{1,17},{2,18},{3,19},{4,20},{5,21},{6,22},{7,23},{8,24},{9,... | collective-permute-start | bytes 786440 | tf_op jit(solution)/shard_map/ppermute | solution.py:135
  11.2 2.6 %collective-permute-start.8 = (bf16[64,1024]{1,0:T(8,128)(2,1)S(1)}, bf16[64,1024]{1,0:T(8,128)(2,1)S(1)}, u32[]{:S(2)}, u32[]{:S(2)}) collective-permute-start(bf16[64,1024]{1,0:T(8,128)(2,1)S(1)} %get-tuple-element.12.own_imag.own), channel_id=1, source_target_pairs={{0,4},{1,5},{2,6},{3,7},{4,0},{5,1},{6,2},{7,3},{8,12},{9,13},{10,... | collective-permute-start | bytes 393224 | tf_op jit(solution)/shard_map/ppermute | solution.py:135
  13.8 0.0 collective-permute-done.4.part
  13.8 2.6 %collective-permute-start.7 = (bf16[64,1024]{1,0:T(8,128)(2,1)S(1)}, bf16[64,1024]{1,0:T(8,128)(2,1)S(1)}, u32[]{:S(2)}, u32[]{:S(2)}) collective-permute-start(bf16[64,1024]{1,0:T(8,128)(2,1)S(1)} %get-tuple-element.14), channel_id=1, source_target_pairs={{0,3},{1,2},{2,1},{3,0},{4,7},{5,6},{6,5},{7,4},{8,11},{9,10},{10,... | collective-permute-start | bytes 393224 | tf_op jit(solution)/shard_map/ppermute | solution.py:135
  16.4 0.5 %collective-permute-start.5 = (bf16[64,1024]{1,0:T(8,128)(2,1)S(1)}, bf16[64,1024]{1,0:T(8,128)(2,1)S(1)}, u32[]{:S(2)}, u32[]{:S(2)}) collective-permute-start(bf16[64,1024]{1,0:T(8,128)(2,1)S(1)} %get-tuple-element.14), channel_id=1, source_target_pairs={{0,1},{1,0},{2,3},{3,2},{4,5},{5,4},{6,7},{7,6},{8,9},{9,8},{10,11... | collective-permute-start | bytes 393224 | tf_op jit(solution)/shard_map/ppermute | solution.py:135
  17.0 0.0 collective-permute-done.1.refs_1_
  17.0 0.5 %collective-permute-start.6 = (bf16[64,1024]{1,0:T(8,128)(2,1)S(1)}, bf16[64,1024]{1,0:T(8,128)(2,1)S(1)}, u32[]{:S(2)}, u32[]{:S(2)}) collective-permute-start(bf16[64,1024]{1,0:T(8,128)(2,1)S(1)} %get-tuple-element.13.refs_0_), channel_id=1, source_target_pairs={{0,2},{1,3},{2,0},{3,1},{4,6},{5,7},{6,4},{7,5},{8,10},{9,11},{10,... | collective-permute-start | bytes 393224 | tf_op jit(solution)/shard_map/ppermute | solution.py:135
  17.5 2.3 %collective-permute-done.2.refs_2_ = bf16[2,64,1024]{2,1,0:T(8,128)(2,1)S(1)} collective-permute-done((bf16[2,64,1024]{2,1,0:T(8,128)(2,1)S(1)}, bf16[2,64,1024]{2,1,0:T(8,128)(2,1)S(1)}, u32[]{:S(2)}, u32[]{:S(2)}) %collective-permute-start.2) | collective-permute-done | bytes 262176 | tf_op jit(solution)/shard_map/ppermute | solution.py:135
  19.7 0.1 shard_map.18.mine
  19.8 0.1 collective-permute-start.3
  20.0 1.6 %collective-permute-start.11 = (bf16[64,1024]{1,0:T(8,128)(2,1)S(1)}, bf16[64,1024]{1,0:T(8,128)(2,1)S(1)}, u32[]{:S(2)}, u32[]{:S(2)}) collective-permute-start(bf16[64,1024]{1,0:T(8,128)(2,1)S(1)} %get-tuple-element.16), channel_id=1, source_target_pairs={{0,3},{1,2},{2,1},{3,0},{4,7},{5,6},{6,5},{7,4},{8,11},{9,10},{10,... | collective-permute-start | bytes 393224 | tf_op jit(solution)/shard_map/ppermute | solution.py:135
  21.5 1.7 %collective-permute-done.6.refs_2_ = bf16[64,1024]{1,0:T(8,128)(2,1)S(1)} collective-permute-done((bf16[64,1024]{1,0:T(8,128)(2,1)S(1)}, bf16[64,1024]{1,0:T(8,128)(2,1)S(1)}, u32[]{:S(2)}, u32[]{:S(2)}) %collective-permute-start.6) | collective-permute-done | bytes 131104 | tf_op jit(solution)/shard_map/ppermute | solution.py:135
  23.2 0.5 %collective-permute-start.9 = (bf16[64,1024]{1,0:T(8,128)(2,1)S(1)}, bf16[64,1024]{1,0:T(8,128)(2,1)S(1)}, u32[]{:S(2)}, u32[]{:S(2)}) collective-permute-start(bf16[64,1024]{1,0:T(8,128)(2,1)S(1)} %get-tuple-element.16), channel_id=1, source_target_pairs={{0,1},{1,0},{2,3},{3,2},{4,5},{5,4},{6,7},{7,6},{8,9},{9,8},{10,11... | collective-permute-start | bytes 393224 | tf_op jit(solution)/shard_map/ppermute | solution.py:135
  23.7 0.0 collective-permute-done.7.refs_3_
  23.7 1.3 %collective-permute-start.10 = (bf16[64,1024]{1,0:T(8,128)(2,1)S(1)}, bf16[64,1024]{1,0:T(8,128)(2,1)S(1)}, u32[]{:S(2)}, u32[]{:S(2)}) collective-permute-start(bf16[64,1024]{1,0:T(8,128)(2,1)S(1)} %get-tuple-element.15.refs_0_), channel_id=1, source_target_pairs={{0,2},{1,3},{2,0},{3,1},{4,6},{5,7},{6,4},{7,5},{8,10},{9,11},{10,... | collective-permute-start | bytes 393224 | tf_op jit(solution)/shard_map/ppermute | solution.py:135
  25.0 0.7 %shard_map.21.so_far = f32[2,256,512]{2,1,0:T(8,128)S(1)} custom-call(bf16[2,256,1024]{2,1,0:T(8,128)(2,1)S(1)} %shard_map.18.mine, bf16[2,256,1024]{2,1,0:T(8,128)(2,1)S(1)} %collective-permute-done.3.other, bf16[64,1024]{1,0:T(8,128)(2,1)S(1)} %get-tuple-element.13.refs_0_, bf16[64,1024]{1,0:T(8,128)(2,1)S(1)} %collective-permute-done.5.refs_1_, ...), custom_call_target="tpu_custom_call" | custom-call | flops 10000000000 | bytes 262144 | tf_op jit(solution)/shard_map/pallas_call | solution.py:143
  25.8 3.0 %collective-permute-done.10.refs_2_ = bf16[64,1024]{1,0:T(8,128)(2,1)S(1)} collective-permute-done((bf16[64,1024]{1,0:T(8,128)(2,1)S(1)}, bf16[64,1024]{1,0:T(8,128)(2,1)S(1)}, u32[]{:S(2)}, u32[]{:S(2)}) %collective-permute-start.10) | collective-permute-done | bytes 131104 | tf_op jit(solution)/shard_map/ppermute | solution.py:135
  28.8 0.8 %collective-permute-done.9.refs_1_ = bf16[64,1024]{1,0:T(8,128)(2,1)S(1)} collective-permute-done((bf16[64,1024]{1,0:T(8,128)(2,1)S(1)}, bf16[64,1024]{1,0:T(8,128)(2,1)S(1)}, u32[]{:S(2)}, u32[]{:S(2)}) %collective-permute-start.9) | collective-permute-done | bytes 131104 | tf_op jit(solution)/shard_map/ppermute | solution.py:135
  29.6 1.6 %shard_map.23 = f32[2,256,512]{2,1,0:T(8,128)} custom-call(bf16[2,256,1024]{2,1,0:T(8,128)(2,1)S(1)} %shard_map.18.mine, bf16[2,256,1024]{2,1,0:T(8,128)(2,1)S(1)} %collective-permute-done.3.other, f32[2,256,512]{2,1,0:T(8,128)S(1)} %shard_map.21.so_far, bf16[64,1024]{1,0:T(8,128)(2,1)S(1)} %get-tuple-element.15.refs_0_, ...), custom_call_target="tpu_custom_call" | custom-call | tf_op jit(solution)/shard_map/pallas_call | solution.py:143
  (9 shorter events, 0.1 us)
Async XLA Ops:
  0.0 6.6 %copy-start = (bf16[2,64,1024]{2,1,0:T(8,128)(2,1)S(1)}, bf16[2,64,1024]{2,1,0:T(8,128)(2,1)}, u32[]{:S(2)}) copy-start(bf16[2,64,1024]{2,1,0:T(8,128)(2,1)} %fields.1) | copy-start | bytes 786436
  0.0 9.6 %collective-permute-start = (bf16[2,64,1024]{2,1,0:T(8,128)(2,1)}, bf16[2,64,1024]{2,1,0:T(8,128)(2,1)S(1)}, u32[]{:S(2)}, u32[]{:S(2)}) collective-permute-start(bf16[2,64,1024]{2,1,0:T(8,128)(2,1)} %fields.1), channel_id=1, source_target_pairs={{0,1},{1,0},{2,3},{3,2},{4,5},{5,4},{6,7},{7,6},{8,9},{9,8},{10,11... | collective-permute-start | bytes 786440 | tf_op jit(solution)/shard_map/ppermute | solution.py:135
  4.0 9.8 %collective-permute-start.4 = (bf16[64,1024]{1,0:T(8,128)(2,1)S(1)}, bf16[64,1024]{1,0:T(8,128)(2,1)S(1)}, u32[]{:S(2)}, u32[]{:S(2)}) collective-permute-start(bf16[64,1024]{1,0:T(8,128)(2,1)S(1)} %get-tuple-element.11.own_real.own), channel_id=1, source_target_pairs={{0,4},{1,5},{2,6},{3,7},{4,0},{5,1},{6,2},{7,3},{8,12},{9,13},{10,... | collective-permute-start | bytes 393224 | tf_op jit(solution)/shard_map/ppermute | solution.py:135
  6.6 10.3 %collective-permute-start.1 = (bf16[2,64,1024]{2,1,0:T(8,128)(2,1)S(1)}, bf16[2,64,1024]{2,1,0:T(8,128)(2,1)S(1)}, u32[]{:S(2)}, u32[]{:S(2)}) collective-permute-start(bf16[2,64,1024]{2,1,0:T(8,128)(2,1)S(1)} %copy-done), channel_id=1, source_target_pairs={{0,16},{1,17},{2,18},{3,19},{4,20},{5,21},{6,22},{7,23},{8,24},{9,... | collective-permute-start | bytes 786440 | tf_op jit(solution)/shard_map/ppermute | solution.py:135
  9.6 10.2 %collective-permute-start.2 = (bf16[2,64,1024]{2,1,0:T(8,128)(2,1)S(1)}, bf16[2,64,1024]{2,1,0:T(8,128)(2,1)S(1)}, u32[]{:S(2)}, u32[]{:S(2)}) collective-permute-start(bf16[2,64,1024]{2,1,0:T(8,128)(2,1)S(1)} %collective-permute-done.refs_0_), channel_id=1, source_target_pairs={{0,16},{1,17},{2,18},{3,19},{4,20},{5,21},{6,22},{7,23},{8,24},{9,... | collective-permute-start | bytes 786440 | tf_op jit(solution)/shard_map/ppermute | solution.py:135
  11.2 8.7 %collective-permute-start.8 = (bf16[64,1024]{1,0:T(8,128)(2,1)S(1)}, bf16[64,1024]{1,0:T(8,128)(2,1)S(1)}, u32[]{:S(2)}, u32[]{:S(2)}) collective-permute-start(bf16[64,1024]{1,0:T(8,128)(2,1)S(1)} %get-tuple-element.12.own_imag.own), channel_id=1, source_target_pairs={{0,4},{1,5},{2,6},{3,7},{4,0},{5,1},{6,2},{7,3},{8,12},{9,13},{10,... | collective-permute-start | bytes 393224 | tf_op jit(solution)/shard_map/ppermute | solution.py:135
  13.8 9.9 %collective-permute-start.7 = (bf16[64,1024]{1,0:T(8,128)(2,1)S(1)}, bf16[64,1024]{1,0:T(8,128)(2,1)S(1)}, u32[]{:S(2)}, u32[]{:S(2)}) collective-permute-start(bf16[64,1024]{1,0:T(8,128)(2,1)S(1)} %get-tuple-element.14), channel_id=1, source_target_pairs={{0,3},{1,2},{2,1},{3,0},{4,7},{5,6},{6,5},{7,4},{8,11},{9,10},{10,... | collective-permute-start | bytes 393224 | tf_op jit(solution)/shard_map/ppermute | solution.py:135
  16.4 8.6 %collective-permute-start.5 = (bf16[64,1024]{1,0:T(8,128)(2,1)S(1)}, bf16[64,1024]{1,0:T(8,128)(2,1)S(1)}, u32[]{:S(2)}, u32[]{:S(2)}) collective-permute-start(bf16[64,1024]{1,0:T(8,128)(2,1)S(1)} %get-tuple-element.14), channel_id=1, source_target_pairs={{0,1},{1,0},{2,3},{3,2},{4,5},{5,4},{6,7},{7,6},{8,9},{9,8},{10,11... | collective-permute-start | bytes 393224 | tf_op jit(solution)/shard_map/ppermute | solution.py:135
  17.0 6.3 %collective-permute-start.6 = (bf16[64,1024]{1,0:T(8,128)(2,1)S(1)}, bf16[64,1024]{1,0:T(8,128)(2,1)S(1)}, u32[]{:S(2)}, u32[]{:S(2)}) collective-permute-start(bf16[64,1024]{1,0:T(8,128)(2,1)S(1)} %get-tuple-element.13.refs_0_), channel_id=1, source_target_pairs={{0,2},{1,3},{2,0},{3,1},{4,6},{5,7},{6,4},{7,5},{8,10},{9,11},{10,... | collective-permute-start | bytes 393224 | tf_op jit(solution)/shard_map/ppermute | solution.py:135
  19.8 5.2 %collective-permute-start.3 = (bf16[2,256,1024]{2,1,0:T(8,128)(2,1)S(1)}, bf16[2,256,1024]{2,1,0:T(8,128)(2,1)S(1)}, u32[]{:S(2)}, u32[]{:S(2)}) collective-permute-start(bf16[2,256,1024]{2,1,0:T(8,128)(2,1)S(1)} %shard_map.18.mine), channel_id=1, source_target_pairs={{0,8},{1,9},{2,10},{3,11},{4,12},{5,13},{6,14},{7,15},{8,0},{9,1},... | collective-permute-start | bytes 3145736 | tf_op jit(solution)/shard_map/ppermute | solution.py:135
  20.0 8.8 %collective-permute-start.11 = (bf16[64,1024]{1,0:T(8,128)(2,1)S(1)}, bf16[64,1024]{1,0:T(8,128)(2,1)S(1)}, u32[]{:S(2)}, u32[]{:S(2)}) collective-permute-start(bf16[64,1024]{1,0:T(8,128)(2,1)S(1)} %get-tuple-element.16), channel_id=1, source_target_pairs={{0,3},{1,2},{2,1},{3,0},{4,7},{5,6},{6,5},{7,4},{8,11},{9,10},{10,... | collective-permute-start | bytes 393224 | tf_op jit(solution)/shard_map/ppermute | solution.py:135
  23.2 6.4 %collective-permute-start.9 = (bf16[64,1024]{1,0:T(8,128)(2,1)S(1)}, bf16[64,1024]{1,0:T(8,128)(2,1)S(1)}, u32[]{:S(2)}, u32[]{:S(2)}) collective-permute-start(bf16[64,1024]{1,0:T(8,128)(2,1)S(1)} %get-tuple-element.16), channel_id=1, source_target_pairs={{0,1},{1,0},{2,3},{3,2},{4,5},{5,4},{6,7},{7,6},{8,9},{9,8},{10,11... | collective-permute-start | bytes 393224 | tf_op jit(solution)/shard_map/ppermute | solution.py:135
  23.7 5.1 %collective-permute-start.10 = (bf16[64,1024]{1,0:T(8,128)(2,1)S(1)}, bf16[64,1024]{1,0:T(8,128)(2,1)S(1)}, u32[]{:S(2)}, u32[]{:S(2)}) collective-permute-start(bf16[64,1024]{1,0:T(8,128)(2,1)S(1)} %get-tuple-element.15.refs_0_), channel_id=1, source_target_pairs={{0,2},{1,3},{2,0},{3,1},{4,6},{5,7},{6,4},{7,5},{8,10},{9,11},{10,... | collective-permute-start | bytes 393224 | tf_op jit(solution)/shard_map/ppermute | solution.py:135

commit v5 on v4

--- a/solution.py
+++ b/solution.py
@@ -74,14 +74,18 @@
     core = lax.rem(lax.axis_index("row"), 2)
     for cols, which in ((mine, core), (other, 1 - core)):
 
-        @pl.loop(0, mine.shape[1] // TILE)
-        def _(tile):
-            here = pl.ds(pl.multiple_of(tile * TILE, TILE), TILE)
+        def one_tile(tile, cols=cols, which=which):
+            here = pl.ds(tile * TILE if isinstance(tile, int) else pl.multiple_of(tile * TILE, TILE), TILE)
             parts = []
             for i in range(TILE // group):
                 at = (2 * (tile * (TILE // group) + i) + which) * group
                 parts.append((slice(i * group, (i + 1) * group), pl.multiple_of(at, group)))
             step(cols[0, here], cols[1, here], parts)
+
+        if mine.shape[1] == TILE:
+            one_tile(0)
+        else:
+            pl.loop(0, mine.shape[1] // TILE)(one_tile)
 
 
 def real_rows_kernel(sizes, places, mine, other, *refs):

time: 31.4 us -> 31.4 us (level)
  no operation moved by 1% of the time
where the time goes in v5:
time: 31.4 us; the launch traced here: 31.2 us
  starting transfers between devices  18.4 us (59%)
  waiting for transfers between devices  9.27 us (30%)
  Pallas kernels  3.53 us (11%)
    ppermute x12, starting transfers between devices, exchange(): return lax.ppermute(array, AXES, pairs)  18.4 us
    ppermute x12, waiting for transfers between devices, exchange(): return lax.ppermute(array, AXES, pairs)  9.27 us
    pallas_call x7, Pallas kernels, call(): pl.pallas_call(kernel, out_shape=out_shape, in_specs=specs or [VMEM] * le...  3.53 us
  transfers between devices with their start and end apart: 12, of which 5 were waited for; matrix products, arithmetic and copies ran while one was open for 0% of the time, Pallas kernels for 6%

profile of v5, /device:TPU:0, one launch (start us, length us, event | category | flops | bytes accessed | tf_op | source)
XLA Modules:
  0.0 31.2 jit_solution(2760375302775527291)
XLA Ops:
  0.0 3.0 %collective-permute-start = (bf16[2,64,1024]{2,1,0:T(8,128)(2,1)}, bf16[2,64,1024]{2,1,0:T(8,128)(2,1)S(1)}, u32[]{:S(2)}, u32[]{:S(2)}) collective-permute-start(bf16[2,64,1024]{2,1,0:T(8,128)(2,1)} %fields.1), channel_id=1, source_target_pairs={{0,1},{1,0},{2,3},{3,2},{4,5},{5,4},{6,7},{7,6},{8,9},{9,8},{10,11... | collective-permute-start | bytes 786440 | tf_op jit(solution)/shard_map/ppermute | solution.py:139
  3.0 1.0 %shard_map.17 = (bf16[64,1024]{1,0:T(8,128)(2,1)S(1)}, bf16[64,1024]{1,0:T(8,128)(2,1)S(1)}) custom-call(bf16[2,64,1024]{2,1,0:T(8,128)(2,1)} %fields.1), custom_call_target="tpu_custom_call" | custom-call | tf_op jit(solution)/shard_map/pallas_call | solution.py:147
  4.0 2.7 %collective-permute-start.4 = (bf16[64,1024]{1,0:T(8,128)(2,1)S(1)}, bf16[64,1024]{1,0:T(8,128)(2,1)S(1)}, u32[]{:S(2)}, u32[]{:S(2)}) collective-permute-start(bf16[64,1024]{1,0:T(8,128)(2,1)S(1)} %get-tuple-element.11.own_real.own), channel_id=1, source_target_pairs={{0,4},{1,5},{2,6},{3,7},{4,0},{5,1},{6,2},{7,3},{8,12},{9,13},{10,... | collective-permute-start | bytes 393224 | tf_op jit(solution)/shard_map/ppermute | solution.py:139
  6.6 1.5 %collective-permute-start.1 = (bf16[2,64,1024]{2,1,0:T(8,128)(2,1)S(1)}, bf16[2,64,1024]{2,1,0:T(8,128)(2,1)S(1)}, u32[]{:S(2)}, u32[]{:S(2)}) collective-permute-start(bf16[2,64,1024]{2,1,0:T(8,128)(2,1)S(1)} %copy-done), channel_id=1, source_target_pairs={{0,16},{1,17},{2,18},{3,19},{4,20},{5,21},{6,22},{7,23},{8,24},{9,... | collective-permute-start | bytes 786440 | tf_op jit(solution)/shard_map/ppermute | solution.py:139
  8.1 1.4 %collective-permute-done.refs_0_ = bf16[2,64,1024]{2,1,0:T(8,128)(2,1)S(1)} collective-permute-done((bf16[2,64,1024]{2,1,0:T(8,128)(2,1)}, bf16[2,64,1024]{2,1,0:T(8,128)(2,1)S(1)}, u32[]{:S(2)}, u32[]{:S(2)}) %collective-permute-start) | collective-permute-done | bytes 262176 | tf_op jit(solution)/shard_map/ppermute | solution.py:139
  9.6 1.6 %collective-permute-start.2 = (bf16[2,64,1024]{2,1,0:T(8,128)(2,1)S(1)}, bf16[2,64,1024]{2,1,0:T(8,128)(2,1)S(1)}, u32[]{:S(2)}, u32[]{:S(2)}) collective-permute-start(bf16[2,64,1024]{2,1,0:T(8,128)(2,1)S(1)} %collective-permute-done.refs_0_), channel_id=1, source_target_pairs={{0,16},{1,17},{2,18},{3,19},{4,20},{5,21},{6,22},{7,23},{8,24},{9,... | collective-permute-start | bytes 786440 | tf_op jit(solution)/shard_map/ppermute | solution.py:139
  11.2 2.6 %collective-permute-start.8 = (bf16[64,1024]{1,0:T(8,128)(2,1)S(1)}, bf16[64,1024]{1,0:T(8,128)(2,1)S(1)}, u32[]{:S(2)}, u32[]{:S(2)}) collective-permute-start(bf16[64,1024]{1,0:T(8,128)(2,1)S(1)} %get-tuple-element.12.own_imag.own), channel_id=1, source_target_pairs={{0,4},{1,5},{2,6},{3,7},{4,0},{5,1},{6,2},{7,3},{8,12},{9,13},{10,... | collective-permute-start | bytes 393224 | tf_op jit(solution)/shard_map/ppermute | solution.py:139
  13.8 0.0 collective-permute-done.4.part
  13.8 2.6 %collective-permute-start.7 = (bf16[64,1024]{1,0:T(8,128)(2,1)S(1)}, bf16[64,1024]{1,0:T(8,128)(2,1)S(1)}, u32[]{:S(2)}, u32[]{:S(2)}) collective-permute-start(bf16[64,1024]{1,0:T(8,128)(2,1)S(1)} %get-tuple-element.14), channel_id=1, source_target_pairs={{0,3},{1,2},{2,1},{3,0},{4,7},{5,6},{6,5},{7,4},{8,11},{9,10},{10,... | collective-permute-start | bytes 393224 | tf_op jit(solution)/shard_map/ppermute | solution.py:139
  16.4 0.5 %collective-permute-start.5 = (bf16[64,1024]{1,0:T(8,128)(2,1)S(1)}, bf16[64,1024]{1,0:T(8,128)(2,1)S(1)}, u32[]{:S(2)}, u32[]{:S(2)}) collective-permute-start(bf16[64,1024]{1,0:T(8,128)(2,1)S(1)} %get-tuple-element.14), channel_id=1, source_target_pairs={{0,1},{1,0},{2,3},{3,2},{4,5},{5,4},{6,7},{7,6},{8,9},{9,8},{10,11... | collective-permute-start | bytes 393224 | tf_op jit(solution)/shard_map/ppermute | solution.py:139
  17.0 0.0 collective-permute-done.1.refs_1_
  17.0 0.5 %collective-permute-start.6 = (bf16[64,1024]{1,0:T(8,128)(2,1)S(1)}, bf16[64,1024]{1,0:T(8,128)(2,1)S(1)}, u32[]{:S(2)}, u32[]{:S(2)}) collective-permute-start(bf16[64,1024]{1,0:T(8,128)(2,1)S(1)} %get-tuple-element.13.refs_0_), channel_id=1, source_target_pairs={{0,2},{1,3},{2,0},{3,1},{4,6},{5,7},{6,4},{7,5},{8,10},{9,11},{10,... | collective-permute-start | bytes 393224 | tf_op jit(solution)/shard_map/ppermute | solution.py:139
  17.5 2.3 %collective-permute-done.2.refs_2_ = bf16[2,64,1024]{2,1,0:T(8,128)(2,1)S(1)} collective-permute-done((bf16[2,64,1024]{2,1,0:T(8,128)(2,1)S(1)}, bf16[2,64,1024]{2,1,0:T(8,128)(2,1)S(1)}, u32[]{:S(2)}, u32[]{:S(2)}) %collective-permute-start.2) | collective-permute-done | bytes 262176 | tf_op jit(solution)/shard_map/ppermute | solution.py:139
  19.7 0.1 shard_map.18.mine
  19.8 0.1 collective-permute-start.3
  20.0 1.6 %collective-permute-start.11 = (bf16[64,1024]{1,0:T(8,128)(2,1)S(1)}, bf16[64,1024]{1,0:T(8,128)(2,1)S(1)}, u32[]{:S(2)}, u32[]{:S(2)}) collective-permute-start(bf16[64,1024]{1,0:T(8,128)(2,1)S(1)} %get-tuple-element.16), channel_id=1, source_target_pairs={{0,3},{1,2},{2,1},{3,0},{4,7},{5,6},{6,5},{7,4},{8,11},{9,10},{10,... | collective-permute-start | bytes 393224 | tf_op jit(solution)/shard_map/ppermute | solution.py:139
  21.5 1.7 %collective-permute-done.6.refs_2_ = bf16[64,1024]{1,0:T(8,128)(2,1)S(1)} collective-permute-done((bf16[64,1024]{1,0:T(8,128)(2,1)S(1)}, bf16[64,1024]{1,0:T(8,128)(2,1)S(1)}, u32[]{:S(2)}, u32[]{:S(2)}) %collective-permute-start.6) | collective-permute-done | bytes 131104 | tf_op jit(solution)/shard_map/ppermute | solution.py:139
  23.2 0.5 %collective-permute-start.9 = (bf16[64,1024]{1,0:T(8,128)(2,1)S(1)}, bf16[64,1024]{1,0:T(8,128)(2,1)S(1)}, u32[]{:S(2)}, u32[]{:S(2)}) collective-permute-start(bf16[64,1024]{1,0:T(8,128)(2,1)S(1)} %get-tuple-element.16), channel_id=1, source_target_pairs={{0,1},{1,0},{2,3},{3,2},{4,5},{5,4},{6,7},{7,6},{8,9},{9,8},{10,11... | collective-permute-start | bytes 393224 | tf_op jit(solution)/shard_map/ppermute | solution.py:139
  23.7 0.0 collective-permute-done.7.refs_3_
  23.7 1.3 %collective-permute-start.10 = (bf16[64,1024]{1,0:T(8,128)(2,1)S(1)}, bf16[64,1024]{1,0:T(8,128)(2,1)S(1)}, u32[]{:S(2)}, u32[]{:S(2)}) collective-permute-start(bf16[64,1024]{1,0:T(8,128)(2,1)S(1)} %get-tuple-element.15.refs_0_), channel_id=1, source_target_pairs={{0,2},{1,3},{2,0},{3,1},{4,6},{5,7},{6,4},{7,5},{8,10},{9,11},{10,... | collective-permute-start | bytes 393224 | tf_op jit(solution)/shard_map/ppermute | solution.py:139
  25.0 0.7 %shard_map.21.so_far = f32[2,256,512]{2,1,0:T(8,128)S(1)} custom-call(bf16[2,256,1024]{2,1,0:T(8,128)(2,1)S(1)} %shard_map.18.mine, bf16[2,256,1024]{2,1,0:T(8,128)(2,1)S(1)} %collective-permute-done.3.other, bf16[64,1024]{1,0:T(8,128)(2,1)S(1)} %get-tuple-element.13.refs_0_, bf16[64,1024]{1,0:T(8,128)(2,1)S(1)} %collective-permute-done.5.refs_1_, ...), custom_call_target="tpu_custom_call" | custom-call | flops 10000000000 | bytes 262144 | tf_op jit(solution)/shard_map/pallas_call | solution.py:147
  25.8 3.0 %collective-permute-done.10.refs_2_ = bf16[64,1024]{1,0:T(8,128)(2,1)S(1)} collective-permute-done((bf16[64,1024]{1,0:T(8,128)(2,1)S(1)}, bf16[64,1024]{1,0:T(8,128)(2,1)S(1)}, u32[]{:S(2)}, u32[]{:S(2)}) %collective-permute-start.10) | collective-permute-done | bytes 131104 | tf_op jit(solution)/shard_map/ppermute | solution.py:139
  28.8 0.8 %collective-permute-done.9.refs_1_ = bf16[64,1024]{1,0:T(8,128)(2,1)S(1)} collective-permute-done((bf16[64,1024]{1,0:T(8,128)(2,1)S(1)}, bf16[64,1024]{1,0:T(8,128)(2,1)S(1)}, u32[]{:S(2)}, u32[]{:S(2)}) %collective-permute-start.9) | collective-permute-done | bytes 131104 | tf_op jit(solution)/shard_map/ppermute | solution.py:139
  29.6 1.6 %shard_map.23 = f32[2,256,512]{2,1,0:T(8,128)} custom-call(bf16[2,256,1024]{2,1,0:T(8,128)(2,1)S(1)} %shard_map.18.mine, bf16[2,256,1024]{2,1,0:T(8,128)(2,1)S(1)} %collective-permute-done.3.other, f32[2,256,512]{2,1,0:T(8,128)S(1)} %shard_map.21.so_far, bf16[64,1024]{1,0:T(8,128)(2,1)S(1)} %get-tuple-element.15.refs_0_, ...), custom_call_target="tpu_custom_call" | custom-call | tf_op jit(solution)/shard_map/pallas_call | solution.py:147
  (9 shorter events, 0.1 us)
Async XLA Ops:
  0.0 6.6 %copy-start = (bf16[2,64,1024]{2,1,0:T(8,128)(2,1)S(1)}, bf16[2,64,1024]{2,1,0:T(8,128)(2,1)}, u32[]{:S(2)}) copy-start(bf16[2,64,1024]{2,1,0:T(8,128)(2,1)} %fields.1) | copy-start | bytes 786436
  0.0 9.6 %collective-permute-start = (bf16[2,64,1024]{2,1,0:T(8,128)(2,1)}, bf16[2,64,1024]{2,1,0:T(8,128)(2,1)S(1)}, u32[]{:S(2)}, u32[]{:S(2)}) collective-permute-start(bf16[2,64,1024]{2,1,0:T(8,128)(2,1)} %fields.1), channel_id=1, source_target_pairs={{0,1},{1,0},{2,3},{3,2},{4,5},{5,4},{6,7},{7,6},{8,9},{9,8},{10,11... | collective-permute-start | bytes 786440 | tf_op jit(solution)/shard_map/ppermute | solution.py:139
  4.0 9.8 %collective-permute-start.4 = (bf16[64,1024]{1,0:T(8,128)(2,1)S(1)}, bf16[64,1024]{1,0:T(8,128)(2,1)S(1)}, u32[]{:S(2)}, u32[]{:S(2)}) collective-permute-start(bf16[64,1024]{1,0:T(8,128)(2,1)S(1)} %get-tuple-element.11.own_real.own), channel_id=1, source_target_pairs={{0,4},{1,5},{2,6},{3,7},{4,0},{5,1},{6,2},{7,3},{8,12},{9,13},{10,... | collective-permute-start | bytes 393224 | tf_op jit(solution)/shard_map/ppermute | solution.py:139
  6.6 10.3 %collective-permute-start.1 = (bf16[2,64,1024]{2,1,0:T(8,128)(2,1)S(1)}, bf16[2,64,1024]{2,1,0:T(8,128)(2,1)S(1)}, u32[]{:S(2)}, u32[]{:S(2)}) collective-permute-start(bf16[2,64,1024]{2,1,0:T(8,128)(2,1)S(1)} %copy-done), channel_id=1, source_target_pairs={{0,16},{1,17},{2,18},{3,19},{4,20},{5,21},{6,22},{7,23},{8,24},{9,... | collective-permute-start | bytes 786440 | tf_op jit(solution)/shard_map/ppermute | solution.py:139
  9.6 10.2 %collective-permute-start.2 = (bf16[2,64,1024]{2,1,0:T(8,128)(2,1)S(1)}, bf16[2,64,1024]{2,1,0:T(8,128)(2,1)S(1)}, u32[]{:S(2)}, u32[]{:S(2)}) collective-permute-start(bf16[2,64,1024]{2,1,0:T(8,128)(2,1)S(1)} %collective-permute-done.refs_0_), channel_id=1, source_target_pairs={{0,16},{1,17},{2,18},{3,19},{4,20},{5,21},{6,22},{7,23},{8,24},{9,... | collective-permute-start | bytes 786440 | tf_op jit(solution)/shard_map/ppermute | solution.py:139
  11.2 8.7 %collective-permute-start.8 = (bf16[64,1024]{1,0:T(8,128)(2,1)S(1)}, bf16[64,1024]{1,0:T(8,128)(2,1)S(1)}, u32[]{:S(2)}, u32[]{:S(2)}) collective-permute-start(bf16[64,1024]{1,0:T(8,128)(2,1)S(1)} %get-tuple-element.12.own_imag.own), channel_id=1, source_target_pairs={{0,4},{1,5},{2,6},{3,7},{4,0},{5,1},{6,2},{7,3},{8,12},{9,13},{10,... | collective-permute-start | bytes 393224 | tf_op jit(solution)/shard_map/ppermute | solution.py:139
  13.8 9.9 %collective-permute-start.7 = (bf16[64,1024]{1,0:T(8,128)(2,1)S(1)}, bf16[64,1024]{1,0:T(8,128)(2,1)S(1)}, u32[]{:S(2)}, u32[]{:S(2)}) collective-permute-start(bf16[64,1024]{1,0:T(8,128)(2,1)S(1)} %get-tuple-element.14), channel_id=1, source_target_pairs={{0,3},{1,2},{2,1},{3,0},{4,7},{5,6},{6,5},{7,4},{8,11},{9,10},{10,... | collective-permute-start | bytes 393224 | tf_op jit(solution)/shard_map/ppermute | solution.py:139
  16.4 8.6 %collective-permute-start.5 = (bf16[64,1024]{1,0:T(8,128)(2,1)S(1)}, bf16[64,1024]{1,0:T(8,128)(2,1)S(1)}, u32[]{:S(2)}, u32[]{:S(2)}) collective-permute-start(bf16[64,1024]{1,0:T(8,128)(2,1)S(1)} %get-tuple-element.14), channel_id=1, source_target_pairs={{0,1},{1,0},{2,3},{3,2},{4,5},{5,4},{6,7},{7,6},{8,9},{9,8},{10,11... | collective-permute-start | bytes 393224 | tf_op jit(solution)/shard_map/ppermute | solution.py:139
  17.0 6.3 %collective-permute-start.6 = (bf16[64,1024]{1,0:T(8,128)(2,1)S(1)}, bf16[64,1024]{1,0:T(8,128)(2,1)S(1)}, u32[]{:S(2)}, u32[]{:S(2)}) collective-permute-start(bf16[64,1024]{1,0:T(8,128)(2,1)S(1)} %get-tuple-element.13.refs_0_), channel_id=1, source_target_pairs={{0,2},{1,3},{2,0},{3,1},{4,6},{5,7},{6,4},{7,5},{8,10},{9,11},{10,... | collective-permute-start | bytes 393224 | tf_op jit(solution)/shard_map/ppermute | solution.py:139
  19.8 5.2 %collective-permute-start.3 = (bf16[2,256,1024]{2,1,0:T(8,128)(2,1)S(1)}, bf16[2,256,1024]{2,1,0:T(8,128)(2,1)S(1)}, u32[]{:S(2)}, u32[]{:S(2)}) collective-permute-start(bf16[2,256,1024]{2,1,0:T(8,128)(2,1)S(1)} %shard_map.18.mine), channel_id=1, source_target_pairs={{0,8},{1,9},{2,10},{3,11},{4,12},{5,13},{6,14},{7,15},{8,0},{9,1},... | collective-permute-start | bytes 3145736 | tf_op jit(solution)/shard_map/ppermute | solution.py:139
  20.0 8.8 %collective-permute-start.11 = (bf16[64,1024]{1,0:T(8,128)(2,1)S(1)}, bf16[64,1024]{1,0:T(8,128)(2,1)S(1)}, u32[]{:S(2)}, u32[]{:S(2)}) collective-permute-start(bf16[64,1024]{1,0:T(8,128)(2,1)S(1)} %get-tuple-element.16), channel_id=1, source_target_pairs={{0,3},{1,2},{2,1},{3,0},{4,7},{5,6},{6,5},{7,4},{8,11},{9,10},{10,... | collective-permute-start | bytes 393224 | tf_op jit(solution)/shard_map/ppermute | solution.py:139
  23.2 6.4 %collective-permute-start.9 = (bf16[64,1024]{1,0:T(8,128)(2,1)S(1)}, bf16[64,1024]{1,0:T(8,128)(2,1)S(1)}, u32[]{:S(2)}, u32[]{:S(2)}) collective-permute-start(bf16[64,1024]{1,0:T(8,128)(2,1)S(1)} %get-tuple-element.16), channel_id=1, source_target_pairs={{0,1},{1,0},{2,3},{3,2},{4,5},{5,4},{6,7},{7,6},{8,9},{9,8},{10,11... | collective-permute-start | bytes 393224 | tf_op jit(solution)/shard_map/ppermute | solution.py:139
  23.7 5.1 %collective-permute-start.10 = (bf16[64,1024]{1,0:T(8,128)(2,1)S(1)}, bf16[64,1024]{1,0:T(8,128)(2,1)S(1)}, u32[]{:S(2)}, u32[]{:S(2)}) collective-permute-start(bf16[64,1024]{1,0:T(8,128)(2,1)S(1)} %get-tuple-element.15.refs_0_), channel_id=1, source_target_pairs={{0,2},{1,3},{2,0},{3,1},{4,6},{5,7},{6,4},{7,5},{8,10},{9,11},{10,... | collective-permute-start | bytes 393224 | tf_op jit(solution)/shard_map/ppermute | solution.py:139

commit v6 on v3

v6 whole, which is shorter than its diff:
```python
import functools

import jax
import jax.numpy as jnp
from jax import lax
from jax.experimental import pallas as pl
from jax.experimental.pallas import tpu as pltpu
from jax.sharding import PartitionSpec as P

AXES = ("row", "col", "slab")
TILE = 256
ANY = pl.BlockSpec(memory_space=pl.ANY)
VMEM = pl.BlockSpec(memory_space=pltpu.VMEM)
PARAMS = pltpu.CompilerParams(vmem_limit_bytes=24 * 1024 * 1024)
EARLY, MIDDLE = 30_000_000_000, 5_000_000_000


def weight(flops):
    return pl.CostEstimate(flops=flops, bytes_accessed=1 << 18, transcendentals=0) if flops else None


def dot(left, right):
    return lax.dot_general(left, right, (((1,), (1,)), ((), ())), preferred_element_type=jnp.float32)


def in_vmem(arrays):
    return [pltpu.with_memory_space_constraint(array, pltpu.VMEM) for array in arrays]


def split_kernel(starts, fields, *refs):
    outs, sems = refs[:-1], refs[-1]
    copies = [
        pltpu.make_async_copy(fields.at[:, :, pl.ds(at, out.shape[2])], out, sems.at[i])
        for i, (at, out) in enumerate(zip(starts, outs))
    ]
    for copy in copies:
        copy.start()
    for copy in copies:
        copy.wait()


def relay_kernel(part, *refs):
    out = refs[-1]
    out[...] = part[...]


def choose_kernel(sizes, own, far, keep, give):
    near = lax.div(lax.axis_index("col"), sizes[1] // 2) == lax.axis_index("slab")
    keep[...] = jnp.where(near, own[...], far[...])
    give[...] = jnp.where(near, far[...], own[...])


def order_kernel(sizes, offsets, starts, *refs):
    r, s = lax.axis_index("row"), lax.axis_index("slab")
    own, cols, mine = refs[: len(starts)], refs[len(starts) : -1], refs[-1]
    size = own[0].shape[1]

    def place(dr, ds):
        at = lax.div(lax.bitwise_xor(r, dr), 2) * sizes[2] + lax.bitwise_xor(s, ds)
        return pl.ds(pl.multiple_of(at * size, size), size)

    for start, part in zip(starts, own):
        mine[:, place(0, 0), start : start + part.shape[2]] = part[...]
    for ref, (dr, ds) in zip(cols, offsets[1:]):
        mine[:, place(dr, ds)] = ref[...]


def rows_in_order(sizes, places, refs, left):
    c, s = lax.axis_index("col"), lax.axis_index("slab")
    for ref, (shift, turn) in zip(refs, places):
        size = ref.shape[1]
        at = lax.rem(lax.bitwise_xor(c, shift), sizes[1] // 2) * sizes[2] + lax.bitwise_xor(s, turn)
        left[:, pl.ds(pl.multiple_of(at * size, size), size)] = ref[...]


def over_columns(sizes, start, left, mine, other, step):
    group = mine.shape[1] // (sizes[0] // 2)
    core = lax.rem(lax.axis_index("row"), 2)
    pixels = pl.ds(start, left.shape[2])
    for cols, which in ((mine, core), (other, 1 - core)):

        @pl.loop(0, mine.shape[1] // TILE)
        def _(tile):
            here = pl.ds(pl.multiple_of(tile * TILE, TILE), TILE)
            c_real, c_imag = cols[0, here, pixels], cols[1, here, pixels]
            real = dot(left[0], c_real) + dot(left[1], c_imag)
            imag = dot(left[0], c_imag) - dot(left[1], c_real)
            for i in range(TILE // group):
                at = pl.multiple_of((2 * (tile * (TILE // group) + i) + which) * group, group)
                step(pl.ds(at, group), at, real[:, i * group : (i + 1) * group], imag[:, i * group : (i + 1) * group])


def middle_kernel(sizes, places, start, first, mine, other, *refs):
    so_far, blocks, (out, left) = (None if first else refs[0]), refs[0 if first else 1 : -2], refs[-2:]
    rows_in_order(sizes, places, blocks, left)

    def step(here, at, real, imag):
        out[0, :, here] = real if first else so_far[0, :, here] + real
        out[1, :, here] = imag if first else so_far[1, :, here] + imag

    over_columns(sizes, start, left, mine, other, step)


def last_kernel(sizes, places, start, mine, other, so_far, *refs):
    blocks, (out, left, wide, sem) = refs[:-4], refs[-4:]
    rows_in_order(sizes, places, blocks, left)
    group = mine.shape[1] // (sizes[0] // 2)

    def copy(at):
        return pltpu.make_async_copy(wide.at[:, :, pl.ds(at, group)], out.at[:, :, pl.ds(at, group)], sem.at[at // group])

    def step(here, at, real, imag):
        wide[0, :, here] = so_far[0, :, here] + real
        wide[1, :, here] = so_far[1, :, here] + imag
        copy(at).start()

    over_columns(sizes, start, left, mine, other, step)

    @pl.loop(0, out.shape[2] // group)
    def _(i):
        copy(pl.multiple_of(i * group, group)).wait()


def solution(mesh):
    sizes = tuple(mesh.shape[axis] for axis in AXES)
    rows, cols, slabs = sizes
    half = cols // 2

    def exchange(array, dr, dc, ds):
        pairs = []
        for r in range(rows):
            for c in range(cols):
                for s in range(slabs):
                    pairs.append(((r * cols + c) * slabs + s, ((r ^ dr) * cols + (c ^ dc)) * slabs + (s ^ ds)))
        return lax.ppermute(array, AXES, pairs)

    def body(fields):
        _, size, pixels = fields.shape
        out_rows, out_cols = half * slabs * size, rows * slabs * size
        parts = [pixels // 2] * 2
        starts = [sum(parts[:i]) for i in range(len(parts))]
        shapes = [pltpu.VMEM((2, size, p), fields.dtype) for p in parts]

        def call(kernel, out_shape, arrays, scratch=(), specs=None, flops=0, out_spec=VMEM):
            return pl.pallas_call(
                kernel,
                out_shape=out_shape,
                in_specs=specs or [VMEM] * len(arrays),
                out_specs=jax.tree.map(lambda _: out_spec, out_shape),
                scratch_shapes=scratch,
                compiler_params=PARAMS,
                cost_estimate=weight(flops),
            )(*(arrays if specs else in_vmem(arrays)))

        own = call(
            functools.partial(split_kernel, starts), shapes, [pltpu.with_memory_space_constraint(fields, pltpu.HBM)],
            [pltpu.SemaphoreType.DMA((len(parts),))], [ANY],
        )
        blocks, offsets = [fields], [(0, 0)]
        steps = [(0, 1)]
        bit = rows // 2
        while bit > 1:
            steps.append((bit, 0))
            bit //= 2
        for dr, ds in steps:
            blocks = blocks + [exchange(block, dr, 0, ds) for block in blocks]
            offsets = offsets + [(a ^ dr, b ^ ds) for a, b in offsets]
        mine = call(
            functools.partial(order_kernel, sizes, offsets, starts),
            pltpu.VMEM((2, out_cols // 2, pixels), fields.dtype), [*own, *blocks[1:]],
        )
        other = exchange(mine, 1, 0, 0)
        places = [(shift, turn) for shift in range(half) for turn in range(slabs)]
        slots = []
        for i, part in enumerate(own):
            if i > 0:
                part = call(relay_kernel, shapes[i], [part, blocks[1]])
            far = exchange(part, 0, half, 0)
            keep, give = call(functools.partial(choose_kernel, sizes), [shapes[i]] * 2, [part, far], flops=EARLY)
            got = [keep]
            for shift, turn in places[1:]:
                got.append(exchange(give if turn else keep, 0, shift, turn))
            slots.append(got)
        so_far = []
        for i in range(len(parts) - 1):
            so_far = [
                call(
                    functools.partial(middle_kernel, sizes, places, starts[i], i == 0),
                    pltpu.VMEM((2, out_rows, out_cols), jnp.float32), [mine, other, *so_far, *slots[i]],
                    [pltpu.VMEM((2, out_rows, parts[i]), fields.dtype)], flops=MIDDLE,
                )
            ]
        return call(
            functools.partial(last_kernel, sizes, places, starts[-1]),
            jax.ShapeDtypeStruct((2, out_rows, out_cols), jnp.float32), [mine, other, *so_far, *slots[-1]],
            [
                pltpu.VMEM((2, out_rows, parts[-1]), fields.dtype),
                pltpu.VMEM((2, out_rows, out_cols), jnp.float32),
                pltpu.SemaphoreType.DMA((rows,)),
            ],
            out_spec=ANY,
        )

    placed = (P(None, AXES, None),)
    return jax.shard_map(
        body, mesh=mesh, in_specs=placed, out_specs=P(None, ("row", "slab"), "col"), check_vma=False
    )
```

time: 31.4 us -> 31.4 us (level)
  no operation moved by 1% of the time
where the time goes in v6:
time: 31.4 us; the launch traced here: 31.2 us
  starting transfers between devices  18.6 us (59%)
  waiting for transfers between devices  9.08 us (29%)
  Pallas kernels  3.54 us (11%)
    ppermute x12, starting transfers between devices, exchange(): return lax.ppermute(array, AXES, pairs)  18.6 us
    ppermute x12, waiting for transfers between devices, exchange(): return lax.ppermute(array, AXES, pairs)  9.08 us
    pallas_call x7, Pallas kernels, call(): pl.pallas_call(kernel, out_shape=out_shape, in_specs=specs or [VMEM] * le...  3.54 us
  transfers between devices with their start and end apart: 12, of which 5 were waited for; matrix products, arithmetic and copies ran while one was open for 0% of the time, Pallas kernels for 6%

profile of v6, /device:TPU:0, one launch (start us, length us, event | category | flops | bytes accessed | tf_op | source)
XLA Modules:
  0.0 31.2 jit_solution(6081805653727607333)
XLA Ops:
  0.0 3.0 %collective-permute-start = (bf16[2,64,1024]{2,1,0:T(8,128)(2,1)}, bf16[2,64,1024]{2,1,0:T(8,128)(2,1)S(1)}, u32[]{:S(2)}, u32[]{:S(2)}) collective-permute-start(bf16[2,64,1024]{2,1,0:T(8,128)(2,1)} %fields.1), channel_id=1, source_target_pairs={{0,1},{1,0},{2,3},{3,2},{4,5},{5,4},{6,7},{7,6},{8,9},{9,8},{10,11... | collective-permute-start | bytes 786440 | tf_op jit(solution)/shard_map/ppermute | solution.py:135
  3.0 1.0 %shard_map.17 = (bf16[2,64,512]{2,1,0:T(8,128)(2,1)S(1)}, bf16[2,64,512]{2,1,0:T(8,128)(2,1)S(1)}) custom-call(bf16[2,64,1024]{2,1,0:T(8,128)(2,1)} %fields.1), custom_call_target="tpu_custom_call" | custom-call | tf_op jit(solution)/shard_map/pallas_call | solution.py:145
  4.0 2.7 %collective-permute-start.4 = (bf16[2,64,512]{2,1,0:T(8,128)(2,1)S(1)}, bf16[2,64,512]{2,1,0:T(8,128)(2,1)S(1)}, u32[]{:S(2)}, u32[]{:S(2)}) collective-permute-start(bf16[2,64,512]{2,1,0:T(8,128)(2,1)S(1)} %get-tuple-element.11.refs_0_.own), channel_id=1, source_target_pairs={{0,4},{1,5},{2,6},{3,7},{4,0},{5,1},{6,2},{7,3},{8,12},{9,13},{10,... | collective-permute-start | bytes 393224 | tf_op jit(solution)/shard_map/ppermute | solution.py:135
  6.6 1.5 %collective-permute-start.1 = (bf16[2,64,1024]{2,1,0:T(8,128)(2,1)S(1)}, bf16[2,64,1024]{2,1,0:T(8,128)(2,1)S(1)}, u32[]{:S(2)}, u32[]{:S(2)}) collective-permute-start(bf16[2,64,1024]{2,1,0:T(8,128)(2,1)S(1)} %copy-done), channel_id=1, source_target_pairs={{0,16},{1,17},{2,18},{3,19},{4,20},{5,21},{6,22},{7,23},{8,24},{9,... | collective-permute-start | bytes 786440 | tf_op jit(solution)/shard_map/ppermute | solution.py:135
  8.1 1.4 %collective-permute-done.refs_2_.refs_0_ = bf16[2,64,1024]{2,1,0:T(8,128)(2,1)S(1)} collective-permute-done((bf16[2,64,1024]{2,1,0:T(8,128)(2,1)}, bf16[2,64,1024]{2,1,0:T(8,128)(2,1)S(1)}, u32[]{:S(2)}, u32[]{:S(2)}) %collective-permute-start) | collective-permute-done | bytes 262176 | tf_op jit(solution)/shard_map/ppermute | solution.py:135
  9.6 2.8 %collective-permute-start.8 = (bf16[2,64,512]{2,1,0:T(8,128)(2,1)S(1)}, bf16[2,64,512]{2,1,0:T(8,128)(2,1)S(1)}, u32[]{:S(2)}, u32[]{:S(2)}) collective-permute-start(bf16[2,64,512]{2,1,0:T(8,128)(2,1)S(1)} %shard_map.21.own), channel_id=1, source_target_pairs={{0,4},{1,5},{2,6},{3,7},{4,0},{5,1},{6,2},{7,3},{8,12},{9,13},{10,... | collective-permute-start | bytes 393224 | tf_op jit(solution)/shard_map/ppermute | solution.py:135
  12.4 1.5 %collective-permute-start.2 = (bf16[2,64,1024]{2,1,0:T(8,128)(2,1)S(1)}, bf16[2,64,1024]{2,1,0:T(8,128)(2,1)S(1)}, u32[]{:S(2)}, u32[]{:S(2)}) collective-permute-start(bf16[2,64,1024]{2,1,0:T(8,128)(2,1)S(1)} %collective-permute-done.refs_2_.refs_0_), channel_id=1, source_target_pairs={{0,16},{1,17},{2,18},{3,19},{4,20},{5,21},{6,22},{7,23},{8,24},{9,... | collective-permute-start | bytes 786440 | tf_op jit(solution)/shard_map/ppermute | solution.py:135
  13.9 0.0 collective-permute-done.4.far
  13.9 2.6 %collective-permute-start.7 = (bf16[2,64,512]{2,1,0:T(8,128)(2,1)S(1)}, bf16[2,64,512]{2,1,0:T(8,128)(2,1)S(1)}, u32[]{:S(2)}, u32[]{:S(2)}) collective-permute-start(bf16[2,64,512]{2,1,0:T(8,128)(2,1)S(1)} %get-tuple-element.14), channel_id=1, source_target_pairs={{0,3},{1,2},{2,1},{3,0},{4,7},{5,6},{6,5},{7,4},{8,11},{9,10},{10,... | collective-permute-start | bytes 393224 | tf_op jit(solution)/shard_map/ppermute | solution.py:135
  16.5 0.5 %collective-permute-start.5 = (bf16[2,64,512]{2,1,0:T(8,128)(2,1)S(1)}, bf16[2,64,512]{2,1,0:T(8,128)(2,1)S(1)}, u32[]{:S(2)}, u32[]{:S(2)}) collective-permute-start(bf16[2,64,512]{2,1,0:T(8,128)(2,1)S(1)} %get-tuple-element.14), channel_id=1, source_target_pairs={{0,1},{1,0},{2,3},{3,2},{4,5},{5,4},{6,7},{7,6},{8,9},{9,8},{10,11... | collective-permute-start | bytes 393224 | tf_op jit(solution)/shard_map/ppermute | solution.py:135
  17.0 0.0 collective-permute-done.1.refs_3_
  17.0 0.5 %collective-permute-start.6 = (bf16[2,64,512]{2,1,0:T(8,128)(2,1)S(1)}, bf16[2,64,512]{2,1,0:T(8,128)(2,1)S(1)}, u32[]{:S(2)}, u32[]{:S(2)}) collective-permute-start(bf16[2,64,512]{2,1,0:T(8,128)(2,1)S(1)} %get-tuple-element.13.refs_0_), channel_id=1, source_target_pairs={{0,2},{1,3},{2,0},{3,1},{4,6},{5,7},{6,4},{7,5},{8,10},{9,11},{10,... | collective-permute-start | bytes 393224 | tf_op jit(solution)/shard_map/ppermute | solution.py:135
  17.5 2.3 %collective-permute-done.2.refs_4_ = bf16[2,64,1024]{2,1,0:T(8,128)(2,1)S(1)} collective-permute-done((bf16[2,64,1024]{2,1,0:T(8,128)(2,1)S(1)}, bf16[2,64,1024]{2,1,0:T(8,128)(2,1)S(1)}, u32[]{:S(2)}, u32[]{:S(2)}) %collective-permute-start.2) | collective-permute-done | bytes 262176 | tf_op jit(solution)/shard_map/ppermute | solution.py:135
  19.7 0.1 shard_map.18.mine
  19.8 0.1 collective-permute-start.3
  20.0 2.1 %collective-permute-start.11 = (bf16[2,64,512]{2,1,0:T(8,128)(2,1)S(1)}, bf16[2,64,512]{2,1,0:T(8,128)(2,1)S(1)}, u32[]{:S(2)}, u32[]{:S(2)}) collective-permute-start(bf16[2,64,512]{2,1,0:T(8,128)(2,1)S(1)} %get-tuple-element.16), channel_id=1, source_target_pairs={{0,3},{1,2},{2,1},{3,0},{4,7},{5,6},{6,5},{7,4},{8,11},{9,10},{10,... | collective-permute-start | bytes 393224 | tf_op jit(solution)/shard_map/ppermute | solution.py:135
  22.1 1.0 %collective-permute-done.6.refs_2_ = bf16[2,64,512]{2,1,0:T(8,128)(2,1)S(1)} collective-permute-done((bf16[2,64,512]{2,1,0:T(8,128)(2,1)S(1)}, bf16[2,64,512]{2,1,0:T(8,128)(2,1)S(1)}, u32[]{:S(2)}, u32[]{:S(2)}) %collective-permute-start.6) | collective-permute-done | bytes 131104 | tf_op jit(solution)/shard_map/ppermute | solution.py:135
  23.1 0.5 %collective-permute-start.9 = (bf16[2,64,512]{2,1,0:T(8,128)(2,1)S(1)}, bf16[2,64,512]{2,1,0:T(8,128)(2,1)S(1)}, u32[]{:S(2)}, u32[]{:S(2)}) collective-permute-start(bf16[2,64,512]{2,1,0:T(8,128)(2,1)S(1)} %get-tuple-element.16), channel_id=1, source_target_pairs={{0,1},{1,0},{2,3},{3,2},{4,5},{5,4},{6,7},{7,6},{8,9},{9,8},{10,11... | collective-permute-start | bytes 393224 | tf_op jit(solution)/shard_map/ppermute | solution.py:135
  23.6 0.0 collective-permute-done.7.refs_3_
  23.6 0.9 %collective-permute-start.10 = (bf16[2,64,512]{2,1,0:T(8,128)(2,1)S(1)}, bf16[2,64,512]{2,1,0:T(8,128)(2,1)S(1)}, u32[]{:S(2)}, u32[]{:S(2)}) collective-permute-start(bf16[2,64,512]{2,1,0:T(8,128)(2,1)S(1)} %get-tuple-element.15.refs_0_), channel_id=1, source_target_pairs={{0,2},{1,3},{2,0},{3,1},{4,6},{5,7},{6,4},{7,5},{8,10},{9,11},{10,... | collective-permute-start | bytes 393224 | tf_op jit(solution)/shard_map/ppermute | solution.py:135
  24.5 0.8 %shard_map.20.so_far = f32[2,256,512]{2,1,0:T(8,128)S(1)} custom-call(bf16[2,256,1024]{2,1,0:T(8,128)(2,1)S(1)} %shard_map.18.mine, bf16[2,256,1024]{2,1,0:T(8,128)(2,1)S(1)} %collective-permute-done.3.other, bf16[2,64,512]{2,1,0:T(8,128)(2,1)S(1)} %get-tuple-element.13.refs_0_, bf16[2,64,512]{2,1,0:T(8,128)(2,1)S(1)} %collective-permute-done.5.refs_1_, ...), custom_call_target="tpu_custom_call" | custom-call | flops 5000000000 | bytes 262144 | tf_op jit(solution)/shard_map/pallas_call | solution.py:145
  25.3 4.0 %collective-permute-done.10.refs_2_ = bf16[2,64,512]{2,1,0:T(8,128)(2,1)S(1)} collective-permute-done((bf16[2,64,512]{2,1,0:T(8,128)(2,1)S(1)}, bf16[2,64,512]{2,1,0:T(8,128)(2,1)S(1)}, u32[]{:S(2)}, u32[]{:S(2)}) %collective-permute-start.10) | collective-permute-done | bytes 131104 | tf_op jit(solution)/shard_map/ppermute | solution.py:135
  29.2 0.4 %collective-permute-done.9.refs_1_ = bf16[2,64,512]{2,1,0:T(8,128)(2,1)S(1)} collective-permute-done((bf16[2,64,512]{2,1,0:T(8,128)(2,1)S(1)}, bf16[2,64,512]{2,1,0:T(8,128)(2,1)S(1)}, u32[]{:S(2)}, u32[]{:S(2)}) %collective-permute-start.9) | collective-permute-done | bytes 131104 | tf_op jit(solution)/shard_map/ppermute | solution.py:135
  29.6 1.6 %shard_map.23 = f32[2,256,512]{2,1,0:T(8,128)} custom-call(bf16[2,256,1024]{2,1,0:T(8,128)(2,1)S(1)} %shard_map.18.mine, bf16[2,256,1024]{2,1,0:T(8,128)(2,1)S(1)} %collective-permute-done.3.other, f32[2,256,512]{2,1,0:T(8,128)S(1)} %shard_map.20.so_far, bf16[2,64,512]{2,1,0:T(8,128)(2,1)S(1)} %get-tuple-element.15.refs_0_, ...), custom_call_target="tpu_custom_call" | custom-call | tf_op jit(solution)/shard_map/pallas_call | solution.py:145
  (9 shorter events, 0.1 us)
Async XLA Ops:
  0.0 6.6 %copy-start = (bf16[2,64,1024]{2,1,0:T(8,128)(2,1)S(1)}, bf16[2,64,1024]{2,1,0:T(8,128)(2,1)}, u32[]{:S(2)}) copy-start(bf16[2,64,1024]{2,1,0:T(8,128)(2,1)} %fields.1) | copy-start | bytes 786436
  0.0 9.6 %collective-permute-start = (bf16[2,64,1024]{2,1,0:T(8,128)(2,1)}, bf16[2,64,1024]{2,1,0:T(8,128)(2,1)S(1)}, u32[]{:S(2)}, u32[]{:S(2)}) collective-permute-start(bf16[2,64,1024]{2,1,0:T(8,128)(2,1)} %fields.1), channel_id=1, source_target_pairs={{0,1},{1,0},{2,3},{3,2},{4,5},{5,4},{6,7},{7,6},{8,9},{9,8},{10,11... | collective-permute-start | bytes 786440 | tf_op jit(solution)/shard_map/ppermute | solution.py:135
  4.0 9.9 %collective-permute-start.4 = (bf16[2,64,512]{2,1,0:T(8,128)(2,1)S(1)}, bf16[2,64,512]{2,1,0:T(8,128)(2,1)S(1)}, u32[]{:S(2)}, u32[]{:S(2)}) collective-permute-start(bf16[2,64,512]{2,1,0:T(8,128)(2,1)S(1)} %get-tuple-element.11.refs_0_.own), channel_id=1, source_target_pairs={{0,4},{1,5},{2,6},{3,7},{4,0},{5,1},{6,2},{7,3},{8,12},{9,13},{10,... | collective-permute-start | bytes 393224 | tf_op jit(solution)/shard_map/ppermute | solution.py:135
  6.6 10.4 %collective-permute-start.1 = (bf16[2,64,1024]{2,1,0:T(8,128)(2,1)S(1)}, bf16[2,64,1024]{2,1,0:T(8,128)(2,1)S(1)}, u32[]{:S(2)}, u32[]{:S(2)}) collective-permute-start(bf16[2,64,1024]{2,1,0:T(8,128)(2,1)S(1)} %copy-done), channel_id=1, source_target_pairs={{0,16},{1,17},{2,18},{3,19},{4,20},{5,21},{6,22},{7,23},{8,24},{9,... | collective-permute-start | bytes 786440 | tf_op jit(solution)/shard_map/ppermute | solution.py:135
  9.6 10.3 %collective-permute-start.8 = (bf16[2,64,512]{2,1,0:T(8,128)(2,1)S(1)}, bf16[2,64,512]{2,1,0:T(8,128)(2,1)S(1)}, u32[]{:S(2)}, u32[]{:S(2)}) collective-permute-start(bf16[2,64,512]{2,1,0:T(8,128)(2,1)S(1)} %shard_map.21.own), channel_id=1, source_target_pairs={{0,4},{1,5},{2,6},{3,7},{4,0},{5,1},{6,2},{7,3},{8,12},{9,13},{10,... | collective-permute-start | bytes 393224 | tf_op jit(solution)/shard_map/ppermute | solution.py:135
  12.4 7.4 %collective-permute-start.2 = (bf16[2,64,1024]{2,1,0:T(8,128)(2,1)S(1)}, bf16[2,64,1024]{2,1,0:T(8,128)(2,1)S(1)}, u32[]{:S(2)}, u32[]{:S(2)}) collective-permute-start(bf16[2,64,1024]{2,1,0:T(8,128)(2,1)S(1)} %collective-permute-done.refs_2_.refs_0_), channel_id=1, source_target_pairs={{0,16},{1,17},{2,18},{3,19},{4,20},{5,21},{6,22},{7,23},{8,24},{9,... | collective-permute-start | bytes 786440 | tf_op jit(solution)/shard_map/ppermute | solution.py:135
  13.9 9.7 %collective-permute-start.7 = (bf16[2,64,512]{2,1,0:T(8,128)(2,1)S(1)}, bf16[2,64,512]{2,1,0:T(8,128)(2,1)S(1)}, u32[]{:S(2)}, u32[]{:S(2)}) collective-permute-start(bf16[2,64,512]{2,1,0:T(8,128)(2,1)S(1)} %get-tuple-element.14), channel_id=1, source_target_pairs={{0,3},{1,2},{2,1},{3,0},{4,7},{5,6},{6,5},{7,4},{8,11},{9,10},{10,... | collective-permute-start | bytes 393224 | tf_op jit(solution)/shard_map/ppermute | solution.py:135
  16.5 8.0 %collective-permute-start.5 = (bf16[2,64,512]{2,1,0:T(8,128)(2,1)S(1)}, bf16[2,64,512]{2,1,0:T(8,128)(2,1)S(1)}, u32[]{:S(2)}, u32[]{:S(2)}) collective-permute-start(bf16[2,64,512]{2,1,0:T(8,128)(2,1)S(1)} %get-tuple-element.14), channel_id=1, source_target_pairs={{0,1},{1,0},{2,3},{3,2},{4,5},{5,4},{6,7},{7,6},{8,9},{9,8},{10,11... | collective-permute-start | bytes 393224 | tf_op jit(solution)/shard_map/ppermute | solution.py:135
  17.0 6.1 %collective-permute-start.6 = (bf16[2,64,512]{2,1,0:T(8,128)(2,1)S(1)}, bf16[2,64,512]{2,1,0:T(8,128)(2,1)S(1)}, u32[]{:S(2)}, u32[]{:S(2)}) collective-permute-start(bf16[2,64,512]{2,1,0:T(8,128)(2,1)S(1)} %get-tuple-element.13.refs_0_), channel_id=1, source_target_pairs={{0,2},{1,3},{2,0},{3,1},{4,6},{5,7},{6,4},{7,5},{8,10},{9,11},{10,... | collective-permute-start | bytes 393224 | tf_op jit(solution)/shard_map/ppermute | solution.py:135
  19.8 4.7 %collective-permute-start.3 = (bf16[2,256,1024]{2,1,0:T(8,128)(2,1)S(1)}, bf16[2,256,1024]{2,1,0:T(8,128)(2,1)S(1)}, u32[]{:S(2)}, u32[]{:S(2)}) collective-permute-start(bf16[2,256,1024]{2,1,0:T(8,128)(2,1)S(1)} %shard_map.18.mine), channel_id=1, source_target_pairs={{0,8},{1,9},{2,10},{3,11},{4,12},{5,13},{6,14},{7,15},{8,0},{9,1},... | collective-permute-start | bytes 3145736 | tf_op jit(solution)/shard_map/ppermute | solution.py:135
  20.0 9.3 %collective-permute-start.11 = (bf16[2,64,512]{2,1,0:T(8,128)(2,1)S(1)}, bf16[2,64,512]{2,1,0:T(8,128)(2,1)S(1)}, u32[]{:S(2)}, u32[]{:S(2)}) collective-permute-start(bf16[2,64,512]{2,1,0:T(8,128)(2,1)S(1)} %get-tuple-element.16), channel_id=1, source_target_pairs={{0,3},{1,2},{2,1},{3,0},{4,7},{5,6},{6,5},{7,4},{8,11},{9,10},{10,... | collective-permute-start | bytes 393224 | tf_op jit(solution)/shard_map/ppermute | solution.py:135
  23.1 6.5 %collective-permute-start.9 = (bf16[2,64,512]{2,1,0:T(8,128)(2,1)S(1)}, bf16[2,64,512]{2,1,0:T(8,128)(2,1)S(1)}, u32[]{:S(2)}, u32[]{:S(2)}) collective-permute-start(bf16[2,64,512]{2,1,0:T(8,128)(2,1)S(1)} %get-tuple-element.16), channel_id=1, source_target_pairs={{0,1},{1,0},{2,3},{3,2},{4,5},{5,4},{6,7},{7,6},{8,9},{9,8},{10,11... | collective-permute-start | bytes 393224 | tf_op jit(solution)/shard_map/ppermute | solution.py:135
  23.6 5.6 %collective-permute-start.10 = (bf16[2,64,512]{2,1,0:T(8,128)(2,1)S(1)}, bf16[2,64,512]{2,1,0:T(8,128)(2,1)S(1)}, u32[]{:S(2)}, u32[]{:S(2)}) collective-permute-start(bf16[2,64,512]{2,1,0:T(8,128)(2,1)S(1)} %get-tuple-element.15.refs_0_), channel_id=1, source_target_pairs={{0,2},{1,3},{2,0},{3,1},{4,6},{5,7},{6,4},{7,5},{8,10},{9,11},{10,... | collective-permute-start | bytes 393224 | tf_op jit(solution)/shard_map/ppermute | solution.py:135

commit v7 on v6

--- a/solution.py
+++ b/solution.py
@@ -12,7 +12,7 @@
 ANY = pl.BlockSpec(memory_space=pl.ANY)
 VMEM = pl.BlockSpec(memory_space=pltpu.VMEM)
 PARAMS = pltpu.CompilerParams(vmem_limit_bytes=24 * 1024 * 1024)
-EARLY, MIDDLE = 30_000_000_000, 5_000_000_000
+EARLY, MIDDLE, LIGHT = 30_000_000_000, 10_000_000_000, 1_000_000_000
 
 
 def weight(flops):
@@ -173,10 +173,10 @@
         places = [(shift, turn) for shift in range(half) for turn in range(slabs)]
         slots = []
         for i, part in enumerate(own):
-            if i > 0:
-                part = call(relay_kernel, shapes[i], [part, blocks[1]])
             far = exchange(part, 0, half, 0)
-            keep, give = call(functools.partial(choose_kernel, sizes), [shapes[i]] * 2, [part, far], flops=EARLY)
+            if i == 0:
+                far = call(relay_kernel, shapes[i], [far], flops=LIGHT)
+            keep, give = call(functools.partial(choose_kernel, sizes), [shapes[i]] * 2, [part, far], flops=EARLY if i else LIGHT)
             got = [keep]
             for shift, turn in places[1:]:
                 got.append(exchange(give if turn else keep, 0, shift, turn))

time: 31.4 us -> 31.4 us (level)
  no operation moved by 1% of the time
where the time goes in v7:
time: 31.4 us; the launch traced here: 31.2 us
  starting transfers between devices  18.4 us (59%)
  waiting for transfers between devices  9.26 us (29%)
  Pallas kernels  3.54 us (11%)
    ppermute x12, starting transfers between devices, exchange(): return lax.ppermute(array, AXES, pairs)  18.4 us
    ppermute x12, waiting for transfers between devices, exchange(): return lax.ppermute(array, AXES, pairs)  9.26 us
    pallas_call x7, Pallas kernels, call(): pl.pallas_call(kernel, out_shape=out_shape, in_specs=specs or [VMEM] * le...  3.54 us
  transfers between devices with their start and end apart: 12, of which 5 were waited for; matrix products, arithmetic and copies ran while one was open for 0% of the time, Pallas kernels for 6%

profile of v7, /device:TPU:0, one launch (start us, length us, event | category | flops | bytes accessed | tf_op | source)
XLA Modules:
  0.0 31.2 jit_solution(3194321364501045543)
XLA Ops:
  0.0 3.0 %collective-permute-start = (bf16[2,64,1024]{2,1,0:T(8,128)(2,1)}, bf16[2,64,1024]{2,1,0:T(8,128)(2,1)S(1)}, u32[]{:S(2)}, u32[]{:S(2)}) collective-permute-start(bf16[2,64,1024]{2,1,0:T(8,128)(2,1)} %fields.1), channel_id=1, source_target_pairs={{0,1},{1,0},{2,3},{3,2},{4,5},{5,4},{6,7},{7,6},{8,9},{9,8},{10,11... | collective-permute-start | bytes 786440 | tf_op jit(solution)/shard_map/ppermute | solution.py:135
  3.0 1.0 %shard_map.17 = (bf16[2,64,512]{2,1,0:T(8,128)(2,1)S(1)}, bf16[2,64,512]{2,1,0:T(8,128)(2,1)S(1)}) custom-call(bf16[2,64,1024]{2,1,0:T(8,128)(2,1)} %fields.1), custom_call_target="tpu_custom_call" | custom-call | tf_op jit(solution)/shard_map/pallas_call | solution.py:145
  4.0 2.7 %collective-permute-start.4 = (bf16[2,64,512]{2,1,0:T(8,128)(2,1)S(1)}, bf16[2,64,512]{2,1,0:T(8,128)(2,1)S(1)}, u32[]{:S(2)}, u32[]{:S(2)}) collective-permute-start(bf16[2,64,512]{2,1,0:T(8,128)(2,1)S(1)} %get-tuple-element.11.refs_0_.own), channel_id=1, source_target_pairs={{0,4},{1,5},{2,6},{3,7},{4,0},{5,1},{6,2},{7,3},{8,12},{9,13},{10,... | collective-permute-start | bytes 393224 | tf_op jit(solution)/shard_map/ppermute | solution.py:135
  6.6 1.5 %collective-permute-start.1 = (bf16[2,64,1024]{2,1,0:T(8,128)(2,1)S(1)}, bf16[2,64,1024]{2,1,0:T(8,128)(2,1)S(1)}, u32[]{:S(2)}, u32[]{:S(2)}) collective-permute-start(bf16[2,64,1024]{2,1,0:T(8,128)(2,1)S(1)} %copy-done), channel_id=1, source_target_pairs={{0,16},{1,17},{2,18},{3,19},{4,20},{5,21},{6,22},{7,23},{8,24},{9,... | collective-permute-start | bytes 786440 | tf_op jit(solution)/shard_map/ppermute | solution.py:135
  8.1 1.4 %collective-permute-done.refs_2_ = bf16[2,64,1024]{2,1,0:T(8,128)(2,1)S(1)} collective-permute-done((bf16[2,64,1024]{2,1,0:T(8,128)(2,1)}, bf16[2,64,1024]{2,1,0:T(8,128)(2,1)S(1)}, u32[]{:S(2)}, u32[]{:S(2)}) %collective-permute-start) | collective-permute-done | bytes 262176 | tf_op jit(solution)/shard_map/ppermute | solution.py:135
  9.6 1.6 %collective-permute-start.2 = (bf16[2,64,1024]{2,1,0:T(8,128)(2,1)S(1)}, bf16[2,64,1024]{2,1,0:T(8,128)(2,1)S(1)}, u32[]{:S(2)}, u32[]{:S(2)}) collective-permute-start(bf16[2,64,1024]{2,1,0:T(8,128)(2,1)S(1)} %collective-permute-done.refs_2_), channel_id=1, source_target_pairs={{0,16},{1,17},{2,18},{3,19},{4,20},{5,21},{6,22},{7,23},{8,24},{9,... | collective-permute-start | bytes 786440 | tf_op jit(solution)/shard_map/ppermute | solution.py:135
  11.2 2.6 %collective-permute-start.8 = (bf16[2,64,512]{2,1,0:T(8,128)(2,1)S(1)}, bf16[2,64,512]{2,1,0:T(8,128)(2,1)S(1)}, u32[]{:S(2)}, u32[]{:S(2)}) collective-permute-start(bf16[2,64,512]{2,1,0:T(8,128)(2,1)S(1)} %get-tuple-element.12.refs_1_.own), channel_id=1, source_target_pairs={{0,4},{1,5},{2,6},{3,7},{4,0},{5,1},{6,2},{7,3},{8,12},{9,13},{10,... | collective-permute-start | bytes 393224 | tf_op jit(solution)/shard_map/ppermute | solution.py:135
  13.8 2.6 %collective-permute-start.7 = (bf16[2,64,512]{2,1,0:T(8,128)(2,1)S(1)}, bf16[2,64,512]{2,1,0:T(8,128)(2,1)S(1)}, u32[]{:S(2)}, u32[]{:S(2)}) collective-permute-start(bf16[2,64,512]{2,1,0:T(8,128)(2,1)S(1)} %get-tuple-element.14), channel_id=1, source_target_pairs={{0,3},{1,2},{2,1},{3,0},{4,7},{5,6},{6,5},{7,4},{8,11},{9,10},{10,... | collective-permute-start | bytes 393224 | tf_op jit(solution)/shard_map/ppermute | solution.py:135
  16.4 0.5 %collective-permute-start.5 = (bf16[2,64,512]{2,1,0:T(8,128)(2,1)S(1)}, bf16[2,64,512]{2,1,0:T(8,128)(2,1)S(1)}, u32[]{:S(2)}, u32[]{:S(2)}) collective-permute-start(bf16[2,64,512]{2,1,0:T(8,128)(2,1)S(1)} %get-tuple-element.14), channel_id=1, source_target_pairs={{0,1},{1,0},{2,3},{3,2},{4,5},{5,4},{6,7},{7,6},{8,9},{9,8},{10,11... | collective-permute-start | bytes 393224 | tf_op jit(solution)/shard_map/ppermute | solution.py:135
  17.0 0.0 collective-permute-done.1.refs_3_
  17.0 0.5 %collective-permute-start.6 = (bf16[2,64,512]{2,1,0:T(8,128)(2,1)S(1)}, bf16[2,64,512]{2,1,0:T(8,128)(2,1)S(1)}, u32[]{:S(2)}, u32[]{:S(2)}) collective-permute-start(bf16[2,64,512]{2,1,0:T(8,128)(2,1)S(1)} %get-tuple-element.13.refs_0_), channel_id=1, source_target_pairs={{0,2},{1,3},{2,0},{3,1},{4,6},{5,7},{6,4},{7,5},{8,10},{9,11},{10,... | collective-permute-start | bytes 393224 | tf_op jit(solution)/shard_map/ppermute | solution.py:135
  17.5 2.3 %collective-permute-done.2.refs_4_ = bf16[2,64,1024]{2,1,0:T(8,128)(2,1)S(1)} collective-permute-done((bf16[2,64,1024]{2,1,0:T(8,128)(2,1)S(1)}, bf16[2,64,1024]{2,1,0:T(8,128)(2,1)S(1)}, u32[]{:S(2)}, u32[]{:S(2)}) %collective-permute-start.2) | collective-permute-done | bytes 262176 | tf_op jit(solution)/shard_map/ppermute | solution.py:135
  19.7 0.1 shard_map.18.mine
  19.8 0.1 collective-permute-start.3
  20.0 1.6 %collective-permute-start.11 = (bf16[2,64,512]{2,1,0:T(8,128)(2,1)S(1)}, bf16[2,64,512]{2,1,0:T(8,128)(2,1)S(1)}, u32[]{:S(2)}, u32[]{:S(2)}) collective-permute-start(bf16[2,64,512]{2,1,0:T(8,128)(2,1)S(1)} %get-tuple-element.16), channel_id=1, source_target_pairs={{0,3},{1,2},{2,1},{3,0},{4,7},{5,6},{6,5},{7,4},{8,11},{9,10},{10,... | collective-permute-start | bytes 393224 | tf_op jit(solution)/shard_map/ppermute | solution.py:135
  21.5 1.7 %collective-permute-done.6.refs_2_ = bf16[2,64,512]{2,1,0:T(8,128)(2,1)S(1)} collective-permute-done((bf16[2,64,512]{2,1,0:T(8,128)(2,1)S(1)}, bf16[2,64,512]{2,1,0:T(8,128)(2,1)S(1)}, u32[]{:S(2)}, u32[]{:S(2)}) %collective-permute-start.6) | collective-permute-done | bytes 131104 | tf_op jit(solution)/shard_map/ppermute | solution.py:135
  23.2 0.5 %collective-permute-start.9 = (bf16[2,64,512]{2,1,0:T(8,128)(2,1)S(1)}, bf16[2,64,512]{2,1,0:T(8,128)(2,1)S(1)}, u32[]{:S(2)}, u32[]{:S(2)}) collective-permute-start(bf16[2,64,512]{2,1,0:T(8,128)(2,1)S(1)} %get-tuple-element.16), channel_id=1, source_target_pairs={{0,1},{1,0},{2,3},{3,2},{4,5},{5,4},{6,7},{7,6},{8,9},{9,8},{10,11... | collective-permute-start | bytes 393224 | tf_op jit(solution)/shard_map/ppermute | solution.py:135
  23.7 0.0 collective-permute-done.7.refs_3_
  23.7 1.3 %collective-permute-start.10 = (bf16[2,64,512]{2,1,0:T(8,128)(2,1)S(1)}, bf16[2,64,512]{2,1,0:T(8,128)(2,1)S(1)}, u32[]{:S(2)}, u32[]{:S(2)}) collective-permute-start(bf16[2,64,512]{2,1,0:T(8,128)(2,1)S(1)} %get-tuple-element.15.refs_0_), channel_id=1, source_target_pairs={{0,2},{1,3},{2,0},{3,1},{4,6},{5,7},{6,4},{7,5},{8,10},{9,11},{10,... | collective-permute-start | bytes 393224 | tf_op jit(solution)/shard_map/ppermute | solution.py:135
  25.0 0.0 collective-permute-done.5.refs_1_
  25.0 0.8 %shard_map.21.so_far = f32[2,256,512]{2,1,0:T(8,128)S(1)} custom-call(bf16[2,256,1024]{2,1,0:T(8,128)(2,1)S(1)} %shard_map.18.mine, bf16[2,256,1024]{2,1,0:T(8,128)(2,1)S(1)} %collective-permute-done.3.other, bf16[2,64,512]{2,1,0:T(8,128)(2,1)S(1)} %get-tuple-element.13.refs_0_, bf16[2,64,512]{2,1,0:T(8,128)(2,1)S(1)} %collective-permute-done.5.refs_1_, ...), custom_call_target="tpu_custom_call" | custom-call | flops 10000000000 | bytes 262144 | tf_op jit(solution)/shard_map/pallas_call | solution.py:145
  25.8 3.0 %collective-permute-done.10.refs_2_ = bf16[2,64,512]{2,1,0:T(8,128)(2,1)S(1)} collective-permute-done((bf16[2,64,512]{2,1,0:T(8,128)(2,1)S(1)}, bf16[2,64,512]{2,1,0:T(8,128)(2,1)S(1)}, u32[]{:S(2)}, u32[]{:S(2)}) %collective-permute-start.10) | collective-permute-done | bytes 131104 | tf_op jit(solution)/shard_map/ppermute | solution.py:135
  28.8 0.8 %collective-permute-done.9.refs_1_ = bf16[2,64,512]{2,1,0:T(8,128)(2,1)S(1)} collective-permute-done((bf16[2,64,512]{2,1,0:T(8,128)(2,1)S(1)}, bf16[2,64,512]{2,1,0:T(8,128)(2,1)S(1)}, u32[]{:S(2)}, u32[]{:S(2)}) %collective-permute-start.9) | collective-permute-done | bytes 131104 | tf_op jit(solution)/shard_map/ppermute | solution.py:135
  29.6 1.6 %shard_map.23 = f32[2,256,512]{2,1,0:T(8,128)} custom-call(bf16[2,256,1024]{2,1,0:T(8,128)(2,1)S(1)} %shard_map.18.mine, bf16[2,256,1024]{2,1,0:T(8,128)(2,1)S(1)} %collective-permute-done.3.other, f32[2,256,512]{2,1,0:T(8,128)S(1)} %shard_map.21.so_far, bf16[2,64,512]{2,1,0:T(8,128)(2,1)S(1)} %get-tuple-element.15.refs_0_, ...), custom_call_target="tpu_custom_call" | custom-call | tf_op jit(solution)/shard_map/pallas_call | solution.py:145
  (9 shorter events, 0.1 us)
Async XLA Ops:
  0.0 6.6 %copy-start = (bf16[2,64,1024]{2,1,0:T(8,128)(2,1)S(1)}, bf16[2,64,1024]{2,1,0:T(8,128)(2,1)}, u32[]{:S(2)}) copy-start(bf16[2,64,1024]{2,1,0:T(8,128)(2,1)} %fields.1) | copy-start | bytes 786436
  0.0 9.6 %collective-permute-start = (bf16[2,64,1024]{2,1,0:T(8,128)(2,1)}, bf16[2,64,1024]{2,1,0:T(8,128)(2,1)S(1)}, u32[]{:S(2)}, u32[]{:S(2)}) collective-permute-start(bf16[2,64,1024]{2,1,0:T(8,128)(2,1)} %fields.1), channel_id=1, source_target_pairs={{0,1},{1,0},{2,3},{3,2},{4,5},{5,4},{6,7},{7,6},{8,9},{9,8},{10,11... | collective-permute-start | bytes 786440 | tf_op jit(solution)/shard_map/ppermute | solution.py:135
  4.0 9.8 %collective-permute-start.4 = (bf16[2,64,512]{2,1,0:T(8,128)(2,1)S(1)}, bf16[2,64,512]{2,1,0:T(8,128)(2,1)S(1)}, u32[]{:S(2)}, u32[]{:S(2)}) collective-permute-start(bf16[2,64,512]{2,1,0:T(8,128)(2,1)S(1)} %get-tuple-element.11.refs_0_.own), channel_id=1, source_target_pairs={{0,4},{1,5},{2,6},{3,7},{4,0},{5,1},{6,2},{7,3},{8,12},{9,13},{10,... | collective-permute-start | bytes 393224 | tf_op jit(solution)/shard_map/ppermute | solution.py:135
  6.6 10.3 %collective-permute-start.1 = (bf16[2,64,1024]{2,1,0:T(8,128)(2,1)S(1)}, bf16[2,64,1024]{2,1,0:T(8,128)(2,1)S(1)}, u32[]{:S(2)}, u32[]{:S(2)}) collective-permute-start(bf16[2,64,1024]{2,1,0:T(8,128)(2,1)S(1)} %copy-done), channel_id=1, source_target_pairs={{0,16},{1,17},{2,18},{3,19},{4,20},{5,21},{6,22},{7,23},{8,24},{9,... | collective-permute-start | bytes 786440 | tf_op jit(solution)/shard_map/ppermute | solution.py:135
  9.6 10.2 %collective-permute-start.2 = (bf16[2,64,1024]{2,1,0:T(8,128)(2,1)S(1)}, bf16[2,64,1024]{2,1,0:T(8,128)(2,1)S(1)}, u32[]{:S(2)}, u32[]{:S(2)}) collective-permute-start(bf16[2,64,1024]{2,1,0:T(8,128)(2,1)S(1)} %collective-permute-done.refs_2_), channel_id=1, source_target_pairs={{0,16},{1,17},{2,18},{3,19},{4,20},{5,21},{6,22},{7,23},{8,24},{9,... | collective-permute-start | bytes 786440 | tf_op jit(solution)/shard_map/ppermute | solution.py:135
  11.2 8.7 %collective-permute-start.8 = (bf16[2,64,512]{2,1,0:T(8,128)(2,1)S(1)}, bf16[2,64,512]{2,1,0:T(8,128)(2,1)S(1)}, u32[]{:S(2)}, u32[]{:S(2)}) collective-permute-start(bf16[2,64,512]{2,1,0:T(8,128)(2,1)S(1)} %get-tuple-element.12.refs_1_.own), channel_id=1, source_target_pairs={{0,4},{1,5},{2,6},{3,7},{4,0},{5,1},{6,2},{7,3},{8,12},{9,13},{10,... | collective-permute-start | bytes 393224 | tf_op jit(solution)/shard_map/ppermute | solution.py:135
  13.8 9.9 %collective-permute-start.7 = (bf16[2,64,512]{2,1,0:T(8,128)(2,1)S(1)}, bf16[2,64,512]{2,1,0:T(8,128)(2,1)S(1)}, u32[]{:S(2)}, u32[]{:S(2)}) collective-permute-start(bf16[2,64,512]{2,1,0:T(8,128)(2,1)S(1)} %get-tuple-element.14), channel_id=1, source_target_pairs={{0,3},{1,2},{2,1},{3,0},{4,7},{5,6},{6,5},{7,4},{8,11},{9,10},{10,... | collective-permute-start | bytes 393224 | tf_op jit(solution)/shard_map/ppermute | solution.py:135
  16.4 8.6 %collective-permute-start.5 = (bf16[2,64,512]{2,1,0:T(8,128)(2,1)S(1)}, bf16[2,64,512]{2,1,0:T(8,128)(2,1)S(1)}, u32[]{:S(2)}, u32[]{:S(2)}) collective-permute-start(bf16[2,64,512]{2,1,0:T(8,128)(2,1)S(1)} %get-tuple-element.14), channel_id=1, source_target_pairs={{0,1},{1,0},{2,3},{3,2},{4,5},{5,4},{6,7},{7,6},{8,9},{9,8},{10,11... | collective-permute-start | bytes 393224 | tf_op jit(solution)/shard_map/ppermute | solution.py:135
  17.0 6.3 %collective-permute-start.6 = (bf16[2,64,512]{2,1,0:T(8,128)(2,1)S(1)}, bf16[2,64,512]{2,1,0:T(8,128)(2,1)S(1)}, u32[]{:S(2)}, u32[]{:S(2)}) collective-permute-start(bf16[2,64,512]{2,1,0:T(8,128)(2,1)S(1)} %get-tuple-element.13.refs_0_), channel_id=1, source_target_pairs={{0,2},{1,3},{2,0},{3,1},{4,6},{5,7},{6,4},{7,5},{8,10},{9,11},{10,... | collective-permute-start | bytes 393224 | tf_op jit(solution)/shard_map/ppermute | solution.py:135
  19.8 5.2 %collective-permute-start.3 = (bf16[2,256,1024]{2,1,0:T(8,128)(2,1)S(1)}, bf16[2,256,1024]{2,1,0:T(8,128)(2,1)S(1)}, u32[]{:S(2)}, u32[]{:S(2)}) collective-permute-start(bf16[2,256,1024]{2,1,0:T(8,128)(2,1)S(1)} %shard_map.18.mine), channel_id=1, source_target_pairs={{0,8},{1,9},{2,10},{3,11},{4,12},{5,13},{6,14},{7,15},{8,0},{9,1},... | collective-permute-start | bytes 3145736 | tf_op jit(solution)/shard_map/ppermute | solution.py:135
  20.0 8.8 %collective-permute-start.11 = (bf16[2,64,512]{2,1,0:T(8,128)(2,1)S(1)}, bf16[2,64,512]{2,1,0:T(8,128)(2,1)S(1)}, u32[]{:S(2)}, u32[]{:S(2)}) collective-permute-start(bf16[2,64,512]{2,1,0:T(8,128)(2,1)S(1)} %get-tuple-element.16), channel_id=1, source_target_pairs={{0,3},{1,2},{2,1},{3,0},{4,7},{5,6},{6,5},{7,4},{8,11},{9,10},{10,... | collective-permute-start | bytes 393224 | tf_op jit(solution)/shard_map/ppermute | solution.py:135
  23.2 6.4 %collective-permute-start.9 = (bf16[2,64,512]{2,1,0:T(8,128)(2,1)S(1)}, bf16[2,64,512]{2,1,0:T(8,128)(2,1)S(1)}, u32[]{:S(2)}, u32[]{:S(2)}) collective-permute-start(bf16[2,64,512]{2,1,0:T(8,128)(2,1)S(1)} %get-tuple-element.16), channel_id=1, source_target_pairs={{0,1},{1,0},{2,3},{3,2},{4,5},{5,4},{6,7},{7,6},{8,9},{9,8},{10,11... | collective-permute-start | bytes 393224 | tf_op jit(solution)/shard_map/ppermute | solution.py:135
  23.7 5.1 %collective-permute-start.10 = (bf16[2,64,512]{2,1,0:T(8,128)(2,1)S(1)}, bf16[2,64,512]{2,1,0:T(8,128)(2,1)S(1)}, u32[]{:S(2)}, u32[]{:S(2)}) collective-permute-start(bf16[2,64,512]{2,1,0:T(8,128)(2,1)S(1)} %get-tuple-element.15.refs_0_), channel_id=1, source_target_pairs={{0,2},{1,3},{2,0},{3,1},{4,6},{5,7},{6,4},{7,5},{8,10},{9,11},{10,... | collective-permute-start | bytes 393224 | tf_op jit(solution)/shard_map/ppermute | solution.py:135

commit v8 on v7

--- a/solution.py
+++ b/solution.py
@@ -79,15 +79,19 @@
     pixels = pl.ds(start, left.shape[2])
     for cols, which in ((mine, core), (other, 1 - core)):
 
-        @pl.loop(0, mine.shape[1] // TILE)
-        def _(tile):
-            here = pl.ds(pl.multiple_of(tile * TILE, TILE), TILE)
+        def one_tile(tile, cols=cols, which=which):
+            here = pl.ds(tile * TILE if isinstance(tile, int) else pl.multiple_of(tile * TILE, TILE), TILE)
             c_real, c_imag = cols[0, here, pixels], cols[1, here, pixels]
             real = dot(left[0], c_real) + dot(left[1], c_imag)
             imag = dot(left[0], c_imag) - dot(left[1], c_real)
             for i in range(TILE // group):
                 at = pl.multiple_of((2 * (tile * (TILE // group) + i) + which) * group, group)
                 step(pl.ds(at, group), at, real[:, i * group : (i + 1) * group], imag[:, i * group : (i + 1) * group])
+
+        if mine.shape[1] == TILE:
+            one_tile(0)
+        else:
+            pl.loop(0, mine.shape[1] // TILE)(one_tile)
 
 
 def middle_kernel(sizes, places, start, first, mine, other, *refs):

time: 31.4 us -> 31.4 us (level)
  no operation moved by 1% of the time
where the time goes in v8:
time: 31.4 us; the launch traced here: 31.2 us
  starting transfers between devices  18.4 us (59%)
  waiting for transfers between devices  9.26 us (29%)
  Pallas kernels  3.54 us (11%)
    ppermute x12, starting transfers between devices, exchange(): return lax.ppermute(array, AXES, pairs)  18.4 us
    ppermute x12, waiting for transfers between devices, exchange(): return lax.ppermute(array, AXES, pairs)  9.26 us
    pallas_call x7, Pallas kernels, call(): pl.pallas_call(kernel, out_shape=out_shape, in_specs=specs or [VMEM] * le...  3.54 us
  transfers between devices with their start and end apart: 12, of which 5 were waited for; matrix products, arithmetic and copies ran while one was open for 0% of the time, Pallas kernels for 6%

profile of v8, /device:TPU:0, one launch (start us, length us, event | category | flops | bytes accessed | tf_op | source)
XLA Modules:
  0.0 31.2 jit_solution(3194321364501045543)
XLA Ops:
  0.0 3.0 %collective-permute-start = (bf16[2,64,1024]{2,1,0:T(8,128)(2,1)}, bf16[2,64,1024]{2,1,0:T(8,128)(2,1)S(1)}, u32[]{:S(2)}, u32[]{:S(2)}) collective-permute-start(bf16[2,64,1024]{2,1,0:T(8,128)(2,1)} %fields.1), channel_id=1, source_target_pairs={{0,1},{1,0},{2,3},{3,2},{4,5},{5,4},{6,7},{7,6},{8,9},{9,8},{10,11... | collective-permute-start | bytes 786440 | tf_op jit(solution)/shard_map/ppermute | solution.py:139
  3.0 1.0 %shard_map.17 = (bf16[2,64,512]{2,1,0:T(8,128)(2,1)S(1)}, bf16[2,64,512]{2,1,0:T(8,128)(2,1)S(1)}) custom-call(bf16[2,64,1024]{2,1,0:T(8,128)(2,1)} %fields.1), custom_call_target="tpu_custom_call" | custom-call | tf_op jit(solution)/shard_map/pallas_call | solution.py:149
  4.0 2.7 %collective-permute-start.4 = (bf16[2,64,512]{2,1,0:T(8,128)(2,1)S(1)}, bf16[2,64,512]{2,1,0:T(8,128)(2,1)S(1)}, u32[]{:S(2)}, u32[]{:S(2)}) collective-permute-start(bf16[2,64,512]{2,1,0:T(8,128)(2,1)S(1)} %get-tuple-element.11.refs_0_.own), channel_id=1, source_target_pairs={{0,4},{1,5},{2,6},{3,7},{4,0},{5,1},{6,2},{7,3},{8,12},{9,13},{10,... | collective-permute-start | bytes 393224 | tf_op jit(solution)/shard_map/ppermute | solution.py:139
  6.6 1.5 %collective-permute-start.1 = (bf16[2,64,1024]{2,1,0:T(8,128)(2,1)S(1)}, bf16[2,64,1024]{2,1,0:T(8,128)(2,1)S(1)}, u32[]{:S(2)}, u32[]{:S(2)}) collective-permute-start(bf16[2,64,1024]{2,1,0:T(8,128)(2,1)S(1)} %copy-done), channel_id=1, source_target_pairs={{0,16},{1,17},{2,18},{3,19},{4,20},{5,21},{6,22},{7,23},{8,24},{9,... | collective-permute-start | bytes 786440 | tf_op jit(solution)/shard_map/ppermute | solution.py:139
  8.1 1.4 %collective-permute-done.refs_2_ = bf16[2,64,1024]{2,1,0:T(8,128)(2,1)S(1)} collective-permute-done((bf16[2,64,1024]{2,1,0:T(8,128)(2,1)}, bf16[2,64,1024]{2,1,0:T(8,128)(2,1)S(1)}, u32[]{:S(2)}, u32[]{:S(2)}) %collective-permute-start) | collective-permute-done | bytes 262176 | tf_op jit(solution)/shard_map/ppermute | solution.py:139
  9.6 1.6 %collective-permute-start.2 = (bf16[2,64,1024]{2,1,0:T(8,128)(2,1)S(1)}, bf16[2,64,1024]{2,1,0:T(8,128)(2,1)S(1)}, u32[]{:S(2)}, u32[]{:S(2)}) collective-permute-start(bf16[2,64,1024]{2,1,0:T(8,128)(2,1)S(1)} %collective-permute-done.refs_2_), channel_id=1, source_target_pairs={{0,16},{1,17},{2,18},{3,19},{4,20},{5,21},{6,22},{7,23},{8,24},{9,... | collective-permute-start | bytes 786440 | tf_op jit(solution)/shard_map/ppermute | solution.py:139
  11.2 2.6 %collective-permute-start.8 = (bf16[2,64,512]{2,1,0:T(8,128)(2,1)S(1)}, bf16[2,64,512]{2,1,0:T(8,128)(2,1)S(1)}, u32[]{:S(2)}, u32[]{:S(2)}) collective-permute-start(bf16[2,64,512]{2,1,0:T(8,128)(2,1)S(1)} %get-tuple-element.12.refs_1_.own), channel_id=1, source_target_pairs={{0,4},{1,5},{2,6},{3,7},{4,0},{5,1},{6,2},{7,3},{8,12},{9,13},{10,... | collective-permute-start | bytes 393224 | tf_op jit(solution)/shard_map/ppermute | solution.py:139
  13.8 2.6 %collective-permute-start.7 = (bf16[2,64,512]{2,1,0:T(8,128)(2,1)S(1)}, bf16[2,64,512]{2,1,0:T(8,128)(2,1)S(1)}, u32[]{:S(2)}, u32[]{:S(2)}) collective-permute-start(bf16[2,64,512]{2,1,0:T(8,128)(2,1)S(1)} %get-tuple-element.14), channel_id=1, source_target_pairs={{0,3},{1,2},{2,1},{3,0},{4,7},{5,6},{6,5},{7,4},{8,11},{9,10},{10,... | collective-permute-start | bytes 393224 | tf_op jit(solution)/shard_map/ppermute | solution.py:139
  16.4 0.5 %collective-permute-start.5 = (bf16[2,64,512]{2,1,0:T(8,128)(2,1)S(1)}, bf16[2,64,512]{2,1,0:T(8,128)(2,1)S(1)}, u32[]{:S(2)}, u32[]{:S(2)}) collective-permute-start(bf16[2,64,512]{2,1,0:T(8,128)(2,1)S(1)} %get-tuple-element.14), channel_id=1, source_target_pairs={{0,1},{1,0},{2,3},{3,2},{4,5},{5,4},{6,7},{7,6},{8,9},{9,8},{10,11... | collective-permute-start | bytes 393224 | tf_op jit(solution)/shard_map/ppermute | solution.py:139
  17.0 0.0 collective-permute-done.1.refs_3_
  17.0 0.5 %collective-permute-start.6 = (bf16[2,64,512]{2,1,0:T(8,128)(2,1)S(1)}, bf16[2,64,512]{2,1,0:T(8,128)(2,1)S(1)}, u32[]{:S(2)}, u32[]{:S(2)}) collective-permute-start(bf16[2,64,512]{2,1,0:T(8,128)(2,1)S(1)} %get-tuple-element.13.refs_0_), channel_id=1, source_target_pairs={{0,2},{1,3},{2,0},{3,1},{4,6},{5,7},{6,4},{7,5},{8,10},{9,11},{10,... | collective-permute-start | bytes 393224 | tf_op jit(solution)/shard_map/ppermute | solution.py:139
  17.5 2.3 %collective-permute-done.2.refs_4_ = bf16[2,64,1024]{2,1,0:T(8,128)(2,1)S(1)} collective-permute-done((bf16[2,64,1024]{2,1,0:T(8,128)(2,1)S(1)}, bf16[2,64,1024]{2,1,0:T(8,128)(2,1)S(1)}, u32[]{:S(2)}, u32[]{:S(2)}) %collective-permute-start.2) | collective-permute-done | bytes 262176 | tf_op jit(solution)/shard_map/ppermute | solution.py:139
  19.7 0.1 shard_map.18.mine
  19.8 0.1 collective-permute-start.3
  20.0 1.6 %collective-permute-start.11 = (bf16[2,64,512]{2,1,0:T(8,128)(2,1)S(1)}, bf16[2,64,512]{2,1,0:T(8,128)(2,1)S(1)}, u32[]{:S(2)}, u32[]{:S(2)}) collective-permute-start(bf16[2,64,512]{2,1,0:T(8,128)(2,1)S(1)} %get-tuple-element.16), channel_id=1, source_target_pairs={{0,3},{1,2},{2,1},{3,0},{4,7},{5,6},{6,5},{7,4},{8,11},{9,10},{10,... | collective-permute-start | bytes 393224 | tf_op jit(solution)/shard_map/ppermute | solution.py:139
  21.5 1.7 %collective-permute-done.6.refs_2_ = bf16[2,64,512]{2,1,0:T(8,128)(2,1)S(1)} collective-permute-done((bf16[2,64,512]{2,1,0:T(8,128)(2,1)S(1)}, bf16[2,64,512]{2,1,0:T(8,128)(2,1)S(1)}, u32[]{:S(2)}, u32[]{:S(2)}) %collective-permute-start.6) | collective-permute-done | bytes 131104 | tf_op jit(solution)/shard_map/ppermute | solution.py:139
  23.2 0.5 %collective-permute-start.9 = (bf16[2,64,512]{2,1,0:T(8,128)(2,1)S(1)}, bf16[2,64,512]{2,1,0:T(8,128)(2,1)S(1)}, u32[]{:S(2)}, u32[]{:S(2)}) collective-permute-start(bf16[2,64,512]{2,1,0:T(8,128)(2,1)S(1)} %get-tuple-element.16), channel_id=1, source_target_pairs={{0,1},{1,0},{2,3},{3,2},{4,5},{5,4},{6,7},{7,6},{8,9},{9,8},{10,11... | collective-permute-start | bytes 393224 | tf_op jit(solution)/shard_map/ppermute | solution.py:139
  23.7 0.0 collective-permute-done.7.refs_3_
  23.7 1.3 %collective-permute-start.10 = (bf16[2,64,512]{2,1,0:T(8,128)(2,1)S(1)}, bf16[2,64,512]{2,1,0:T(8,128)(2,1)S(1)}, u32[]{:S(2)}, u32[]{:S(2)}) collective-permute-start(bf16[2,64,512]{2,1,0:T(8,128)(2,1)S(1)} %get-tuple-element.15.refs_0_), channel_id=1, source_target_pairs={{0,2},{1,3},{2,0},{3,1},{4,6},{5,7},{6,4},{7,5},{8,10},{9,11},{10,... | collective-permute-start | bytes 393224 | tf_op jit(solution)/shard_map/ppermute | solution.py:139
  25.0 0.0 collective-permute-done.5.refs_1_
  25.0 0.8 %shard_map.21.so_far = f32[2,256,512]{2,1,0:T(8,128)S(1)} custom-call(bf16[2,256,1024]{2,1,0:T(8,128)(2,1)S(1)} %shard_map.18.mine, bf16[2,256,1024]{2,1,0:T(8,128)(2,1)S(1)} %collective-permute-done.3.other, bf16[2,64,512]{2,1,0:T(8,128)(2,1)S(1)} %get-tuple-element.13.refs_0_, bf16[2,64,512]{2,1,0:T(8,128)(2,1)S(1)} %collective-permute-done.5.refs_1_, ...), custom_call_target="tpu_custom_call" | custom-call | flops 10000000000 | bytes 262144 | tf_op jit(solution)/shard_map/pallas_call | solution.py:149
  25.8 3.0 %collective-permute-done.10.refs_2_ = bf16[2,64,512]{2,1,0:T(8,128)(2,1)S(1)} collective-permute-done((bf16[2,64,512]{2,1,0:T(8,128)(2,1)S(1)}, bf16[2,64,512]{2,1,0:T(8,128)(2,1)S(1)}, u32[]{:S(2)}, u32[]{:S(2)}) %collective-permute-start.10) | collective-permute-done | bytes 131104 | tf_op jit(solution)/shard_map/ppermute | solution.py:139
  28.8 0.8 %collective-permute-done.9.refs_1_ = bf16[2,64,512]{2,1,0:T(8,128)(2,1)S(1)} collective-permute-done((bf16[2,64,512]{2,1,0:T(8,128)(2,1)S(1)}, bf16[2,64,512]{2,1,0:T(8,128)(2,1)S(1)}, u32[]{:S(2)}, u32[]{:S(2)}) %collective-permute-start.9) | collective-permute-done | bytes 131104 | tf_op jit(solution)/shard_map/ppermute | solution.py:139
  29.6 1.6 %shard_map.23 = f32[2,256,512]{2,1,0:T(8,128)} custom-call(bf16[2,256,1024]{2,1,0:T(8,128)(2,1)S(1)} %shard_map.18.mine, bf16[2,256,1024]{2,1,0:T(8,128)(2,1)S(1)} %collective-permute-done.3.other, f32[2,256,512]{2,1,0:T(8,128)S(1)} %shard_map.21.so_far, bf16[2,64,512]{2,1,0:T(8,128)(2,1)S(1)} %get-tuple-element.15.refs_0_, ...), custom_call_target="tpu_custom_call" | custom-call | tf_op jit(solution)/shard_map/pallas_call | solution.py:149
  (9 shorter events, 0.1 us)
Async XLA Ops:
  0.0 6.6 %copy-start = (bf16[2,64,1024]{2,1,0:T(8,128)(2,1)S(1)}, bf16[2,64,1024]{2,1,0:T(8,128)(2,1)}, u32[]{:S(2)}) copy-start(bf16[2,64,1024]{2,1,0:T(8,128)(2,1)} %fields.1) | copy-start | bytes 786436
  0.0 9.6 %collective-permute-start = (bf16[2,64,1024]{2,1,0:T(8,128)(2,1)}, bf16[2,64,1024]{2,1,0:T(8,128)(2,1)S(1)}, u32[]{:S(2)}, u32[]{:S(2)}) collective-permute-start(bf16[2,64,1024]{2,1,0:T(8,128)(2,1)} %fields.1), channel_id=1, source_target_pairs={{0,1},{1,0},{2,3},{3,2},{4,5},{5,4},{6,7},{7,6},{8,9},{9,8},{10,11... | collective-permute-start | bytes 786440 | tf_op jit(solution)/shard_map/ppermute | solution.py:139
  4.0 9.8 %collective-permute-start.4 = (bf16[2,64,512]{2,1,0:T(8,128)(2,1)S(1)}, bf16[2,64,512]{2,1,0:T(8,128)(2,1)S(1)}, u32[]{:S(2)}, u32[]{:S(2)}) collective-permute-start(bf16[2,64,512]{2,1,0:T(8,128)(2,1)S(1)} %get-tuple-element.11.refs_0_.own), channel_id=1, source_target_pairs={{0,4},{1,5},{2,6},{3,7},{4,0},{5,1},{6,2},{7,3},{8,12},{9,13},{10,... | collective-permute-start | bytes 393224 | tf_op jit(solution)/shard_map/ppermute | solution.py:139
  6.6 10.3 %collective-permute-start.1 = (bf16[2,64,1024]{2,1,0:T(8,128)(2,1)S(1)}, bf16[2,64,1024]{2,1,0:T(8,128)(2,1)S(1)}, u32[]{:S(2)}, u32[]{:S(2)}) collective-permute-start(bf16[2,64,1024]{2,1,0:T(8,128)(2,1)S(1)} %copy-done), channel_id=1, source_target_pairs={{0,16},{1,17},{2,18},{3,19},{4,20},{5,21},{6,22},{7,23},{8,24},{9,... | collective-permute-start | bytes 786440 | tf_op jit(solution)/shard_map/ppermute | solution.py:139
  9.6 10.2 %collective-permute-start.2 = (bf16[2,64,1024]{2,1,0:T(8,128)(2,1)S(1)}, bf16[2,64,1024]{2,1,0:T(8,128)(2,1)S(1)}, u32[]{:S(2)}, u32[]{:S(2)}) collective-permute-start(bf16[2,64,1024]{2,1,0:T(8,128)(2,1)S(1)} %collective-permute-done.refs_2_), channel_id=1, source_target_pairs={{0,16},{1,17},{2,18},{3,19},{4,20},{5,21},{6,22},{7,23},{8,24},{9,... | collective-permute-start | bytes 786440 | tf_op jit(solution)/shard_map/ppermute | solution.py:139
  11.2 8.7 %collective-permute-start.8 = (bf16[2,64,512]{2,1,0:T(8,128)(2,1)S(1)}, bf16[2,64,512]{2,1,0:T(8,128)(2,1)S(1)}, u32[]{:S(2)}, u32[]{:S(2)}) collective-permute-start(bf16[2,64,512]{2,1,0:T(8,128)(2,1)S(1)} %get-tuple-element.12.refs_1_.own), channel_id=1, source_target_pairs={{0,4},{1,5},{2,6},{3,7},{4,0},{5,1},{6,2},{7,3},{8,12},{9,13},{10,... | collective-permute-start | bytes 393224 | tf_op jit(solution)/shard_map/ppermute | solution.py:139
  13.8 9.9 %collective-permute-start.7 = (bf16[2,64,512]{2,1,0:T(8,128)(2,1)S(1)}, bf16[2,64,512]{2,1,0:T(8,128)(2,1)S(1)}, u32[]{:S(2)}, u32[]{:S(2)}) collective-permute-start(bf16[2,64,512]{2,1,0:T(8,128)(2,1)S(1)} %get-tuple-element.14), channel_id=1, source_target_pairs={{0,3},{1,2},{2,1},{3,0},{4,7},{5,6},{6,5},{7,4},{8,11},{9,10},{10,... | collective-permute-start | bytes 393224 | tf_op jit(solution)/shard_map/ppermute | solution.py:139
  16.4 8.6 %collective-permute-start.5 = (bf16[2,64,512]{2,1,0:T(8,128)(2,1)S(1)}, bf16[2,64,512]{2,1,0:T(8,128)(2,1)S(1)}, u32[]{:S(2)}, u32[]{:S(2)}) collective-permute-start(bf16[2,64,512]{2,1,0:T(8,128)(2,1)S(1)} %get-tuple-element.14), channel_id=1, source_target_pairs={{0,1},{1,0},{2,3},{3,2},{4,5},{5,4},{6,7},{7,6},{8,9},{9,8},{10,11... | collective-permute-start | bytes 393224 | tf_op jit(solution)/shard_map/ppermute | solution.py:139
  17.0 6.3 %collective-permute-start.6 = (bf16[2,64,512]{2,1,0:T(8,128)(2,1)S(1)}, bf16[2,64,512]{2,1,0:T(8,128)(2,1)S(1)}, u32[]{:S(2)}, u32[]{:S(2)}) collective-permute-start(bf16[2,64,512]{2,1,0:T(8,128)(2,1)S(1)} %get-tuple-element.13.refs_0_), channel_id=1, source_target_pairs={{0,2},{1,3},{2,0},{3,1},{4,6},{5,7},{6,4},{7,5},{8,10},{9,11},{10,... | collective-permute-start | bytes 393224 | tf_op jit(solution)/shard_map/ppermute | solution.py:139
  19.8 5.2 %collective-permute-start.3 = (bf16[2,256,1024]{2,1,0:T(8,128)(2,1)S(1)}, bf16[2,256,1024]{2,1,0:T(8,128)(2,1)S(1)}, u32[]{:S(2)}, u32[]{:S(2)}) collective-permute-start(bf16[2,256,1024]{2,1,0:T(8,128)(2,1)S(1)} %shard_map.18.mine), channel_id=1, source_target_pairs={{0,8},{1,9},{2,10},{3,11},{4,12},{5,13},{6,14},{7,15},{8,0},{9,1},... | collective-permute-start | bytes 3145736 | tf_op jit(solution)/shard_map/ppermute | solution.py:139
  20.0 8.8 %collective-permute-start.11 = (bf16[2,64,512]{2,1,0:T(8,128)(2,1)S(1)}, bf16[2,64,512]{2,1,0:T(8,128)(2,1)S(1)}, u32[]{:S(2)}, u32[]{:S(2)}) collective-permute-start(bf16[2,64,512]{2,1,0:T(8,128)(2,1)S(1)} %get-tuple-element.16), channel_id=1, source_target_pairs={{0,3},{1,2},{2,1},{3,0},{4,7},{5,6},{6,5},{7,4},{8,11},{9,10},{10,... | collective-permute-start | bytes 393224 | tf_op jit(solution)/shard_map/ppermute | solution.py:139
  23.2 6.4 %collective-permute-start.9 = (bf16[2,64,512]{2,1,0:T(8,128)(2,1)S(1)}, bf16[2,64,512]{2,1,0:T(8,128)(2,1)S(1)}, u32[]{:S(2)}, u32[]{:S(2)}) collective-permute-start(bf16[2,64,512]{2,1,0:T(8,128)(2,1)S(1)} %get-tuple-element.16), channel_id=1, source_target_pairs={{0,1},{1,0},{2,3},{3,2},{4,5},{5,4},{6,7},{7,6},{8,9},{9,8},{10,11... | collective-permute-start | bytes 393224 | tf_op jit(solution)/shard_map/ppermute | solution.py:139
  23.7 5.1 %collective-permute-start.10 = (bf16[2,64,512]{2,1,0:T(8,128)(2,1)S(1)}, bf16[2,64,512]{2,1,0:T(8,128)(2,1)S(1)}, u32[]{:S(2)}, u32[]{:S(2)}) collective-permute-start(bf16[2,64,512]{2,1,0:T(8,128)(2,1)S(1)} %get-tuple-element.15.refs_0_), channel_id=1, source_target_pairs={{0,2},{1,3},{2,0},{3,1},{4,6},{5,7},{6,4},{7,5},{8,10},{9,11},{10,... | collective-permute-start | bytes 393224 | tf_op jit(solution)/shard_map/ppermute | solution.py:139
